TPU v7x, 32 devices: a whole 2x2x4 slice. The times are simulated.
32 devices in a mesh: dp: 4 (over y, x), exp: 2 (over core), col: 4 (over z).
Axes of the slice: x: 2, y: 2, z: 4, core: 2. Of those that a mesh axis runs over, the one named last changes fastest.
Arguments:
- inputs: bfloat16 [8192, 2048], P(('dp', 'exp', 'col')), may hold values from -6 to 6
- expert_ids: int32 [8192, 8], P(('dp', 'exp', 'col')), may hold values from 0 to 31, all different within a row; in each aligned block of 256 rows (0 to 255, 256 to 511, ...) at most 80 rows name the same one
- positions: int32 [8192], P(('dp', 'exp')), may hold values from 0 to 3069, as said below
- cotangent: bfloat16 [8192, 2048], P(('dp', 'exp', 'col')), may hold values from -6 to 6
- attn_gain: float32 [2048], replicated, may hold values from 0.5 to 1.5
- query_proj: bfloat16 [2048, 4096], P('exp', 'col'), may hold values from -0.125 to 0.125
- key_projection: bfloat16 [2048, 512], P('exp', 'col'), may hold values from -0.125 to 0.125
- value_projection: bfloat16 [2048, 512], P('exp', 'col'), may hold values from -0.125 to 0.125
- query_norm_gain: float32 [128], replicated, may hold values from 1 to 2
- key_norm_gain: float32 [128], replicated, may hold values from 1 to 2
- out_proj: bfloat16 [2048, 4096], P('exp', 'col'), may hold values from -0.5 to 0.5
- moe_gain: float32 [2048], replicated, may hold values from 0.5 to 1.5
- router: bfloat16 [2048, 32], replicated, may hold values from -0.0625 to 0.0625
- gate_proj: bfloat16 [32, 2048, 768], P(('dp', 'exp', 'col')), may hold values from -0.125 to 0.125
- up_proj: bfloat16 [32, 2048, 768], P(('dp', 'exp', 'col')), may hold values from -0.125 to 0.125
- down_proj: bfloat16 [32, 768, 2048], P(('dp', 'exp', 'col')), may hold values from -0.875 to 0.875
Outputs:
- outputs: bfloat16 [8192, 2048], P(('dp', 'exp', 'col'))
- grad_inputs: bfloat16 [8192, 2048], P(('dp', 'exp', 'col'))
- grad_attn_gain: float32 [2048], replicated
- grad_query_proj: float32 [2048, 4096], P(('dp', 'exp'), 'col')
- grad_key_proj: float32 [2048, 512], P(('dp', 'exp'), 'col')
- grad_value_proj: float32 [2048, 512], P(('dp', 'exp'), 'col')
- grad_query_gain: float32 [128], replicated
- grad_key_gain: float32 [128], replicated
- grad_out_proj: float32 [2048, 4096], P(('dp', 'exp'), 'col')
- grad_moe_gain: float32 [2048], replicated
- grad_router: float32 [2048, 32], replicated
- grad_gate_proj: float32 [32, 2048, 768], P(('dp', 'exp', 'col'))
- grad_up_proj: float32 [32, 2048, 768], P(('dp', 'exp', 'col'))
- grad_down_proj: float32 [32, 768, 2048], P(('dp', 'exp', 'col'))
Inputs may be any that keep to these rules, and one draw needn't show every extreme that they name: `expert_ids`: each row names 8 different experts. Among the rows of one device no expert is named by more than 80 rows, a bound that some block reaches of them. Within each sequence of 1024 tokens the positions start at 0 and rise by 1 to 3 from one token to the next; in one sequence every rise is 3.
All inputs are finite; a program needn't handle non-finite values.
Results may differ from a plain program's by a relative error of at most 0.025.
Values may be sent and summed in bfloat16 or wider, within the bound.
No kernel may reach another device: no remote copies, remote signals or barrier semaphores. Data moves between devices by JAX's collectives and lax.ppermute only.
A program may use at most 256 MiB of HBM per device.

v0:
```python
import jax
import jax.numpy as jnp
from jax import lax
from jax.sharding import PartitionSpec as P

epsilon = 1e-06
rotary_base = 1000000.0


def rms_scale(values, gain):
    return values * lax.rsqrt(jnp.mean(values * values, axis=-1, keepdims=True) + epsilon) * gain


def rotary_tables(positions, head_width):
    halves = head_width // 2
    frequency = rotary_base ** (-2.0 * jnp.arange(halves, dtype=jnp.float32) / head_width)
    angles = positions.astype(jnp.float32)[:, None] * frequency[None, :]
    return (jnp.cos(angles), jnp.sin(angles))


def rotary(values, cosine, sine_part):
    halves = values.shape[-1] // 2
    former = values[..., :halves]
    latter = values[..., halves:]
    cos_rows = cosine[:, None, :]
    sin_rows = sine_part[:, None, :]
    return jnp.concatenate(
        [former * cos_rows - latter * sin_rows, latter * cos_rows + former * sin_rows], axis=-1
    )


def route_rows(buffer):
    return lax.all_to_all(buffer, ("dp", "exp", "col"), split_axis=0, concat_axis=0, tiled=True)


def contract_last(left_side, right_side):
    return lax.dot_general(
        left_side, right_side, (((1,), (1,)), ((), ())), preferred_element_type=jnp.float32
    )


def contract_first(left_side, right_side):
    return lax.dot_general(
        left_side, right_side, (((0,), (0,)), ((), ())), preferred_element_type=jnp.float32
    )


def local(
    inputs,
    expert_ids,
    positions,
    cotangent,
    attn_gain,
    query_proj,
    key_projection,
    value_projection,
    query_norm_gain,
    key_norm_gain,
    out_proj,
    moe_gain,
    router,
    gate_proj,
    up_proj,
    down_proj,
):
    tokens_here, model_width = inputs.shape
    head_size = query_norm_gain.shape[0]
    choices_per = expert_ids.shape[1]
    experts = router.shape[1]
    most_rows = tokens_here * choices_per * 5 // (4 * experts)
    assigned = tokens_here * choices_per
    input_rows = inputs.astype(jnp.float32)
    normed, pull_first = jax.vjp(rms_scale, input_rows, attn_gain)
    sequence = lax.all_gather(normed.astype(jnp.bfloat16), "col", axis=0, tiled=True)
    full_query, full_key, full_value, full_out = (
        lax.all_gather(query_proj, "exp", axis=0, tiled=True),
        lax.all_gather(key_projection, "exp", axis=0, tiled=True),
        lax.all_gather(value_projection, "exp", axis=0, tiled=True),
        lax.all_gather(out_proj, "exp", axis=0, tiled=True),
    )
    seq_len = sequence.shape[0]
    query_heads = full_query.shape[1] // head_size
    kv_heads = full_key.shape[1] // head_size
    grouping = query_heads // kv_heads
    q_raw = jnp.dot(sequence, full_query, preferred_element_type=jnp.float32)
    k_raw = jnp.dot(sequence, full_key, preferred_element_type=jnp.float32)
    v_raw = jnp.dot(sequence, full_value, preferred_element_type=jnp.float32)
    cosine, sine_part = rotary_tables(positions, head_size)

    def shape_heads(q_in, k_in, q_scale, k_scale):
        q_out = rotary(
            rms_scale(q_in.reshape(seq_len, query_heads, head_size), q_scale), cosine, sine_part
        )
        k_out = rotary(
            rms_scale(k_in.reshape(seq_len, kv_heads, head_size), k_scale), cosine, sine_part
        )
        return (q_out, k_out)

    (q_rot, k_rot), pull_heads = jax.vjp(shape_heads, q_raw, k_raw, query_norm_gain, key_norm_gain)
    query_rows = q_rot.astype(jnp.bfloat16).reshape(seq_len, kv_heads, grouping, head_size)
    keys_low = k_rot.astype(jnp.bfloat16)
    values_low = v_raw.astype(jnp.bfloat16).reshape(seq_len, kv_heads, head_size)
    score_scale = head_size ** (-0.5)
    span_rows = min(512, seq_len)
    blocks = seq_len // span_rows
    key_index = jnp.arange(seq_len)
    offsets = jnp.arange(blocks, dtype=jnp.int32) * span_rows

    def scores_for(offset):
        rows_q = lax.dynamic_slice_in_dim(query_rows, offset, span_rows, 0)
        raw_scores = (
            jnp.einsum("bkgd,tkd->kgbt", rows_q, keys_low, preferred_element_type=jnp.float32)
            * score_scale
        )
        allowed = (offset + jnp.arange(span_rows))[:, None] >= key_index[None, :]
        return (rows_q, jnp.where(allowed, raw_scores, -1e30))

    def forward_block(offset):
        rows_q, scores = scores_for(offset)
        row_peak = jnp.max(scores, axis=-1, keepdims=True)
        exponent = jnp.exp(scores - row_peak)
        summed = jnp.sum(exponent, axis=-1, keepdims=True)
        probabilities = exponent / summed
        expert_mixture = jnp.einsum(
            "kgbt,tkd->bkgd",
            probabilities.astype(jnp.bfloat16),
            values_low,
            preferred_element_type=jnp.float32,
        )
        return (expert_mixture, row_peak + jnp.log(summed))

    expert_mixture, log_sums = lax.map(forward_block, offsets)
    attended = expert_mixture.reshape(seq_len, query_heads * head_size).astype(jnp.bfloat16)
    branch = lax.psum_scatter(
        contract_last(attended, full_out).astype(jnp.bfloat16),
        "col",
        scatter_dimension=0,
        tiled=True,
    ).astype(jnp.float32)
    hidden = input_rows + branch
    routed, pull_second = jax.vjp(rms_scale, hidden, moe_gain)
    routed_low = routed.astype(jnp.bfloat16)
    logits = jnp.dot(routed_low, router, preferred_element_type=jnp.float32)
    chosen = jnp.take_along_axis(logits, expert_ids, axis=1)
    gate_weights = jax.nn.softmax(chosen, axis=-1)
    flat_ids = expert_ids.reshape(assigned)
    expert_index = jnp.arange(experts, dtype=jnp.int32)
    matches = (flat_ids[:, None] == expert_index[None, :]).astype(jnp.int32)
    slot_rank = jnp.sum((jnp.cumsum(matches, axis=0) - 1) * matches, axis=1)
    destination = flat_ids * most_rows + slot_rank
    slot_table = (
        jnp.full((experts * most_rows,), assigned, jnp.int32)
        .at[destination]
        .set(jnp.arange(assigned, dtype=jnp.int32))
    )
    filled = (slot_table < assigned)[:, None]
    source_rows = jnp.minimum(slot_table // choices_per, tokens_here - 1)
    sending = jnp.where(filled, routed_low[source_rows], jnp.zeros((), jnp.bfloat16))
    arrived = route_rows(sending.reshape(experts, most_rows, model_width)).reshape(
        experts * most_rows, model_width
    )
    gate_weight = gate_proj[0]
    up_weight = up_proj[0]
    down_weight = down_proj[0]
    gate_part = jnp.dot(arrived, gate_weight, preferred_element_type=jnp.float32)
    up_part = jnp.dot(arrived, up_weight, preferred_element_type=jnp.float32)

    def activate(gate_in, up_in):
        return jax.nn.silu(gate_in) * up_in

    acted, pull_act = jax.vjp(activate, gate_part, up_part)
    acted_low = acted.astype(jnp.bfloat16)
    expert_out = jnp.dot(acted_low, down_weight, preferred_element_type=jnp.float32).astype(
        jnp.bfloat16
    )
    returned = route_rows(expert_out.reshape(experts, most_rows, model_width)).reshape(
        experts * most_rows, model_width
    )
    picked = returned[destination].reshape(tokens_here, choices_per, model_width)
    combined = jnp.einsum("tk,tkd->td", gate_weights, picked.astype(jnp.float32))
    outputs = (hidden + combined).astype(jnp.bfloat16)
    upstream = cotangent.astype(jnp.float32)
    grad_gates = jnp.einsum("tkd,td->tk", picked.astype(jnp.float32), upstream)
    grad_picked = (
        (gate_weights[:, :, None] * upstream[:, None, :])
        .astype(jnp.bfloat16)
        .reshape(assigned, model_width)
    )
    grad_send = jnp.where(
        filled, grad_picked[jnp.minimum(slot_table, assigned - 1)], jnp.zeros((), jnp.bfloat16)
    )
    grad_arrived = route_rows(grad_send.reshape(experts, most_rows, model_width)).reshape(
        experts * most_rows, model_width
    )
    grad_acted = contract_last(grad_arrived, down_weight)
    grad_down = contract_first(acted_low, grad_arrived)
    grad_gate_part, grad_up_part = pull_act(grad_acted)
    gate_grad_low = grad_gate_part.astype(jnp.bfloat16)
    up_grad_low = grad_up_part.astype(jnp.bfloat16)
    grad_gate_weight = contract_first(arrived, gate_grad_low)
    grad_up_weight = contract_first(arrived, up_grad_low)
    grad_rows = (
        contract_last(gate_grad_low, gate_weight) + contract_last(up_grad_low, up_weight)
    ).astype(jnp.bfloat16)
    back_rows = route_rows(grad_rows.reshape(experts, most_rows, model_width)).reshape(
        experts * most_rows, model_width
    )
    grad_routed = jnp.sum(
        back_rows[destination].reshape(tokens_here, choices_per, model_width).astype(jnp.float32),
        axis=1,
    )
    grad_chosen = gate_weights * (
        grad_gates - jnp.sum(gate_weights * grad_gates, axis=-1, keepdims=True)
    )
    grad_logits = jnp.sum(
        jnp.where(
            expert_ids[:, :, None] == expert_index[None, None, :], grad_chosen[:, :, None], 0.0
        ),
        axis=1,
    ).astype(jnp.bfloat16)
    grad_routed = grad_routed + contract_last(grad_logits, router)
    grad_router = contract_first(routed_low, grad_logits)
    grad_hidden_norm, grad_moe_gain = pull_second(grad_routed)
    grad_hidden = upstream + grad_hidden_norm
    grad_seq = lax.all_gather(grad_hidden.astype(jnp.bfloat16), "col", axis=0, tiled=True)
    grad_attended = jnp.dot(grad_seq, full_out, preferred_element_type=jnp.float32).astype(
        jnp.bfloat16
    )
    grad_out_weight = contract_first(grad_seq, attended)
    grad_mixture = grad_attended.reshape(seq_len, kv_heads, grouping, head_size)

    def backward_block(running, offset):
        grad_keys, grad_values = running
        rows_q, scores = scores_for(offset)
        probabilities = jnp.exp(scores - log_sums[offset // span_rows])
        rows_grad = lax.dynamic_slice_in_dim(grad_mixture, offset, span_rows, 0)
        grad_probs = jnp.einsum(
            "bkgd,tkd->kgbt", rows_grad, values_low, preferred_element_type=jnp.float32
        )
        inner_sum = jnp.sum(probabilities * grad_probs, axis=-1, keepdims=True)
        grad_scores = (probabilities * (grad_probs - inner_sum)).astype(jnp.bfloat16)
        grad_rows_q = (
            jnp.einsum("kgbt,tkd->bkgd", grad_scores, keys_low, preferred_element_type=jnp.float32)
            * score_scale
        )
        grad_keys = (
            grad_keys
            + jnp.einsum("kgbt,bkgd->tkd", grad_scores, rows_q, preferred_element_type=jnp.float32)
            * score_scale
        )
        grad_values = grad_values + jnp.einsum(
            "kgbt,bkgd->tkd",
            probabilities.astype(jnp.bfloat16),
            rows_grad,
            preferred_element_type=jnp.float32,
        )
        return ((grad_keys, grad_values), grad_rows_q)

    zeros_kv = jnp.zeros((seq_len, kv_heads, head_size), jnp.float32)
    (grad_keys, grad_values), grad_queries = lax.scan(backward_block, (zeros_kv, zeros_kv), offsets)
    grad_q_raw, grad_k_raw, grad_query_gain, grad_key_gain = pull_heads(
        (grad_queries.reshape(seq_len, query_heads, head_size), grad_keys)
    )
    grad_q_low = grad_q_raw.astype(jnp.bfloat16)
    grad_k_low = grad_k_raw.astype(jnp.bfloat16)
    grad_v_low = grad_values.reshape(seq_len, kv_heads * head_size).astype(jnp.bfloat16)
    grad_query_weight = contract_first(sequence, grad_q_low)
    grad_key_weight = contract_first(sequence, grad_k_low)
    grad_value_weight = contract_first(sequence, grad_v_low)
    total_rows = contract_last(grad_q_low, full_query)
    total_rows = total_rows + contract_last(grad_k_low, full_key)
    grad_normed = lax.psum_scatter(
        (total_rows + contract_last(grad_v_low, full_value)).astype(jnp.bfloat16),
        "col",
        scatter_dimension=0,
        tiled=True,
    ).astype(jnp.float32)
    grad_input_norm, grad_attn_gain = pull_first(grad_normed)
    grad_inputs = (grad_hidden + grad_input_norm).astype(jnp.bfloat16)
    reduced = (
        lax.psum_scatter(
            grad_query_weight.astype(jnp.bfloat16), ("dp", "exp"), scatter_dimension=0, tiled=True
        ).astype(jnp.float32),
        lax.psum_scatter(
            grad_key_weight.astype(jnp.bfloat16), ("dp", "exp"), scatter_dimension=0, tiled=True
        ).astype(jnp.float32),
        lax.psum_scatter(
            grad_value_weight.astype(jnp.bfloat16), ("dp", "exp"), scatter_dimension=0, tiled=True
        ).astype(jnp.float32),
        lax.psum_scatter(
            grad_out_weight.astype(jnp.bfloat16), ("dp", "exp"), scatter_dimension=0, tiled=True
        ).astype(jnp.float32),
    )
    shared = lax.psum(
        (grad_attn_gain, grad_query_gain, grad_key_gain, grad_moe_gain, grad_router),
        ("dp", "exp", "col"),
    )
    return (
        outputs,
        grad_inputs,
        shared[0],
        reduced[0],
        reduced[1],
        reduced[2],
        shared[1],
        shared[2],
        reduced[3],
        shared[3],
        shared[4],
        grad_gate_weight[None],
        grad_up_weight[None],
        grad_down[None],
    )


def solution(mesh):
    return jax.shard_map(
        local,
        mesh=mesh,
        in_specs=(
            P(("dp", "exp", "col"), None),
            P(("dp", "exp", "col"), None),
            P(("dp", "exp")),
            P(("dp", "exp", "col"), None),
            P(),
            P("exp", "col"),
            P("exp", "col"),
            P("exp", "col"),
            P(),
            P(),
            P("exp", "col"),
            P(),
            P(),
            P(("dp", "exp", "col"), None, None),
            P(("dp", "exp", "col"), None, None),
            P(("dp", "exp", "col"), None, None),
        ),
        out_specs=(
            P(("dp", "exp", "col"), None),
            P(("dp", "exp", "col"), None),
            P(),
            P(("dp", "exp"), "col"),
            P(("dp", "exp"), "col"),
            P(("dp", "exp"), "col"),
            P(),
            P(),
            P(("dp", "exp"), "col"),
            P(),
            P(),
            P(("dp", "exp", "col"), None, None),
            P(("dp", "exp", "col"), None, None),
            P(("dp", "exp", "col"), None, None),
        ),
        check_vma=False,
    )
```

profile of v0, /device:TPU:0, one launch (start us, length us, event | category | flops | bytes accessed | tf_op | source)
XLA Modules:
  0.0 2055.1 jit_solution(8758713217645897591)
XLA Ops:
  23.7 72.5 %all-gather.5.cloned.1.call-done = bf16[1024,2048]{1,0:T(8,128)(2,1)} async-done(((bf16[256,2048]{1,0:T(8,128)(2,1)}), bf16[1024,2048]{1,0:T(8,128)(2,1)}) %all-gather.5.cloned.1.call-update) | async-done | bytes 4194320 | tf_op jit(solution)/shard_map/all_gather | solution.py:74
  137.5 39.4 %while.30 = (s32[]{:T(128)}, bf16[2,512,1,8,128]{4,1,3,2,0:T(8,128)(2,1)}, f32[2,1,8,512,1]{3,2,4,1,0:T(8,128)S(1)}, s32[2]{0:T(128)S(1)}, bf16[1024,1,8,128]{3,...) while((s32[]{:T(128)}, ...), condition=%wide.region_6.7_spmd.clone, body=%wide.region_3.6_spmd.clone.sunk | while | flops 2198336000 | bytes 74060040 | solution.py:132
  192.7 15.9 reduce-window.6
  219.5 49.3 %reduce-scatter.7.cloned.1.call-done = bf16[256,2048]{1,0:T(8,128)(2,1)} async-done(((bf16[1024,2048]{1,0:T(8,128)(2,1)}), bf16[256,2048]{1,0:T(8,128)(2,1)}) %reduce-scatter.7.cloned.1.call-update) | async-done | bytes 1048592 | tf_op jit(solution)/shard_map/reduce_scatter | solution.py:134
  273.7 21.5 %gather_fusion = bf16[2560,2048]{1,0:T(8,128)(2,1)} fusion(bf16[256,2048]{1,0:T(8,128)(2,1)} %multiply_convert_fusion.2, s32[3072]{0:T(1024)S(1)} %pad_clamp_fusion.1), kind=kCustom, calls=%fused_computation | custom fusion | bytes 20981760 | tf_op jit(solution)/shard_map/gather | solution.py:158
  300.9 232.2 %all_to_all.20 = bf16[32,80,2048]{2,1,0:T(8,128)(2,1)S(1)} all-to-all(bf16[32,80,2048]{2,1,0:T(8,128)(2,1)S(1)} %broadcast_select_fusion.1), channel_id=1, replica_groups=mesh['dp'=4,'exp'=2,'col'=4] {'dp','exp','col'}, dimensions={0} | all-to-all | bytes 20971520 | tf_op jit(solution)/shard_map/all_to_all | solution.py:33
  580.6 16.8 gather_fusion.4
  597.6 204.4 %all-to-all-done.1 = bf16[32,80,2048]{2,1,0:T(8,128)(2,1)} async-done(((bf16[32,80,2048]{2,1,0:T(8,128)(2,1)}), bf16[32,80,2048]{2,1,0:T(8,128)(2,1)}, u32[]{:S(2)}, u32[]{:S(2)}) %all-to-all-start.1) | async-done | bytes 10485792 | tf_op jit(solution)/shard_map/all_to_all | solution.py:33
  802.0 21.6 %gather_fusion.1 = bf16[2048,2048]{1,0:T(8,128)(2,1)} fusion(bf16[2560,2048]{1,0:T(8,128)(2,1)} %bitcast.18, s32[2048]{0:T(1024)S(1)} %broadcast_clamp_fusion), kind=kCustom, calls=%fused_computation.1 | custom fusion | bytes 16785408 | tf_op jit(solution)/shard_map/gather | solution.py:179
  838.8 24.6 %gather_fusion.2 = bf16[2560,2048]{1,0:T(8,128)(2,1)} fusion(bf16[2048,2048]{1,0:T(8,128)(2,1)} %fusion.52, s32[3072]{0:T(1024)S(1)} %pad_clamp_fusion), kind=kCustom, calls=%fused_computation.2 | custom fusion | bytes 20981760 | tf_op jit(solution)/shard_map/gather | solution.py:190
  869.1 237.5 %all_to_all.21 = bf16[32,80,2048]{2,1,0:T(8,128)(2,1)} all-to-all(bf16[32,80,2048]{2,1,0:T(8,128)(2,1)S(1)} %broadcast_select_fusion), channel_id=1, replica_groups=mesh['dp'=4,'exp'=2,'col'=4] {'dp','exp','col'}, dimensions={0} | all-to-all | bytes 20971520 | tf_op jit(solution)/shard_map/all_to_all | solution.py:33
  1106.6 19.1 multiply_convert_fusion
  1139.3 16.0 add_convert_fusion
  1160.2 225.9 %all-to-all-done.3 = bf16[32,80,2048]{2,1,0:T(8,128)(2,1)} async-done(((bf16[32,80,2048]{2,1,0:T(8,128)(2,1)}), bf16[32,80,2048]{2,1,0:T(8,128)(2,1)}, u32[]{:S(2)}, u32[]{:S(2)}) %all-to-all-start.3) | async-done | bytes 10485792 | tf_op jit(solution)/shard_map/all_to_all | solution.py:33
  1386.0 21.6 %gather_fusion.3 = bf16[2048,2048]{1,0:T(8,128)(2,1)} fusion(bf16[2560,2048]{1,0:T(8,128)(2,1)} %bitcast.25, s32[2048]{0:T(1024)S(1)} %broadcast_clamp_fusion), kind=kCustom, calls=%fused_computation.3 | custom fusion | bytes 16785408 | tf_op jit(solution)/shard_map/gather | solution.py:209
  1425.8 86.0 %all-gather.11.cloned.1.call-done = bf16[1024,2048]{1,0:T(8,128)(2,1)} async-done(((bf16[256,2048]{1,0:T(8,128)(2,1)}), bf16[1024,2048]{1,0:T(8,128)(2,1)}) %all-gather.11.cloned.1.call-update) | async-done | bytes 4194320 | tf_op jit(solution)/shard_map/all_gather | solution.py:225
  1521.2 125.5 %while.31 = (s32[]{:T(128)}, f32[1024,1,128]{0,2,1:T(8,128)}, f32[1024,1,128]{0,2,1:T(8,128)}, f32[2,512,1,8,128]{4,3,1,0,2:T(8,128)}, s32[2]{0:T(128)S(1)}, /*i...) while((s32[]{:T(128)}, f32[1024,1,128]{0,2,1:T(8,128)}, ...), condition=%wide.region_21.22_spmd.clone, body=%wide.region_19.21_spmd.clone.sunk | while | flops 5408158208 | bytes 274551296 | solution.py:260
  1550.2 15.1 fusion.210
  1612.5 15.1 fusion.210
  1763.7 17.6 reduce-scatter.17.cloned.1.call-done
  1783.5 52.6 %reduce-scatter.11.cloned.1.call-done = bf16[256,1024]{1,0:T(8,128)(2,1)} async-done(((bf16[2048,1024]{1,0:T(8,128)(2,1)}), bf16[256,1024]{1,0:T(8,128)(2,1)}) %reduce-scatter.11.cloned.1.call-update) | async-done | bytes 524304 | tf_op jit(solution)/shard_map/reduce_scatter | solution.py:281
  1838.2 76.9 %reduce-scatter.9.cloned.1.call-done = bf16[256,2048]{1,0:T(8,128)(2,1)} async-done(((bf16[1024,2048]{1,0:T(8,128)(2,1)}), bf16[256,2048]{1,0:T(8,128)(2,1)}) %reduce-scatter.9.cloned.1.call-update) | async-done | bytes 1048592 | tf_op jit(solution)/shard_map/reduce_scatter | solution.py:272
  1924.4 41.2 %all-reduce.4 = (f32[2048]{0:T(1024)}, f32[128]{0:T(128)}, f32[128]{0:T(128)}, f32[2048]{0:T(1024)}) all-reduce(f32[2048]{0:T(1024)S(1)} %get-tuple-element.359, f32[128]{0:T(128)S(1)} %get-tuple-element.355, f32[128]{0:T(128)S(1)} %get-tuple-element.361, ...), channel_id=1, replica_groups=mesh['dp'=4,'exp'=2,'col'=4] {'dp','exp','col'}, use_global_device_ids=true, to_apply=%region_27.28 | all-reduce | flops 4352 | bytes 34816 | tf_op jit(solution)/shard_map/psum | solution.py:294
  1965.6 81.1 %all-reduce.7.cloned.1.call-done = f32[2048,32]{0,1:T(8,128)} async-done(((f32[2048,32]{0,1:T(8,128)}), f32[2048,32]{0,1:T(8,128)}) %all-reduce.7.cloned.1.call-update) | async-done | bytes 262160 | tf_op jit(solution)/shard_map/psum | solution.py:294
  (370 shorter events, 462.6 us)
Async XLA Ops:
  7.2 550.9 %copy-start = (bf16[1,768,2048]{2,1,0:T(8,128)(2,1)S(1)}, bf16[1,768,2048]{2,1,0:T(8,128)(2,1)}, u32[]{:S(2)}) copy-start(bf16[1,768,2048]{2,1,0:T(8,128)(2,1)} %param.35) | copy-start | bytes 9437188
  7.2 89.0 %all-gather.5.cloned.1.call-start = ((), (), s32[]{:S(2)}) async-start(), calls=%async_computation.10 | async-start | bytes 5242880 | tf_op jit(solution)/shard_map/all_gather | solution.py:74
  12.6 97.4 %all-gather.7.cloned.1.call-start = ((), (), s32[]{:S(2)}) async-start(), calls=%async_computation.11 | async-start | bytes 6291456 | tf_op jit(solution)/shard_map/all_gather | solution.py:76
  13.4 167.9 %all-gather.9.cloned.1.call-start = ((), (), s32[]{:S(2)}) async-start(), calls=%async_computation.12 | async-start | bytes 6291456 | tf_op jit(solution)/shard_map/all_gather | solution.py:79
  14.1 254.6 %reduce-scatter.7.cloned.1.call-start = ((), (), s32[]{:S(2)}) async-start(), calls=%async_computation.13 | async-start | bytes 5242880 | tf_op jit(solution)/shard_map/reduce_scatter | solution.py:134
  300.8 232.2 %copy-start.78 = (bf16[1,2048,768]{2,1,0:T(8,128)(2,1)S(1)}, bf16[1,2048,768]{2,1,0:T(8,128)(2,1)}, u32[]{:S(2)}) copy-start(bf16[1,2048,768]{2,1,0:T(8,128)(2,1)} %param.33) | copy-start | bytes 9437188
  571.1 230.9 %all-to-all-start.1 = ((bf16[32,80,2048]{2,1,0:T(8,128)(2,1)}), bf16[32,80,2048]{2,1,0:T(8,128)(2,1)}, u32[]{:S(2)}, u32[]{:S(2)}) async-start(bf16[32,80,2048]{2,1,0:T(8,128)(2,1)} %bitcast.371), calls=%async_computation.2 | async-start | bytes 20971520 | tf_op jit(solution)/shard_map/all_to_all | solution.py:33
  832.7 327.4 %copy-start.47 = (f32[256,8]{0,1:T(8,128)}, f32[256,8]{0,1:T(8,128)S(1)}, u32[]{:S(2)}) copy-start(f32[256,8]{0,1:T(8,128)S(1)} %get-tuple-element.402) | copy-start | bytes 24580
  1155.3 230.7 %all-to-all-start.3 = ((bf16[32,80,2048]{2,1,0:T(8,128)(2,1)}), bf16[32,80,2048]{2,1,0:T(8,128)(2,1)}, u32[]{:S(2)}, u32[]{:S(2)}) async-start(bf16[32,80,2048]{2,1,0:T(8,128)(2,1)} %bitcast.372), calls=%async_computation.4 | async-start | bytes 20971520 | tf_op jit(solution)/shard_map/all_to_all | solution.py:33
  1159.9 351.9 %all-gather.11.cloned.1.call-start = ((), (), s32[]{:S(2)}) async-start(), calls=%async_computation.14 | async-start | bytes 5242880 | tf_op jit(solution)/shard_map/all_gather | solution.py:225
  1160.2 259.0 %copy-start.40 = (bf16[256,32]{0,1:T(8,128)(2,1)}, bf16[256,32]{0,1:T(8,128)(2,1)S(1)}, u32[]{:S(2)}) copy-start(bf16[256,32]{0,1:T(8,128)(2,1)S(1)} %select_reduce_fusion) | copy-start | bytes 49156
  1425.6 335.0 %reduce-scatter.13.cloned.1.call-start = ((), (), s32[]{:S(2)}) async-start(), calls=%async_computation.17 | async-start | bytes 589824 | tf_op jit(solution)/shard_map/reduce_scatter | solution.py:284
  1655.6 106.6 %reduce-scatter.15.cloned.1.call-start = ((), (), s32[]{:S(2)}) async-start(), calls=%async_computation.18 | async-start | bytes 589824 | tf_op jit(solution)/shard_map/reduce_scatter | solution.py:287
  1660.2 121.1 %reduce-scatter.17.cloned.1.call-start = ((), (), s32[]{:S(2)}) async-start(), calls=%async_computation.19 | async-start | bytes 4718592 | tf_op jit(solution)/shard_map/reduce_scatter | solution.py:290
  1668.9 167.2 %reduce-scatter.11.cloned.1.call-start = ((), (), s32[]{:S(2)}) async-start(), calls=%async_computation.16 | async-start | bytes 4718592 | tf_op jit(solution)/shard_map/reduce_scatter | solution.py:281
  1699.2 215.8 %reduce-scatter.9.cloned.1.call-start = ((), (), s32[]{:S(2)}) async-start(), calls=%async_computation.15 | async-start | bytes 5242880 | tf_op jit(solution)/shard_map/reduce_scatter | solution.py:272
  1711.6 335.1 %all-reduce.7.cloned.1.call-start = ((), (), s32[]{:S(2)}) async-start(), calls=%async_computation.20 | async-start | bytes 524288 | tf_op jit(solution)/shard_map/psum | solution.py:294
  1749.4 165.7 %copy-start.49 = (f32[2048]{0:T(1024)S(1)}, f32[2048]{0:T(1024)}, u32[]{:S(2)}) copy-start(f32[2048]{0:T(1024)} %param.24) | copy-start | bytes 24580
  1749.4 165.6 %copy-start.63 = (f32[256]{0:T(256)S(1)}, f32[256]{0:T(256)}, u32[]{:S(2)}) copy-start(f32[256]{0:T(256)} %copy-done.62) | copy-start | bytes 3076
  1760.6 154.5 %copy-start.9 = (bf16[256,2048]{1,0:T(8,128)(2,1)S(1)}, bf16[256,2048]{1,0:T(8,128)(2,1)}, u32[]{:S(2)}) copy-start(bf16[256,2048]{1,0:T(8,128)(2,1)} %param.20) | copy-start | bytes 3145732
  1760.6 156.8 %copy-start.67 = (f32[256]{0:T(256)S(1)}, f32[256]{0:T(256)}, u32[]{:S(2)}) copy-start(f32[256]{0:T(256)} %copy-done.66) | copy-start | bytes 3076
  1760.6 156.8 %copy-start.44 = (f32[2048]{0:T(1024)S(1)}, f32[2048]{0:T(1024)}, u32[]{:S(2)}) copy-start(f32[2048]{0:T(1024)} %param.31) | copy-start | bytes 24580
  1760.6 156.8 %copy-start.61 = (f32[256]{0:T(256)S(1)}, f32[256]{0:T(256)}, u32[]{:S(2)}) copy-start(f32[256]{0:T(256)} %copy-done.59) | copy-start | bytes 3076
  1760.6 156.8 %copy-start.65 = (f32[256]{0:T(256)S(1)}, f32[256]{0:T(256)}, u32[]{:S(2)}) copy-start(f32[256]{0:T(256)} %copy-done.64) | copy-start | bytes 3076
  (85 other events, 2088.4 us)
Sparse Core Ops, SparseCore 0:
  12.8 83.4 all-gather.4
  97.8 12.2 all-gather.6
  111.6 14.8 all-gather.8
  190.8 77.9 reduce-scatter.6
  1425.8 85.9 all-gather.10
  1655.7 32.6 reduce-scatter.12
  1692.1 34.1 reduce-scatter.14
  1730.0 51.3 reduce-scatter.16
  1784.7 51.2 reduce-scatter.10
  1838.3 76.7 reduce-scatter.8
  1921.2 125.5 all-reduce.6
where the time goes:
time: 2070 us; the launch traced here: 2060 us
  waiting for transfers between devices  874 us (42%)
  blocking collectives  517 us (25%)
  matrix products  309 us (15%)
  local copies, waits for them, and re-layouts  164 us (8%)
  other arithmetic  152 us (7%)
    all_to_all x2, blocking collectives, route_rows(): lax.all_to_all(buffer, ('dp', 'exp', 'col'), split_axis=0, concat_axis=0,...  470 us
    all_to_all x2, waiting for transfers between devices, route_rows(): lax.all_to_all(buffer, ('dp', 'exp', 'col'), split_axis=0, concat_axis=0,...  430 us
    all_gather x1, waiting for transfers between devices, local(): lax.all_gather(grad_hidden.astype(jnp.bfloat16), 'col', axis=0, tiled=True)  86 us
    psum x1, waiting for transfers between devices, local(): lax.psum((grad_attn_gain, grad_query_gain, grad_key_gain, grad_moe_gain,...  81.1 us
    reduce_scatter x1, waiting for transfers between devices, local(): lax.psum_scatter((total_rows + contract_last(grad_v_low, full_value)).ast...  76.9 us
    all_gather x1, waiting for transfers between devices, local(): lax.all_gather(normed.astype(jnp.bfloat16), 'col', axis=0, tiled=True)  72.5 us
    dot_general x8, matrix products, contract_last(): lax.dot_general(left_side, right_side, (((1,), (1,)), ((), ())), preferre...  71.4 us
    dot_general x8, matrix products, contract_first(): lax.dot_general(left_side, right_side, (((0,), (0,)), ((), ())), preferre...  67.3 us
  transfers between devices with their start and end apart: 13, of which 10 were waited for; matrix products, arithmetic and copies ran while one was open for 12% of the time, Pallas kernels for 0%

commit v1 on v0

v1 whole, which is shorter than its diff:
```python
import functools

import jax
import jax.numpy as jnp
from jax import lax
from jax.experimental import pallas as pl
from jax.experimental.pallas import tpu as pltpu
from jax.sharding import PartitionSpec as P

epsilon = 1e-06
rotary_base = 1000000.0
plane = ("dp", "exp")
everyone = ("dp", "exp", "col")
f32 = jnp.float32
bf16 = jnp.bfloat16


def dot_nn(a, b):
    return lax.dot_general(a, b, (((1,), (0,)), ((), ())), preferred_element_type=f32)


def dot_nt(a, b):
    return lax.dot_general(a, b, (((1,), (1,)), ((), ())), preferred_element_type=f32)


def dot_tn(a, b):
    return lax.dot_general(a, b, (((0,), (0,)), ((), ())), preferred_element_type=f32)


def inverse_rms(rows):
    return lax.rsqrt(jnp.mean(rows * rows, axis=-1, keepdims=True) + epsilon)


def rotary_tables(positions, head_size):
    halves = head_size // 2
    frequency = rotary_base ** (-2.0 * jnp.arange(halves, dtype=f32) / head_size)
    angles = positions.astype(f32)[:, None] * frequency[None, :]
    cosine, sine = jnp.cos(angles), jnp.sin(angles)
    return (
        jnp.concatenate([cosine, cosine], axis=1),
        jnp.concatenate([-sine, sine], axis=1),
    )


def turn(rows, cosine, sine):
    return rows * cosine + pltpu.roll(rows, rows.shape[-1] // 2, 1) * sine


def turn_back(rows, cosine, sine):
    return rows * cosine - pltpu.roll(rows, rows.shape[-1] // 2, 1) * sine


def place_of(col_ref, blocks, tokens, true_block):
    return pl.multiple_of(lax.rem(col_ref[0] - true_block + blocks, blocks) * tokens, tokens)


def softmax_rows(query, keys_ref, first, tokens, scale):
    diagonal = dot_nt(query, keys_ref[pl.ds(first, tokens), :])
    row = lax.broadcasted_iota(jnp.int32, diagonal.shape, 0)
    column = lax.broadcasted_iota(jnp.int32, diagonal.shape, 1)
    diagonal = jnp.where(row >= column, diagonal * scale, -1e30)
    peak = jnp.max(diagonal, axis=1, keepdims=True)
    if first:
        former = dot_nt(query, keys_ref[pl.ds(0, first), :]) * scale
        peak = jnp.maximum(peak, jnp.max(former, axis=1, keepdims=True))
        former = jnp.exp(former - peak)
        diagonal = jnp.exp(diagonal - peak)
        inverse = 1.0 / (
            jnp.sum(former, axis=1, keepdims=True) + jnp.sum(diagonal, axis=1, keepdims=True)
        )
        return former * inverse, diagonal * inverse
    diagonal = jnp.exp(diagonal - peak)
    return None, diagonal / jnp.sum(diagonal, axis=1, keepdims=True)


def forward_kernel(
    blocks, tokens, scale, col_ref, q_ref, k_ref, v_ref, cos_ref, sin_ref, qg_ref, kg_ref, out_ref, keys, values
):
    @pl.when(pl.program_id(0) == 0)
    def _():
        for block in range(blocks):
            here = pl.ds(place_of(col_ref, blocks, tokens, block), tokens)
            there = pl.ds(block * tokens, tokens)
            raw = k_ref[here, :]
            rows = raw * inverse_rms(raw) * kg_ref[...]
            keys[there, :] = turn(rows, cos_ref[there, :], sin_ref[there, :]).astype(bf16)
            values[there, :] = v_ref[here, :].astype(bf16)

    for block in range(blocks):
        here = pl.ds(place_of(col_ref, blocks, tokens, block), tokens)
        first = block * tokens
        there = pl.ds(first, tokens)
        raw = q_ref[here, :]
        rows = raw * inverse_rms(raw) * qg_ref[...]
        query = turn(rows, cos_ref[there, :], sin_ref[there, :]).astype(bf16)
        former, diagonal = softmax_rows(query, keys, first, tokens, scale)
        mixed = dot_nn(diagonal.astype(bf16), values[there, :])
        if first:
            mixed = mixed + dot_nn(former.astype(bf16), values[pl.ds(0, first), :])
        out_ref[here, :] = mixed.astype(bf16)


def attention_forward(col, qkv, cosine, sine, query_gain, key_gain, heads, tokens):
    seq_len, head_size = qkv.shape[0], query_gain.shape[-1]
    column = lambda index: pl.BlockSpec((seq_len, head_size), index)
    whole = pl.BlockSpec((seq_len, head_size), lambda h, c: (0, 0))
    gain = pl.BlockSpec((1, head_size), lambda h, c: (0, 0))
    return pl.pallas_call(
        functools.partial(forward_kernel, seq_len // tokens, tokens, head_size ** (-0.5)),
        out_shape=jax.ShapeDtypeStruct((seq_len, heads * head_size), bf16),
        grid_spec=pltpu.PrefetchScalarGridSpec(
            num_scalar_prefetch=1,
            grid=(heads,),
            in_specs=[
                column(lambda h, c: (0, h)),
                column(lambda h, c: (0, heads)),
                column(lambda h, c: (0, heads + 1)),
                whole,
                whole,
                gain,
                gain,
            ],
            out_specs=column(lambda h, c: (0, h)),
            scratch_shapes=[
                pltpu.VMEM((seq_len, head_size), bf16),
                pltpu.VMEM((seq_len, head_size), bf16),
            ],
        ),
        compiler_params=pltpu.CompilerParams(vmem_limit_bytes=40 * 2**20),
        cost_estimate=pl.CostEstimate(
            flops=3 * heads * seq_len * seq_len * head_size,
            bytes_accessed=6 * seq_len * heads * head_size,
            transcendentals=heads * seq_len * seq_len // 2,
        ),
        name="attention_forward",
    )(col, qkv, qkv, qkv, cosine, sine, query_gain, key_gain)


def backward_kernel(
    blocks, tokens, scale, heads,
    col_ref, q_ref, k_ref, v_ref, g_ref, cos_ref, sin_ref, qg_ref, kg_ref,
    grad_ref, qgain_ref, kgain_ref,
    keys, values, grad_keys, grad_values,
):
    step = pl.program_id(0)

    @pl.when(step == 0)
    def _():
        for block in range(blocks):
            here = pl.ds(place_of(col_ref, blocks, tokens, block), tokens)
            there = pl.ds(block * tokens, tokens)
            raw = k_ref[here, :]
            rows = raw * inverse_rms(raw) * kg_ref[...]
            keys[there, :] = turn(rows, cos_ref[there, :], sin_ref[there, :]).astype(bf16)
            values[there, :] = v_ref[here, :].astype(bf16)
        grad_keys[...] = jnp.zeros_like(grad_keys)
        grad_values[...] = jnp.zeros_like(grad_values)
        qgain_ref[...] = jnp.zeros_like(qgain_ref)
        kgain_ref[...] = jnp.zeros_like(kgain_ref)

    def through_norm(grad_rot, unit, inverse, there, gain_ref, gain_grad_ref):
        grad_scaled = turn_back(grad_rot, cos_ref[there, :], sin_ref[there, :])
        gain_grad_ref[0:1, :] += jnp.sum(grad_scaled * unit, axis=0, keepdims=True)
        grad_unit = grad_scaled * gain_ref[...]
        return inverse * (grad_unit - unit * jnp.mean(grad_unit * unit, axis=1, keepdims=True))

    @pl.when(step < heads)
    def _():
        for block in range(blocks):
            here = pl.ds(place_of(col_ref, blocks, tokens, block), tokens)
            first = block * tokens
            there = pl.ds(first, tokens)
            raw = q_ref[here, :]
            inverse = inverse_rms(raw)
            unit = raw * inverse
            query = turn(unit * qg_ref[...], cos_ref[there, :], sin_ref[there, :]).astype(bf16)
            grad_mixed = g_ref[here, :]
            former, diagonal = softmax_rows(query, keys, first, tokens, scale)
            grad_diagonal = dot_nt(grad_mixed, values[there, :])
            inner = jnp.sum(diagonal * grad_diagonal, axis=1, keepdims=True)
            if first:
                before = pl.ds(0, first)
                grad_former = dot_nt(grad_mixed, values[before, :])
                inner = inner + jnp.sum(former * grad_former, axis=1, keepdims=True)
                score_former = (former * (grad_former - inner)).astype(bf16)
                grad_keys[before, :] += dot_tn(score_former, query)
                grad_values[before, :] += dot_tn(former.astype(bf16), grad_mixed)
            score_diagonal = (diagonal * (grad_diagonal - inner)).astype(bf16)
            grad_keys[there, :] += dot_tn(score_diagonal, query)
            grad_values[there, :] += dot_tn(diagonal.astype(bf16), grad_mixed)
            grad_query = dot_nn(score_diagonal, keys[there, :])
            if first:
                grad_query = grad_query + dot_nn(score_former, keys[before, :])
            grad_ref[here, :] = through_norm(
                grad_query * scale, unit, inverse, there, qg_ref, qgain_ref
            ).astype(bf16)

    @pl.when(step == heads)
    def _():
        for block in range(blocks):
            here = pl.ds(place_of(col_ref, blocks, tokens, block), tokens)
            there = pl.ds(block * tokens, tokens)
            raw = k_ref[here, :]
            inverse = inverse_rms(raw)
            grad_ref[here, :] = through_norm(
                grad_keys[there, :] * scale, raw * inverse, inverse, there, kg_ref, kgain_ref
            ).astype(bf16)

    @pl.when(step == heads + 1)
    def _():
        for block in range(blocks):
            here = pl.ds(place_of(col_ref, blocks, tokens, block), tokens)
            grad_ref[here, :] = grad_values[pl.ds(block * tokens, tokens), :].astype(bf16)


def attention_backward(col, qkv, grad_attended, cosine, sine, query_gain, key_gain, heads, tokens):
    seq_len, head_size = qkv.shape[0], query_gain.shape[-1]
    column = lambda index: pl.BlockSpec((seq_len, head_size), index)
    whole = pl.BlockSpec((seq_len, head_size), lambda h, c: (0, 0))
    gain = pl.BlockSpec((1, head_size), lambda h, c: (0, 0))
    gain_out = pl.BlockSpec((8, head_size), lambda h, c: (0, 0))
    last = heads - 1
    return pl.pallas_call(
        functools.partial(backward_kernel, seq_len // tokens, tokens, head_size ** (-0.5), heads),
        out_shape=(
            jax.ShapeDtypeStruct(qkv.shape, bf16),
            jax.ShapeDtypeStruct((8, head_size), f32),
            jax.ShapeDtypeStruct((8, head_size), f32),
        ),
        grid_spec=pltpu.PrefetchScalarGridSpec(
            num_scalar_prefetch=1,
            grid=(heads + 2,),
            in_specs=[
                column(lambda h, c: (0, jnp.minimum(h, last))),
                column(lambda h, c: (0, heads)),
                column(lambda h, c: (0, heads + 1)),
                column(lambda h, c: (0, jnp.minimum(h, last))),
                whole,
                whole,
                gain,
                gain,
            ],
            out_specs=(column(lambda h, c: (0, h)), gain_out, gain_out),
            scratch_shapes=[
                pltpu.VMEM((seq_len, head_size), bf16),
                pltpu.VMEM((seq_len, head_size), bf16),
                pltpu.VMEM((seq_len, head_size), f32),
                pltpu.VMEM((seq_len, head_size), f32),
            ],
        ),
        compiler_params=pltpu.CompilerParams(vmem_limit_bytes=48 * 2**20),
        cost_estimate=pl.CostEstimate(
            flops=7 * heads * seq_len * seq_len * head_size,
            bytes_accessed=8 * seq_len * heads * head_size,
            transcendentals=heads * seq_len * seq_len // 2,
        ),
        name="attention_backward",
    )(col, qkv, qkv, qkv, grad_attended, cosine, sine, query_gain, key_gain)


def local(
    inputs,
    expert_ids,
    positions,
    cotangent,
    attn_gain,
    query_proj,
    key_projection,
    value_projection,
    query_norm_gain,
    key_norm_gain,
    out_proj,
    moe_gain,
    router,
    gate_proj,
    up_proj,
    down_proj,
):
    tokens, width = inputs.shape
    head_size = query_norm_gain.shape[0]
    choices = expert_ids.shape[1]
    experts = router.shape[1]
    capacity = tokens * choices * 5 // (4 * experts)
    columns = lax.axis_size("col")
    peers = lax.axis_size("dp") * lax.axis_size("exp")
    col = lax.axis_index("col")
    col_array = jnp.reshape(col, (1,)).astype(jnp.int32)
    heads = query_proj.shape[1] // head_size
    assert key_projection.shape[1] == head_size and experts == peers * columns
    around = [(i, (i + 1) % columns) for i in range(columns)]

    def shift(block):
        return lax.ppermute(block, "col", around)

    def ring_gather(block):
        blocks = [block]
        for _ in range(columns - 1):
            blocks.append(shift(blocks[-1]))
        return blocks

    def ring_sum(part_of):
        running = part_of(1)
        for step in range(2, columns + 1):
            running = shift(running.astype(bf16)).astype(f32) + part_of(step % columns)
        return running

    def swap(rows):
        return lax.all_to_all(
            rows.reshape(peers, rows.shape[0] // peers, *rows.shape[1:]), plane, 0, 0, tiled=True
        ).reshape(rows.shape)

    def true_block(step):
        return lax.rem(col - step + columns, columns)

    local_qkv = jnp.concatenate([query_proj, key_projection, value_projection], axis=1)
    full_qkv = lax.all_gather(local_qkv, "exp", axis=0, tiled=True)
    full_out = lax.all_gather(out_proj, "exp", axis=0, tiled=True)

    input_blocks = ring_gather(inputs)
    sequence_in = jnp.concatenate(input_blocks, axis=0).astype(f32)
    inverse_in = inverse_rms(sequence_in)
    sequence = (sequence_in * inverse_in * attn_gain).astype(bf16)
    qkv = dot_nn(sequence, full_qkv)
    cosine, sine = rotary_tables(positions, head_size)
    query_gain, key_gain = query_norm_gain[None, :], key_norm_gain[None, :]
    attended = attention_forward(
        col_array, qkv, cosine, sine, query_gain, key_gain, heads, tokens
    )

    def rows_of(array, step):
        return lax.slice_in_dim(array, step * tokens, (step + 1) * tokens, axis=0)

    branch = ring_sum(lambda step: dot_nt(rows_of(attended, step), full_out))
    hidden = inputs.astype(f32) + branch
    inverse_hidden = inverse_rms(hidden)
    routed = (hidden * inverse_hidden * moe_gain).astype(bf16)

    gathered_ids = lax.all_gather(expert_ids, "col", axis=0)
    earlier = (
        lax.broadcasted_iota(jnp.int32, (tokens, tokens), 0)
        < lax.broadcasted_iota(jnp.int32, (tokens, tokens), 1)
    ).astype(bf16)

    def slots_of(ids, named):
        chosen = jnp.any(ids.T[None, :, :] == named[:, None, None], axis=1)
        rank = dot_nn(chosen.astype(bf16), earlier)
        code = jnp.where(chosen, rank, -1.0)
        place = lax.broadcasted_iota(jnp.int32, (1, capacity, 1), 1).astype(f32)
        return chosen, code[:, None, :] == place

    plane_experts = jnp.arange(peers, dtype=jnp.int32) * columns + col
    slot_mats = []
    for step in range(columns):
        ids = lax.dynamic_index_in_dim(gathered_ids, true_block(step), 0, keepdims=False)
        _, slots = slots_of(ids, plane_experts)
        slot_mats.append(slots.astype(bf16).reshape(peers * capacity, tokens))
    chosen_all, slots_all = slots_of(expert_ids, jnp.arange(experts, dtype=jnp.int32))

    def dispatch(step, block):
        return swap(dot_nn(slot_mats[step], block).astype(bf16))

    gate_weight, up_weight, down_weight = gate_proj[0], up_proj[0], down_proj[0]
    cotangent_rows = [dispatch(s, b) for s, b in enumerate(ring_gather(cotangent))]
    drive = [dot_nt(rows, down_weight) for rows in cotangent_rows]

    logits = dot_general_t(router, routed)
    logits = jnp.where(chosen_all, logits, -1e30)
    exponent = jnp.exp(logits - jnp.max(logits, axis=0, keepdims=True))
    exponent = jnp.where(chosen_all, exponent, 0.0)
    gates = exponent / jnp.sum(exponent, axis=0, keepdims=True)

    def swap_all(values):
        return lax.all_to_all(values, everyone, 0, 0, tiled=True)

    gate_slots = swap_all(jnp.sum(jnp.where(slots_all, gates[:, None, :], 0.0), axis=2))
    gate_slots = gate_slots.reshape(peers, columns, capacity)

    def ring_slots(values, step):
        return lax.dynamic_index_in_dim(values, true_block(step), 1, keepdims=False)

    arrived = [dispatch(s, b) for s, b in enumerate(ring_gather(routed))]
    acted_rows, gate_grads, up_grads, weighted_rows, row_grads, gate_dots = [], [], [], [], [], []
    for step in range(columns):
        gate_part = dot_nn(arrived[step], gate_weight)
        up_part = dot_nn(arrived[step], up_weight)
        sigmoid = jax.nn.sigmoid(gate_part)
        silu = gate_part * sigmoid
        acted = silu * up_part
        weight = ring_slots(gate_slots, step).reshape(peers * capacity, 1)
        grad_acted = drive[step] * weight
        gate_dots.append(jnp.sum(acted * drive[step], axis=1).reshape(peers, capacity))
        gate_grad = (grad_acted * up_part * sigmoid * (1.0 + gate_part * (1.0 - sigmoid))).astype(bf16)
        up_grad = (grad_acted * silu).astype(bf16)
        weighted_rows.append((acted * weight).astype(bf16))
        gate_grads.append(gate_grad)
        up_grads.append(up_grad)
        row_grads.append((dot_nt(gate_grad, gate_weight) + dot_nt(up_grad, up_weight)).astype(bf16))

    dots = jnp.stack(gate_dots, axis=1)
    order = lax.rem(col - jnp.arange(columns, dtype=jnp.int32) + columns, columns)
    dots = jnp.take(dots, order, axis=1).reshape(experts, capacity)
    dots = swap_all(dots)
    grad_gates = jnp.sum(jnp.where(slots_all, dots[:, :, None], 0.0), axis=1)
    grad_logits = (
        gates * (grad_gates - jnp.sum(gates * grad_gates, axis=0, keepdims=True))
    ).astype(bf16)

    def collect(rows):
        back = {s: swap(rows[s]) for s in [*range(1, columns), 0]}
        return ring_sum(lambda step: dot_tn(slot_mats[step], back[step]))

    grad_routed = collect(row_grads) + lax.dot_general(grad_logits, router, (((0,), (1,)), ((), ())), preferred_element_type=f32)
    upstream = cotangent.astype(f32)
    scaled = grad_routed * moe_gain
    grad_hidden = (
        upstream
        + scaled * inverse_hidden
        - hidden * (jnp.mean(hidden * scaled, axis=-1, keepdims=True) * inverse_hidden**3)
    )
    grad_moe_gain = jnp.sum(grad_routed * hidden * inverse_hidden, axis=0)
    grad_router = dot_general_t(routed, grad_logits)

    grad_sequence = jnp.concatenate(ring_gather(grad_hidden.astype(bf16)), axis=0)
    grad_attended = dot_nn(grad_sequence, full_out).astype(bf16)
    grad_qkv, grad_query_gain, grad_key_gain = attention_backward(
        col_array, qkv, grad_attended, cosine, sine, query_gain, key_gain, heads, tokens
    )
    grad_out_weight = dot_tn(grad_sequence, attended)
    partial_normed = dot_nt(grad_qkv, full_qkv)
    grad_attn_gain = jnp.sum(partial_normed * sequence_in * inverse_in, axis=0)
    grad_normed = ring_sum(lambda step: rows_of(partial_normed, step))
    input_rows = inputs.astype(f32)
    inverse_own = inverse_rms(input_rows)
    scaled_in = grad_normed * attn_gain
    grad_inputs = (
        grad_hidden
        + scaled_in * inverse_own
        - input_rows * (jnp.mean(input_rows * scaled_in, axis=-1, keepdims=True) * inverse_own**3)
    ).astype(bf16)
    grad_qkv_weight = dot_tn(sequence, grad_qkv)

    returned = [dot_nn(rows, down_weight).astype(bf16) for rows in weighted_rows]
    outputs = (hidden + collect(returned)).astype(bf16)

    arrived_all = jnp.concatenate(arrived, axis=0)
    grad_gate_weight = dot_tn(arrived_all, jnp.concatenate(gate_grads, axis=0))
    grad_up_weight = dot_tn(arrived_all, jnp.concatenate(up_grads, axis=0))
    grad_down = dot_tn(
        jnp.concatenate(weighted_rows, axis=0), jnp.concatenate(cotangent_rows, axis=0)
    )

    reduced_qkv = lax.psum_scatter(
        grad_qkv_weight.astype(bf16), plane, scatter_dimension=0, tiled=True
    ).astype(f32)
    reduced_out = lax.psum_scatter(
        grad_out_weight.astype(bf16), plane, scatter_dimension=0, tiled=True
    ).astype(f32)
    shared = lax.psum(
        (grad_attn_gain, grad_query_gain[0], grad_key_gain[0], grad_moe_gain, grad_router),
        everyone,
    )
    split = heads * head_size
    return (
        outputs,
        grad_inputs,
        shared[0],
        reduced_qkv[:, :split],
        reduced_qkv[:, split : split + head_size],
        reduced_qkv[:, split + head_size :],
        shared[1],
        shared[2],
        reduced_out,
        shared[3],
        shared[4],
        grad_gate_weight[None],
        grad_up_weight[None],
        grad_down[None],
    )


def dot_general_t(a, b):
    contract = (((0,), (1,)), ((), ()))
    return lax.dot_general(a, b, contract, preferred_element_type=f32)


def solution(mesh):
    return jax.shard_map(
        local,
        mesh=mesh,
        in_specs=(
            P(("dp", "exp", "col"), None),
            P(("dp", "exp", "col"), None),
            P(("dp", "exp")),
            P(("dp", "exp", "col"), None),
            P(),
            P("exp", "col"),
            P("exp", "col"),
            P("exp", "col"),
            P(),
            P(),
            P("exp", "col"),
            P(),
            P(),
            P(("dp", "exp", "col"), None, None),
            P(("dp", "exp", "col"), None, None),
            P(("dp", "exp", "col"), None, None),
        ),
        out_specs=(
            P(("dp", "exp", "col"), None),
            P(("dp", "exp", "col"), None),
            P(),
            P(("dp", "exp"), "col"),
            P(("dp", "exp"), "col"),
            P(("dp", "exp"), "col"),
            P(),
            P(),
            P(("dp", "exp"), "col"),
            P(),
            P(),
            P(("dp", "exp", "col"), None, None),
            P(("dp", "exp", "col"), None, None),
            P(("dp", "exp", "col"), None, None),
        ),
        check_vma=False,
    )
```

time: 2070 us -> 1130 us (0.55)
  waiting for transfers between devices: 874 us -> 472 us
  blocking collectives: 517 us -> 123 us
  local copies, waits for them, and re-layouts: 164 us -> 25.7 us
  other arithmetic: 152 us -> 59.4 us
  starting transfers between devices: 10.2 us -> 84.3 us
  Pallas kernels: 0 us -> 63.6 us
  matrix products: 309 us -> 267 us
    all_to_all x2 -> x1, blocking collectives: 470 us -> 9.1 us  [swap_all(): return lax.all_to_all(values, everyone, 0, 0, tiled=True)]
    ppermute x0 -> x24, waiting for transfers between devices: none -> 326 us  [shift(): return lax.ppermute(block, 'col', around)]
    all_to_all x2 -> x17, waiting for transfers between devices: 430 us -> 146 us  [the longest x16 139 us: swap(): lax.all_to_all(rows.reshape(peers, rows.shape[0] // peers, *rows.shape[1:...]
    reduce_scatter x6 -> x2, waiting for transfers between devices: 196 us -> 0.01 us  [the longest x1 0.01 us: local(): lax.psum_scatter(grad_out_weight.astype(bf16), plane, scatter_dimension=0...]
    all_gather x4 -> x2, waiting for transfers between devices: 165 us -> 0.02 us  [the longest x1 0.02 us: local(): full_qkv = lax.all_gather(local_qkv, 'exp', axis=0, tiled=True)]
    gather x9 -> x2, local copies, waits for them, and re-layouts: 107 us -> 0.56 us  [local(): dots = jnp.take(dots, order, axis=1).reshape(experts, capacity)]
    psum x1, waiting for transfers between devices: 81.1 us -> 0.14 us  [local(): lax.psum((grad_attn_gain, grad_query_gain[0], grad_key_gain[0], grad_moe_...]
    all_to_all x2 -> x17, starting transfers between devices: 9.35 us -> 77.5 us  [the longest x16 73.2 us: swap(): lax.all_to_all(rows.reshape(peers, rows.shape[0] // peers, *rows.shape[1:...]
  transfers between devices with their start and end apart: 13 -> 46, of which waited for: 10 -> 30; matrix products, arithmetic and copies ran while one was open for 12% -> 27% of each run, Pallas kernels for 0% -> 6%
where the time goes in v1:
time: 1130 us; the launch traced here: 1110 us
  waiting for transfers between devices  472 us (42%)
  matrix products  267 us (24%)
  blocking collectives  123 us (11%)
  starting transfers between devices  84.3 us (7%)
  Pallas kernels  63.6 us (6%)
  other arithmetic  59.4 us (5%)
  local copies, waits for them, and re-layouts  25.7 us (2%)
  between operations  15.2 us (1%)
    ppermute x24, waiting for transfers between devices, shift(): return lax.ppermute(block, 'col', around)  326 us
    all_to_all x16, waiting for transfers between devices, swap(): lax.all_to_all(rows.reshape(peers, rows.shape[0] // peers, *rows.shape[1:...  139 us
    dot_general x27, matrix products, dot_nn(): lax.dot_general(a, b, (((1,), (0,)), ((), ())), preferred_element_type=f32)  106 us
    dot_general x13, matrix products, dot_tn(): lax.dot_general(a, b, (((0,), (0,)), ((), ())), preferred_element_type=f32)  85.1 us
    all_to_all x16, starting transfers between devices, swap(): lax.all_to_all(rows.reshape(peers, rows.shape[0] // peers, *rows.shape[1:...  73.2 us
    dot_general x17, matrix products, dot_nt(): lax.dot_general(a, b, (((1,), (1,)), ((), ())), preferred_element_type=f32)  71.4 us
    psum x1, blocking collectives, local(): lax.psum((grad_attn_gain, grad_query_gain[0], grad_key_gain[0], grad_moe_...  63.1 us
    all_gather x1, blocking collectives, local(): gathered_ids = lax.all_gather(expert_ids, 'col', axis=0)  51.2 us
  transfers between devices with their start and end apart: 46, of which 30 were waited for; matrix products, arithmetic and copies ran while one was open for 27% of the time, Pallas kernels for 6%

profile of v1, /device:TPU:0, one launch (start us, length us, event | category | flops | bytes accessed | tf_op | source)
XLA Modules:
  0.0 1111.0 jit_solution(2421868503104675372)
XLA Ops:
  15.6 24.7 %collective-permute-done = bf16[256,2048]{1,0:T(8,128)(2,1)} collective-permute-done((bf16[256,2048]{1,0:T(8,128)(2,1)}, bf16[256,2048]{1,0:T(8,128)(2,1)}, u32[]{:S(2)}, u32[]{:S(2)}) %collective-permute-start) | collective-permute-done | bytes 1048608 | tf_op jit(solution)/shard_map/ppermute | solution.py:293
  40.5 51.2 %all-gather = s32[1024,8]{0,1:T(8,128)S(1)} all-gather(s32[256,8]{0,1:T(8,128)S(1)} %copy-done.62), channel_id=2, replica_groups=mesh['dp'=4,'exp'=2,'col'=4] {'col'}, dimensions={0}, use_global_device_ids=true | all-gather | bytes 40960 | tf_op jit(solution)/shard_map/all_gather | solution.py:338
  130.9 24.8 %attention_forward.1 = bf16[1024,1024]{1,0:T(8,128)(2,1)S(1)} custom-call(s32[1]{0:T(128)} %bitcast.col_ref, f32[1024,1280]{1,0:T(8,128)S(1)} %fusion.103.q_ref.k_ref.v_ref, f32[1024,1280]{1,0:T(8,128)S(1)} %fusion.103.q_ref.k_ref.v_ref, f32[1024,1280]{1,0:T(8,128)S(1)} %fusion.103.q_ref.k_ref.v_ref, f32[1024,128]{1,0:T(8,128)S(1)} %copy-done.2, ...), custom_call_target="tpu_custom_call" | custom-call | flops 3221225472 | bytes 6291456 | tf_op jit(solution)/shard_map/attention_forward/pallas_call | solution.py:108
  172.2 15.5 %collective-permute-done.3 = bf16[256,2048]{1,0:T(8,128)(2,1)} collective-permute-done((bf16[256,2048]{1,0:T(8,128)(2,1)}, bf16[256,2048]{1,0:T(8,128)(2,1)}, u32[]{:S(2)}, u32[]{:S(2)}) %collective-permute-start.3) | collective-permute-done | bytes 1048608 | tf_op jit(solution)/shard_map/ppermute | solution.py:293
  194.1 25.5 %collective-permute-done.4 = bf16[256,2048]{1,0:T(8,128)(2,1)S(1)} collective-permute-done((bf16[256,2048]{1,0:T(8,128)(2,1)S(1)}, bf16[256,2048]{1,0:T(8,128)(2,1)S(1)}, u32[]{:S(2)}, u32[]{:S(2)}) %collective-permute-start.4) | collective-permute-done | bytes 1048608 | tf_op jit(solution)/shard_map/ppermute | solution.py:293
  220.8 21.2 %collective-permute-done.14 = bf16[256,2048]{1,0:T(8,128)(2,1)S(1)} collective-permute-done((bf16[256,2048]{1,0:T(8,128)(2,1)}, bf16[256,2048]{1,0:T(8,128)(2,1)S(1)}, u32[]{:S(2)}, u32[]{:S(2)}) %collective-permute-start.14) | collective-permute-done | bytes 1048608 | tf_op jit(solution)/shard_map/ppermute | solution.py:293
  265.7 16.3 %all-to-all-done.11 = bf16[8,80,2048]{2,1,0:T(8,128)(2,1)} async-done(((bf16[8,80,2048]{2,1,0:T(8,128)(2,1)}), bf16[8,80,2048]{2,1,0:T(8,128)(2,1)}, u32[]{:S(2)}, u32[]{:S(2)}) %all-to-all-start.11) | async-done | bytes 2621472 | tf_op jit(solution)/shard_map/all_to_all | solution.py:308
  286.5 27.4 %collective-permute-done.6 = bf16[256,2048]{1,0:T(8,128)(2,1)S(1)} collective-permute-done((bf16[256,2048]{1,0:T(8,128)(2,1)}, bf16[256,2048]{1,0:T(8,128)(2,1)S(1)}, u32[]{:S(2)}, u32[]{:S(2)}) %collective-permute-start.6) | collective-permute-done | bytes 1048608 | tf_op jit(solution)/shard_map/ppermute | solution.py:293
  324.8 26.5 %collective-permute-done.16 = bf16[256,2048]{1,0:T(8,128)(2,1)} collective-permute-done((bf16[256,2048]{1,0:T(8,128)(2,1)}, bf16[256,2048]{1,0:T(8,128)(2,1)}, u32[]{:S(2)}, u32[]{:S(2)}) %collective-permute-start.16) | collective-permute-done | bytes 1048608 | tf_op jit(solution)/shard_map/ppermute | solution.py:293
  355.3 17.8 %collective-permute-done.8 = bf16[256,2048]{1,0:T(8,128)(2,1)} collective-permute-done((bf16[256,2048]{1,0:T(8,128)(2,1)}, bf16[256,2048]{1,0:T(8,128)(2,1)}, u32[]{:S(2)}, u32[]{:S(2)}) %collective-permute-start.8) | collective-permute-done | bytes 1048608 | tf_op jit(solution)/shard_map/ppermute | solution.py:293
  544.3 20.9 %all-to-all-done.10 = bf16[8,80,2048]{2,1,0:T(8,128)(2,1)} async-done(((bf16[8,80,2048]{2,1,0:T(8,128)(2,1)}), bf16[8,80,2048]{2,1,0:T(8,128)(2,1)}, u32[]{:S(2)}, u32[]{:S(2)}) %all-to-all-start.10) | async-done | bytes 2621472 | tf_op jit(solution)/shard_map/all_to_all | solution.py:308
  581.2 20.8 %all-to-all-done.12 = bf16[8,80,2048]{2,1,0:T(8,128)(2,1)} async-done(((bf16[8,80,2048]{2,1,0:T(8,128)(2,1)}), bf16[8,80,2048]{2,1,0:T(8,128)(2,1)}, u32[]{:S(2)}, u32[]{:S(2)}) %all-to-all-start.12) | async-done | bytes 2621472 | tf_op jit(solution)/shard_map/all_to_all | solution.py:308
  616.1 20.7 %collective-permute-done.13 = bf16[256,2048]{1,0:T(8,128)(2,1)S(1)} collective-permute-done((bf16[256,2048]{1,0:T(8,128)(2,1)S(1)}, bf16[256,2048]{1,0:T(8,128)(2,1)S(1)}, u32[]{:S(2)}, u32[]{:S(2)}) %collective-permute-start.13) | collective-permute-done | bytes 1048608 | tf_op jit(solution)/shard_map/ppermute | solution.py:293
  651.9 15.5 %collective-permute-done.15 = bf16[256,2048]{1,0:T(8,128)(2,1)} collective-permute-done((bf16[256,2048]{1,0:T(8,128)(2,1)}, bf16[256,2048]{1,0:T(8,128)(2,1)}, u32[]{:S(2)}, u32[]{:S(2)}) %collective-permute-start.15) | collective-permute-done | bytes 1048608 | tf_op jit(solution)/shard_map/ppermute | solution.py:293
  700.1 24.6 %collective-permute-done.18 = bf16[256,2048]{1,0:T(8,128)(2,1)S(1)} collective-permute-done((bf16[256,2048]{1,0:T(8,128)(2,1)S(1)}, bf16[256,2048]{1,0:T(8,128)(2,1)S(1)}, u32[]{:S(2)}, u32[]{:S(2)}) %collective-permute-start.18) | collective-permute-done | bytes 1048608 | tf_op jit(solution)/shard_map/ppermute | solution.py:293
  724.7 23.6 %collective-permute-done.19 = bf16[256,2048]{1,0:T(8,128)(2,1)S(1)} collective-permute-done((bf16[256,2048]{1,0:T(8,128)(2,1)S(1)}, bf16[256,2048]{1,0:T(8,128)(2,1)S(1)}, u32[]{:S(2)}, u32[]{:S(2)}) %collective-permute-start.19) | collective-permute-done | bytes 1048608 | tf_op jit(solution)/shard_map/ppermute | solution.py:293
  748.3 22.7 %collective-permute-done.20 = bf16[256,2048]{1,0:T(8,128)(2,1)S(1)} collective-permute-done((bf16[256,2048]{1,0:T(8,128)(2,1)S(1)}, bf16[256,2048]{1,0:T(8,128)(2,1)S(1)}, u32[]{:S(2)}, u32[]{:S(2)}) %collective-permute-start.20) | collective-permute-done | bytes 1048608 | tf_op jit(solution)/shard_map/ppermute | solution.py:293
  786.7 38.8 %attention_backward.1 = (bf16[1024,1280]{1,0:T(8,128)(2,1)S(1)}, f32[8,128]{1,0:T(8,128)S(1)}, f32[8,128]{1,0:T(8,128)S(1)}) custom-call(s32[1]{0:T(128)} %bitcast.col_ref, f32[1024,1280]{1,0:T(8,128)} %copy-done.1, f32[1024,1280]{1,0:T(8,128)} %copy-done.1, f32[1024,1280]{1,0:T(8,128)} %copy-done.1, ...), custom_call_target="tpu_custom_call" | custom-call | flops 7516192768 | bytes 8388608 | tf_op jit(solution)/shard_map/attention_backward/pallas_call | solution.py:223
  852.6 38.9 %all-to-all-done.2 = bf16[8,80,2048]{2,1,0:T(8,128)(2,1)} async-done(((bf16[8,80,2048]{2,1,0:T(8,128)(2,1)}), bf16[8,80,2048]{2,1,0:T(8,128)(2,1)}, u32[]{:S(2)}, u32[]{:S(2)}) %all-to-all-start.2) | async-done | bytes 2621472 | tf_op jit(solution)/shard_map/all_to_all | solution.py:308
  896.2 14.2 %fusion.36 = f32[1,2048,768]{2,1,0:T(8,128)} fusion(bf16[640,768]{1,0:T(8,128)(2,1)} %copy-done.48, bf16[640,768]{1,0:T(8,128)(2,1)} %copy-done.46, bf16[640,768]{1,0:T(8,128)(2,1)} %copy-done.44, bf16[640,768]{1,0:T(8,128)(2,1)} %copy-done.49, bf16[640,2048]{1,0:T(8,128)(2,1)} %bitcast.30, bf16[640,2048]{1,0:T(8,128)(2,1)} %bitcast.23, ...), kind=kOutput, calls=%fused_computation.48 | convolution fusion | flops 8110735360 | bytes 20709376 | tf_op jit(solution)/shard_map/dot_general | solution.py:27
  937.8 14.2 %fusion.39 = f32[1,2048,768]{2,1,0:T(8,128)} fusion(bf16[640,768]{1,0:T(8,128)(2,1)} %copy-done.45, bf16[640,768]{1,0:T(8,128)(2,1)} %copy-done.42, bf16[640,768]{1,0:T(8,128)(2,1)} %copy-done.40, bf16[640,768]{1,0:T(8,128)(2,1)} %copy-done.47, bf16[640,2048]{1,0:T(8,128)(2,1)} %bitcast.30, bf16[640,2048]{1,0:T(8,128)(2,1)} %bitcast.23, ...), kind=kOutput, calls=%fused_computation.49 | convolution fusion | flops 8110735360 | bytes 20709376 | tf_op jit(solution)/shard_map/dot_general | solution.py:27
  978.1 13.9 %fusion.42 = f32[1,768,2048]{2,1,0:T(8,128)} fusion(bf16[640,2048]{1,0:T(8,128)(2,1)} %bitcast.49, bf16[640,2048]{1,0:T(8,128)(2,1)} %bitcast.45, bf16[640,2048]{1,0:T(8,128)(2,1)} %bitcast.41, bf16[640,2048]{1,0:T(8,128)(2,1)} %bitcast.53, bf16[640,768]{1,0:T(8,128)(2,1)} %get-tuple-element.49, bf16[640,768]{1,0:T(8,128)(2,1)} %get-tuple-element.43, ...), kind=kOutput, calls=%fused_computation.50 | convolution fusion | flops 8110735360 | bytes 20709376 | tf_op jit(solution)/shard_map/dot_general | solution.py:27
  994.8 20.1 %collective-permute-done.22 = bf16[256,2048]{1,0:T(8,128)(2,1)} collective-permute-done((bf16[256,2048]{1,0:T(8,128)(2,1)}, bf16[256,2048]{1,0:T(8,128)(2,1)}, u32[]{:S(2)}, u32[]{:S(2)}) %collective-permute-start.22) | collective-permute-done | bytes 1048608 | tf_op jit(solution)/shard_map/ppermute | solution.py:293
  1024.8 63.1 %all-reduce = (f32[2048]{0:T(1024)}, f32[128]{0:T(128)}, f32[128]{0:T(128)}, f32[2048]{0:T(1024)}) all-reduce(f32[2048]{0:T(1024)S(1)} %get-tuple-element.80, f32[128]{0:T(128)S(1)} %slice_bitcast_fusion.1, f32[128]{0:T(128)S(1)} %slice_bitcast_fusion, ...), channel_id=1, replica_groups=mesh['dp'=4,'exp'=2,'col'=4] {'dp','exp','col'}, use_global_device_ids=true, to_apply=%region_20.21 | all-reduce | flops 4352 | bytes 34816 | tf_op jit(solution)/shard_map/psum | solution.py:458
  (385 shorter events, 492.7 us)
Async XLA Ops:
  7.2 112.2 %all-gather.4.cloned.1.call-start = ((), (), s32[]{:S(2)}) async-start(), calls=%async_computation.20 | async-start | bytes 7864320 | tf_op jit(solution)/shard_map/all_gather | solution.py:316
  10.9 148.5 %all-gather.6.cloned.1.call-start = ((), (), s32[]{:S(2)}) async-start(), calls=%async_computation.21 | async-start | bytes 6291456 | tf_op jit(solution)/shard_map/all_gather | solution.py:317
  14.0 150.0 %collective-permute-start.12 = (bf16[256,2048]{1,0:T(8,128)(2,1)}, bf16[256,2048]{1,0:T(8,128)(2,1)}, u32[]{:S(2)}, u32[]{:S(2)}) collective-permute-start(bf16[256,2048]{1,0:T(8,128)(2,1)} %param.19), channel_id=1, source_target_pairs={{0,1},{1,2},{2,3},{3,0},{4,5},{5,6},{6,7},{7,4},{8,9},{9,10},{10,1... | collective-permute-start | bytes 3145736 | tf_op jit(solution)/shard_map/ppermute | solution.py:293
  40.4 52.0 %collective-permute-start.1 = (bf16[256,2048]{1,0:T(8,128)(2,1)}, bf16[256,2048]{1,0:T(8,128)(2,1)}, u32[]{:S(2)}, u32[]{:S(2)}) collective-permute-start(bf16[256,2048]{1,0:T(8,128)(2,1)} %collective-permute-done), channel_id=1, source_target_pairs={{0,1},{1,2},{2,3},{3,0},{4,5},{5,6},{6,7},{7,4},{8,9},{9,10},{10,1... | collective-permute-start | bytes 3145736 | tf_op jit(solution)/shard_map/ppermute | solution.py:293
  98.3 69.3 %all-to-all-start.15 = ((bf16[8,80,2048]{2,1,0:T(8,128)(2,1)}), bf16[8,80,2048]{2,1,0:T(8,128)(2,1)}, u32[]{:S(2)}, u32[]{:S(2)}) async-start(bf16[8,80,2048]{2,1,0:T(8,128)(2,1)} %bitcast.235), calls=%async_computation.15 | async-start | bytes 5242880 | tf_op jit(solution)/shard_map/all_to_all | solution.py:308
  167.6 77.7 %all-to-all-start.9 = ((bf16[8,80,2048]{2,1,0:T(8,128)(2,1)}), bf16[8,80,2048]{2,1,0:T(8,128)(2,1)}, u32[]{:S(2)}, u32[]{:S(2)}) async-start(bf16[8,80,2048]{2,1,0:T(8,128)(2,1)} %bitcast.236), calls=%async_computation.9 | async-start | bytes 5242880 | tf_op jit(solution)/shard_map/all_to_all | solution.py:308
  191.7 50.4 %collective-permute-start.14 = (bf16[256,2048]{1,0:T(8,128)(2,1)}, bf16[256,2048]{1,0:T(8,128)(2,1)S(1)}, u32[]{:S(2)}, u32[]{:S(2)}) collective-permute-start(bf16[256,2048]{1,0:T(8,128)(2,1)} %collective-permute-done.12), channel_id=1, source_target_pairs={{0,1},{1,2},{2,3},{3,0},{4,5},{5,6},{6,7},{7,4},{8,9},{9,10},{10,1... | collective-permute-start | bytes 3145736 | tf_op jit(solution)/shard_map/ppermute | solution.py:293
  220.8 38.3 %collective-permute-start.5 = (bf16[256,2048]{1,0:T(8,128)(2,1)}, bf16[256,2048]{1,0:T(8,128)(2,1)}, u32[]{:S(2)}, u32[]{:S(2)}) collective-permute-start(bf16[256,2048]{1,0:T(8,128)(2,1)} %add_convert_fusion.9), channel_id=1, source_target_pairs={{0,1},{1,2},{2,3},{3,0},{4,5},{5,6},{6,7},{7,4},{8,9},{9,10},{10,1... | collective-permute-start | bytes 3145736 | tf_op jit(solution)/shard_map/ppermute | solution.py:293
  318.7 58.0 %all-to-all-start = ((bf16[8,80,2048]{2,1,0:T(8,128)(2,1)}), bf16[8,80,2048]{2,1,0:T(8,128)(2,1)}, u32[]{:S(2)}, u32[]{:S(2)}) async-start(bf16[8,80,2048]{2,1,0:T(8,128)(2,1)} %bitcast.234), calls=%async_computation | async-start | bytes 5242880 | tf_op jit(solution)/shard_map/all_to_all | solution.py:308
  323.2 49.9 %collective-permute-start.8 = (bf16[256,2048]{1,0:T(8,128)(2,1)}, bf16[256,2048]{1,0:T(8,128)(2,1)}, u32[]{:S(2)}, u32[]{:S(2)}) collective-permute-start(bf16[256,2048]{1,0:T(8,128)(2,1)} %copy-done.38), channel_id=1, source_target_pairs={{0,1},{1,2},{2,3},{3,0},{4,5},{5,6},{6,7},{7,4},{8,9},{9,10},{10,1... | collective-permute-start | bytes 3145736 | tf_op jit(solution)/shard_map/ppermute | solution.py:293
  602.0 42.4 %all-to-all-start.14 = ((bf16[8,80,2048]{2,1,0:T(8,128)(2,1)}), bf16[8,80,2048]{2,1,0:T(8,128)(2,1)}, u32[]{:S(2)}, u32[]{:S(2)}) async-start(bf16[8,80,2048]{2,1,0:T(8,128)(2,1)} %bitcast.243), calls=%async_computation.14 | async-start | bytes 5242880 | tf_op jit(solution)/shard_map/all_to_all | solution.py:308
  648.9 447.7 %reduce-scatter.5.cloned.1.call-start = ((), (), s32[]{:S(2)}) async-start(), calls=%async_computation.23 | async-start | bytes 4718592 | tf_op jit(solution)/shard_map/reduce_scatter | solution.py:455
  778.2 320.6 %reduce-scatter.3.cloned.1.call-start = ((), (), s32[]{:S(2)}) async-start(), calls=%async_computation.22 | async-start | bytes 5898240 | tf_op jit(solution)/shard_map/reduce_scatter | solution.py:452
  840.8 50.7 %all-to-all-start.2 = ((bf16[8,80,2048]{2,1,0:T(8,128)(2,1)}), bf16[8,80,2048]{2,1,0:T(8,128)(2,1)}, u32[]{:S(2)}, u32[]{:S(2)}) async-start(bf16[8,80,2048]{2,1,0:T(8,128)(2,1)} %bitcast.248), calls=%async_computation.2 | async-start | bytes 5242880 | tf_op jit(solution)/shard_map/all_to_all | solution.py:308
  845.3 257.4 %all-reduce.3.cloned.1.call-start = ((), (), s32[]{:S(2)}) async-start(), calls=%async_computation.24 | async-start | bytes 524288 | tf_op jit(solution)/shard_map/psum | solution.py:458
  891.6 41.4 %all-to-all-start.4 = ((bf16[8,80,2048]{2,1,0:T(8,128)(2,1)}), bf16[8,80,2048]{2,1,0:T(8,128)(2,1)}, u32[]{:S(2)}, u32[]{:S(2)}) async-start(bf16[8,80,2048]{2,1,0:T(8,128)(2,1)} %bitcast.244), calls=%async_computation.4 | async-start | bytes 5242880 | tf_op jit(solution)/shard_map/all_to_all | solution.py:308
  918.2 37.6 %collective-permute-start.7 = (bf16[256,2048]{1,0:T(8,128)(2,1)}, bf16[256,2048]{1,0:T(8,128)(2,1)}, u32[]{:S(2)}, u32[]{:S(2)}) collective-permute-start(bf16[256,2048]{1,0:T(8,128)(2,1)} %fusion.89), channel_id=1, source_target_pairs={{0,1},{1,2},{2,3},{3,0},{4,5},{5,6},{6,7},{7,4},{8,9},{9,10},{10,1... | collective-permute-start | bytes 3145736 | tf_op jit(solution)/shard_map/ppermute | solution.py:293
  930.7 39.6 %collective-permute-start.21 = (bf16[256,2048]{1,0:T(8,128)(2,1)}, bf16[256,2048]{1,0:T(8,128)(2,1)}, u32[]{:S(2)}, u32[]{:S(2)}) collective-permute-start(bf16[256,2048]{1,0:T(8,128)(2,1)} %slice.92), channel_id=1, source_target_pairs={{0,1},{1,2},{2,3},{3,0},{4,5},{5,6},{6,7},{7,4},{8,9},{9,10},{10,1... | collective-permute-start | bytes 3145736 | tf_op jit(solution)/shard_map/ppermute | solution.py:293
  933.0 40.5 %all-to-all-start.6 = ((bf16[8,80,2048]{2,1,0:T(8,128)(2,1)}), bf16[8,80,2048]{2,1,0:T(8,128)(2,1)}, u32[]{:S(2)}, u32[]{:S(2)}) async-start(bf16[8,80,2048]{2,1,0:T(8,128)(2,1)} %bitcast.242), calls=%async_computation.6 | async-start | bytes 5242880 | tf_op jit(solution)/shard_map/all_to_all | solution.py:308
  959.9 58.2 %collective-permute-start.9 = (bf16[256,2048]{1,0:T(8,128)(2,1)}, bf16[256,2048]{1,0:T(8,128)(2,1)}, u32[]{:S(2)}, u32[]{:S(2)}) collective-permute-start(bf16[256,2048]{1,0:T(8,128)(2,1)} %add_convert_fusion.8), channel_id=1, source_target_pairs={{0,1},{1,2},{2,3},{3,0},{4,5},{5,6},{6,7},{7,4},{8,9},{9,10},{10,1... | collective-permute-start | bytes 3145736 | tf_op jit(solution)/shard_map/ppermute | solution.py:293
  973.4 41.5 %collective-permute-start.22 = (bf16[256,2048]{1,0:T(8,128)(2,1)}, bf16[256,2048]{1,0:T(8,128)(2,1)}, u32[]{:S(2)}, u32[]{:S(2)}) collective-permute-start(bf16[256,2048]{1,0:T(8,128)(2,1)} %fusion.97), channel_id=1, source_target_pairs={{0,1},{1,2},{2,3},{3,0},{4,5},{5,6},{6,7},{7,4},{8,9},{9,10},{10,1... | collective-permute-start | bytes 3145736 | tf_op jit(solution)/shard_map/ppermute | solution.py:293
  973.4 47.2 %all-to-all-start.8 = ((bf16[8,80,2048]{2,1,0:T(8,128)(2,1)}), bf16[8,80,2048]{2,1,0:T(8,128)(2,1)}, u32[]{:S(2)}, u32[]{:S(2)}) async-start(bf16[8,80,2048]{2,1,0:T(8,128)(2,1)} %bitcast.241), calls=%async_computation.8 | async-start | bytes 5242880 | tf_op jit(solution)/shard_map/all_to_all | solution.py:308
  1018.1 69.9 %collective-permute-start.23 = (bf16[256,2048]{1,0:T(8,128)(2,1)}, bf16[256,2048]{1,0:T(8,128)(2,1)}, u32[]{:S(2)}, u32[]{:S(2)}) collective-permute-start(bf16[256,2048]{1,0:T(8,128)(2,1)} %fusion.96), channel_id=1, source_target_pairs={{0,1},{1,2},{2,3},{3,0},{4,5},{5,6},{6,7},{7,4},{8,9},{9,10},{10,1... | collective-permute-start | bytes 3145736 | tf_op jit(solution)/shard_map/ppermute | solution.py:293
  1020.6 70.3 %collective-permute-start.11 = (bf16[256,2048]{1,0:T(8,128)(2,1)}, bf16[256,2048]{1,0:T(8,128)(2,1)}, u32[]{:S(2)}, u32[]{:S(2)}) collective-permute-start(bf16[256,2048]{1,0:T(8,128)(2,1)} %add_convert_fusion.7), channel_id=1, source_target_pairs={{0,1},{1,2},{2,3},{3,0},{4,5},{5,6},{6,7},{7,4},{8,9},{9,10},{10,1... | collective-permute-start | bytes 3145736 | tf_op jit(solution)/shard_map/ppermute | solution.py:293
  (114 other events, 2636.5 us)
Sparse Core Ops, SparseCore 0:
  11.0 17.9 all-gather.3
  30.5 14.8 all-gather.5
  778.3 48.5 reduce-scatter.4
  836.1 73.3 reduce-scatter.2
  915.4 187.2 all-reduce.2

commit v2 on v1

v2 whole, which is shorter than its diff:
```python
import functools

import jax
import jax.numpy as jnp
from jax import lax
from jax.experimental import pallas as pl
from jax.experimental.pallas import tpu as pltpu
from jax.sharding import PartitionSpec as P

epsilon = 1e-06
rotary_base = 1000000.0
plane = ("dp", "exp")
everyone = ("dp", "exp", "col")
f32 = jnp.float32
bf16 = jnp.bfloat16


def dot_nn(a, b):
    return lax.dot_general(a, b, (((1,), (0,)), ((), ())), preferred_element_type=f32)


def dot_nt(a, b):
    return lax.dot_general(a, b, (((1,), (1,)), ((), ())), preferred_element_type=f32)


def dot_tn(a, b):
    return lax.dot_general(a, b, (((0,), (0,)), ((), ())), preferred_element_type=f32)


def inverse_rms(rows):
    return lax.rsqrt(jnp.mean(rows * rows, axis=-1, keepdims=True) + epsilon)


def rotary_tables(positions, head_size):
    halves = head_size // 2
    frequency = rotary_base ** (-2.0 * jnp.arange(halves, dtype=f32) / head_size)
    angles = positions.astype(f32)[:, None] * frequency[None, :]
    cosine, sine = jnp.cos(angles), jnp.sin(angles)
    return (
        jnp.concatenate([cosine, cosine], axis=1),
        jnp.concatenate([-sine, sine], axis=1),
    )


def turn(rows, cosine, sine):
    return rows * cosine + pltpu.roll(rows, rows.shape[-1] // 2, 1) * sine


def turn_back(rows, cosine, sine):
    return rows * cosine - pltpu.roll(rows, rows.shape[-1] // 2, 1) * sine


def place_of(col_ref, blocks, tokens, step):
    return pl.multiple_of(lax.rem(col_ref[0] - step + blocks, blocks) * tokens, tokens)


def in_order(col_ref, refs, held):
    tokens = refs[0].shape[0]
    for step, ref in enumerate(refs):
        held[pl.ds(place_of(col_ref, len(refs), tokens, step), tokens), :] = ref[...].astype(held.dtype)


def out_of_order(col_ref, held, refs):
    tokens = refs[0].shape[0]
    for step, ref in enumerate(refs):
        ref[...] = held[pl.ds(place_of(col_ref, len(refs), tokens, step), tokens), :].astype(ref.dtype)


def softmax_rows(query, keys_ref, first, tokens, scale):
    diagonal = dot_nt(query, keys_ref[pl.ds(first, tokens), :])
    row = lax.broadcasted_iota(jnp.int32, diagonal.shape, 0)
    column = lax.broadcasted_iota(jnp.int32, diagonal.shape, 1)
    diagonal = jnp.where(row >= column, diagonal * scale, -1e30)
    peak = jnp.max(diagonal, axis=1, keepdims=True)
    if first:
        former = dot_nt(query, keys_ref[pl.ds(0, first), :]) * scale
        peak = jnp.maximum(peak, jnp.max(former, axis=1, keepdims=True))
        former = jnp.exp(former - peak)
        diagonal = jnp.exp(diagonal - peak)
        inverse = 1.0 / (
            jnp.sum(former, axis=1, keepdims=True) + jnp.sum(diagonal, axis=1, keepdims=True)
        )
        return former * inverse, diagonal * inverse
    diagonal = jnp.exp(diagonal - peak)
    return None, diagonal / jnp.sum(diagonal, axis=1, keepdims=True)


def prepare_keys(col_ref, k_refs, v_refs, cos_ref, sin_ref, kg_ref, raw_rows, keys, values):
    in_order(col_ref, k_refs, raw_rows)
    in_order(col_ref, v_refs, values)
    tokens = k_refs[0].shape[0]
    for block in range(len(k_refs)):
        there = pl.ds(block * tokens, tokens)
        raw = raw_rows[there, :]
        rows = raw * inverse_rms(raw) * kg_ref[...]
        keys[there, :] = turn(rows, cos_ref[there, :], sin_ref[there, :]).astype(bf16)


def forward_kernel(blocks, scale, col_ref, *refs):
    q_refs, k_refs, v_refs = refs[:blocks], refs[blocks : 2 * blocks], refs[2 * blocks : 3 * blocks]
    cos_ref, sin_ref, qg_ref, kg_ref = refs[3 * blocks : 3 * blocks + 4]
    out_refs = refs[3 * blocks + 4 : 4 * blocks + 4]
    raw_rows, keys, values, mixed_rows = refs[4 * blocks + 4 :]
    tokens = q_refs[0].shape[0]

    @pl.when(pl.program_id(0) == 0)
    def _():
        prepare_keys(col_ref, k_refs, v_refs, cos_ref, sin_ref, kg_ref, raw_rows, keys, values)

    in_order(col_ref, q_refs, raw_rows)
    for block in range(blocks):
        first = block * tokens
        there = pl.ds(first, tokens)
        raw = raw_rows[there, :]
        rows = raw * inverse_rms(raw) * qg_ref[...]
        query = turn(rows, cos_ref[there, :], sin_ref[there, :]).astype(bf16)
        former, diagonal = softmax_rows(query, keys, first, tokens, scale)
        mixed = dot_nn(diagonal.astype(bf16), values[there, :])
        if first:
            mixed = mixed + dot_nn(former.astype(bf16), values[pl.ds(0, first), :])
        mixed_rows[there, :] = mixed.astype(bf16)
    out_of_order(col_ref, mixed_rows, out_refs)


def attention_forward(col, qkv, cosine, sine, query_gain, key_gain, heads):
    blocks, tokens, head_size = len(qkv), qkv[0].shape[0], query_gain.shape[-1]
    seq_len = blocks * tokens
    column = lambda index: [pl.BlockSpec((tokens, head_size), index)] * blocks
    whole = pl.BlockSpec((seq_len, head_size), lambda h, c: (0, 0))
    gain = pl.BlockSpec((1, head_size), lambda h, c: (0, 0))
    return pl.pallas_call(
        functools.partial(forward_kernel, blocks, head_size ** (-0.5)),
        out_shape=[jax.ShapeDtypeStruct((tokens, heads * head_size), bf16)] * blocks,
        grid_spec=pltpu.PrefetchScalarGridSpec(
            num_scalar_prefetch=1,
            grid=(heads,),
            in_specs=[
                *column(lambda h, c: (0, h)),
                *column(lambda h, c: (0, heads)),
                *column(lambda h, c: (0, heads + 1)),
                whole,
                whole,
                gain,
                gain,
            ],
            out_specs=column(lambda h, c: (0, h)),
            scratch_shapes=[
                pltpu.VMEM((seq_len, head_size), f32),
                pltpu.VMEM((seq_len, head_size), bf16),
                pltpu.VMEM((seq_len, head_size), bf16),
                pltpu.VMEM((seq_len, head_size), bf16),
            ],
        ),
        compiler_params=pltpu.CompilerParams(vmem_limit_bytes=60 * 2**20),
        cost_estimate=pl.CostEstimate(flops=1000, bytes_accessed=1000, transcendentals=0),
        name="attention_forward",
    )(col, *qkv, *qkv, *qkv, cosine, sine, query_gain, key_gain)


def backward_kernel(blocks, scale, first_head, heads, final, col_ref, *refs):
    q_refs, k_refs, v_refs, g_refs = (refs[i * blocks : (i + 1) * blocks] for i in range(4))
    cos_ref, sin_ref, qg_ref, kg_ref = refs[4 * blocks : 4 * blocks + 4]
    refs = refs[4 * blocks + 4 :]
    if first_head:
        refs = refs[blocks:]
        held_refs, refs = refs[:4], refs[4:]
    grad_refs, refs = refs[:blocks], refs[blocks:]
    qgain_ref, kgain_ref, out_keys, out_values = refs[:4]
    raw_rows, mixed_rows, keys, values, grad_rows, grad_keys, grad_values = refs[4:]
    tokens = q_refs[0].shape[0]
    step = pl.program_id(0)

    @pl.when(step == 0)
    def _():
        prepare_keys(col_ref, k_refs, v_refs, cos_ref, sin_ref, kg_ref, raw_rows, keys, values)
        if first_head:
            qgain_ref[...] = held_refs[0][...]
            kgain_ref[...] = held_refs[1][...]
            grad_keys[...] = held_refs[2][...]
            grad_values[...] = held_refs[3][...]
        else:
            grad_keys[...] = jnp.zeros_like(grad_keys)
            grad_values[...] = jnp.zeros_like(grad_values)
            qgain_ref[...] = jnp.zeros_like(qgain_ref)
            kgain_ref[...] = jnp.zeros_like(kgain_ref)

    def through_norm(grad_rot, unit, inverse, there, gain_ref, gain_grad_ref):
        grad_scaled = turn_back(grad_rot, cos_ref[there, :], sin_ref[there, :])
        gain_grad_ref[0:1, :] += jnp.sum(grad_scaled * unit, axis=0, keepdims=True)
        grad_unit = grad_scaled * gain_ref[...]
        return inverse * (grad_unit - unit * jnp.mean(grad_unit * unit, axis=1, keepdims=True))

    @pl.when(step < heads)
    def _():
        in_order(col_ref, q_refs, raw_rows)
        in_order(col_ref, g_refs, mixed_rows)
        for block in range(blocks):
            first = block * tokens
            there = pl.ds(first, tokens)
            raw = raw_rows[there, :]
            inverse = inverse_rms(raw)
            unit = raw * inverse
            query = turn(unit * qg_ref[...], cos_ref[there, :], sin_ref[there, :]).astype(bf16)
            grad_mixed = mixed_rows[there, :]
            former, diagonal = softmax_rows(query, keys, first, tokens, scale)
            grad_diagonal = dot_nt(grad_mixed, values[there, :])
            inner = jnp.sum(diagonal * grad_diagonal, axis=1, keepdims=True)
            if first:
                before = pl.ds(0, first)
                grad_former = dot_nt(grad_mixed, values[before, :])
                inner = inner + jnp.sum(former * grad_former, axis=1, keepdims=True)
                score_former = (former * (grad_former - inner)).astype(bf16)
                grad_keys[before, :] += dot_tn(score_former, query)
                grad_values[before, :] += dot_tn(former.astype(bf16), grad_mixed)
            score_diagonal = (diagonal * (grad_diagonal - inner)).astype(bf16)
            grad_keys[there, :] += dot_tn(score_diagonal, query)
            grad_values[there, :] += dot_tn(diagonal.astype(bf16), grad_mixed)
            grad_query = dot_nn(score_diagonal, keys[there, :])
            if first:
                grad_query = grad_query + dot_nn(score_former, keys[before, :])
            grad_rows[there, :] = through_norm(
                grad_query * scale, unit, inverse, there, qg_ref, qgain_ref
            ).astype(bf16)

    if not final:

        @pl.when(step == heads - 1)
        def _():
            out_keys[...] = grad_keys[...]
            out_values[...] = grad_values[...]

    @pl.when(step == heads)
    def _():
        in_order(col_ref, k_refs, raw_rows)
        for block in range(blocks):
            there = pl.ds(block * tokens, tokens)
            raw = raw_rows[there, :]
            inverse = inverse_rms(raw)
            grad_rows[there, :] = through_norm(
                grad_keys[there, :] * scale, raw * inverse, inverse, there, kg_ref, kgain_ref
            ).astype(bf16)

    @pl.when(step == heads + 1)
    def _():
        grad_rows[...] = grad_values[...].astype(bf16)

    out_of_order(col_ref, grad_rows, grad_refs)


def attention_backward(
    col, qkv, grad_attended, cosine, sine, query_gain, key_gain, all_heads, first, heads, former=None
):
    blocks, tokens, head_size = len(qkv), qkv[0].shape[0], query_gain.shape[-1]
    seq_len = blocks * tokens
    final = first + heads == all_heads
    column = lambda index: [pl.BlockSpec((tokens, head_size), index)] * blocks
    whole = pl.BlockSpec((seq_len, head_size), lambda h, c: (0, 0))
    gain = pl.BlockSpec((1, head_size), lambda h, c: (0, 0))
    gain_out = pl.BlockSpec((8, head_size), lambda h, c: (0, 0))
    last = all_heads - 1
    held = [] if former is None else former
    return pl.pallas_call(
        functools.partial(backward_kernel, blocks, head_size ** (-0.5), first, heads, final),
        out_shape=[
            *[jax.ShapeDtypeStruct(qkv[0].shape, bf16)] * blocks,
            jax.ShapeDtypeStruct((8, head_size), f32),
            jax.ShapeDtypeStruct((8, head_size), f32),
            jax.ShapeDtypeStruct((seq_len, head_size), f32),
            jax.ShapeDtypeStruct((seq_len, head_size), f32),
        ],
        grid_spec=pltpu.PrefetchScalarGridSpec(
            num_scalar_prefetch=1,
            grid=(heads + 2 if final else heads,),
            in_specs=[
                *column(lambda h, c: (0, jnp.minimum(h + first, last))),
                *column(lambda h, c: (0, all_heads)),
                *column(lambda h, c: (0, all_heads + 1)),
                *column(lambda h, c: (0, jnp.minimum(h + first, last))),
                whole,
                whole,
                gain,
                gain,
                *([] if former is None else [pl.BlockSpec(memory_space=pl.ANY)] * blocks),
                *([] if former is None else [gain_out, gain_out, whole, whole]),
            ],
            out_specs=[*column(lambda h, c: (0, h + first)), gain_out, gain_out, whole, whole],
            scratch_shapes=[
                pltpu.VMEM((seq_len, head_size), f32),
                pltpu.VMEM((seq_len, head_size), bf16),
                pltpu.VMEM((seq_len, head_size), bf16),
                pltpu.VMEM((seq_len, head_size), bf16),
                pltpu.VMEM((seq_len, head_size), bf16),
                pltpu.VMEM((seq_len, head_size), f32),
                pltpu.VMEM((seq_len, head_size), f32),
            ],
        ),
        input_output_aliases={} if former is None else {1 + 4 * blocks + 4 + i: i for i in range(blocks)},
        compiler_params=pltpu.CompilerParams(vmem_limit_bytes=60 * 2**20),
        cost_estimate=pl.CostEstimate(flops=1000, bytes_accessed=1000, transcendentals=0),
        name="attention_backward",
    )(col, *qkv, *qkv, *qkv, *grad_attended, cosine, sine, query_gain, key_gain, *held)


def weight_kernel(blocks, rights, weighted, *refs):
    left_refs, refs = refs[:blocks], refs[blocks:]
    right_refs, refs = refs[: blocks * rights], refs[blocks * rights :]
    if weighted:
        weight_refs, refs = refs[:blocks], refs[blocks:]
        out_refs, held = refs[:rights], refs[rights:]

        @pl.when(pl.program_id(0) == 0)
        def _():
            for index, ref in enumerate(right_refs):
                scaled = ref[...].astype(f32) * weight_refs[index % blocks][...]
                held[index][...] = scaled.astype(bf16)

        right_refs = held
    else:
        out_refs = refs
    for index, out_ref in enumerate(out_refs):
        total = dot_tn(left_refs[0][...], right_refs[index * blocks][...])
        for block in range(1, blocks):
            total = total + dot_tn(left_refs[block][...], right_refs[index * blocks + block][...])
        out_ref[...] = total.astype(out_ref.dtype)


def weight_gradients(lefts, rights, out_type, weights=None, tile=256, order=None):
    order = order or (lambda i: i)
    blocks, rows, tall = len(lefts), lefts[0].shape[0], lefts[0].shape[1]
    flat = [block for right in rights for block in right]
    fixed = lambda array: pl.BlockSpec(array.shape, lambda i: (0, 0))
    return pl.pallas_call(
        functools.partial(weight_kernel, blocks, len(rights), weights is not None),
        out_shape=[jax.ShapeDtypeStruct((tall, right[0].shape[1]), out_type) for right in rights],
        grid=(tall // tile,),
        in_specs=[
            *[pl.BlockSpec((rows, tile), lambda i: (0, i))] * blocks,
            *[fixed(block) for block in flat],
            *([] if weights is None else [fixed(weight) for weight in weights]),
        ],
        out_specs=[
            pl.BlockSpec((tile, right[0].shape[1]), lambda i: (order(i), 0)) for right in rights
        ],
        scratch_shapes=[] if weights is None else [pltpu.VMEM(block.shape, bf16) for block in flat],
        compiler_params=pltpu.CompilerParams(vmem_limit_bytes=60 * 2**20),
        cost_estimate=pl.CostEstimate(flops=1000, bytes_accessed=1000, transcendentals=0),
        name="weight_gradients",
    )(*lefts, *flat, *([] if weights is None else weights))


def spread_kernel(with_units, *refs):
    block_refs, weight_ref, refs = refs[:4], refs[4], refs[5:]
    if with_units:
        unit_refs, refs = refs[:4], refs[4:]
    up_ref, down_ref, up_rest, down_rest, own_ref = refs[:5]
    weight = weight_ref[...]
    middle = own_ref.shape[0] // 2
    shares = {}
    for step in (2, 3, 1, 0):
        shares[step] = dot_nt(block_refs[step][...], weight)
    up_ref[:middle, :] = shares[2][:middle].astype(bf16)
    up_ref[middle:, :] = shares[3][middle:].astype(bf16)
    down_ref[:middle, :] = shares[1][:middle].astype(bf16)
    down_ref[middle:, :] = shares[2][middle:].astype(bf16)
    up_rest[...] = shares[3][:middle]
    down_rest[...] = shares[1][middle:]
    own_ref[...] = shares[0]
    if with_units:
        total = sum(
            jnp.sum(shares[step] * unit_refs[step][...], axis=0, keepdims=True) for step in range(4)
        )
        refs[5][...] = jnp.broadcast_to(total, refs[5].shape)


def spread(blocks, weight, units=None, tile=512):
    tokens, depth = blocks[0].shape
    width = weight.shape[0]
    part = lambda rows: pl.BlockSpec((rows, tile), lambda i: (0, i))
    shape = jax.ShapeDtypeStruct
    return pl.pallas_call(
        functools.partial(spread_kernel, units is not None),
        out_shape=[
            shape((tokens, width), bf16),
            shape((tokens, width), bf16),
            shape((tokens // 2, width), f32),
            shape((tokens // 2, width), f32),
            shape((tokens, width), f32),
            *([] if units is None else [shape((8, width), f32)]),
        ],
        grid=(width // tile,),
        in_specs=[
            *[pl.BlockSpec((tokens, depth), lambda i: (0, 0))] * 4,
            pl.BlockSpec((tile, depth), lambda i: (i, 0)),
            *([] if units is None else [part(tokens)] * 4),
        ],
        out_specs=[
            part(tokens),
            part(tokens),
            part(tokens // 2),
            part(tokens // 2),
            part(tokens),
            *([] if units is None else [part(8)]),
        ],
        compiler_params=pltpu.CompilerParams(vmem_limit_bytes=60 * 2**20),
        cost_estimate=pl.CostEstimate(flops=1000, bytes_accessed=1000, transcendentals=0),
        name="spread",
    )(*blocks, weight, *([] if units is None else units))


def product_kernel(transposed, left_ref, right_ref, *refs):
    result = (dot_tn if transposed else dot_nn)(left_ref[...], right_ref[...])
    if len(refs) > 1:
        result = result + refs[0][...].astype(f32)
    refs[-1][...] = result.astype(refs[-1].dtype)


def product(left, right, addend=None, out_type=bf16, transposed=False, tile=512):
    rows = left.shape[1 if transposed else 0]
    part = lambda height: pl.BlockSpec((height, tile), lambda i: (0, i))
    return pl.pallas_call(
        functools.partial(product_kernel, transposed),
        out_shape=jax.ShapeDtypeStruct((rows, right.shape[1]), out_type),
        grid=(right.shape[1] // tile,),
        in_specs=[
            pl.BlockSpec(left.shape, lambda i: (0, 0)),
            part(right.shape[0]),
            *([] if addend is None else [part(rows)]),
        ],
        out_specs=part(rows),
        compiler_params=pltpu.CompilerParams(vmem_limit_bytes=60 * 2**20),
        cost_estimate=pl.CostEstimate(flops=1000, bytes_accessed=1000, transcendentals=0),
        name="product",
    )(left, right, *([] if addend is None else [addend]))


def expert_kernel(
    rows_ref, upstream_ref, gate_ref, up_ref, down_ref,
    acted_ref, gate_grad_ref, up_grad_ref, row_grad_ref, returned_ref, dots_ref,
    gates, ups, downs, gate_grads, up_grads, acted_rows,
):
    step = pl.program_id(0)
    tile = gate_ref.shape[1]
    gate_part = dot_nn(rows_ref[...], gate_ref[...])
    up_part = dot_nn(rows_ref[...], up_ref[...])
    drive = dot_nt(upstream_ref[...], down_ref[...])
    sigmoid = jax.nn.sigmoid(gate_part)
    silu = gate_part * sigmoid
    acted = silu * up_part
    acted_low = acted.astype(bf16)
    gate_grad = (drive * up_part * sigmoid * (1.0 + gate_part * (1.0 - sigmoid))).astype(bf16)
    up_grad = (drive * silu).astype(bf16)
    acted_ref[...] = acted_low
    gate_grad_ref[...] = gate_grad
    up_grad_ref[...] = up_grad
    dots = jnp.sum(acted * drive, axis=1, keepdims=True)
    for index in range(gates.shape[1] // tile):

        @pl.when(step == index)
        def _():
            here = pl.ds(index * tile, tile)
            gates[:, here] = gate_ref[...]
            ups[:, here] = up_ref[...]
            downs[here, :] = down_ref[...]
            gate_grads[:, here] = gate_grad
            up_grads[:, here] = up_grad
            acted_rows[:, here] = acted_low

    @pl.when(step == 0)
    def _():
        dots_ref[...] = dots

    @pl.when(step > 0)
    def _():
        dots_ref[...] += dots

    @pl.when(step == pl.num_programs(0) - 1)
    def _():
        for first in range(0, row_grad_ref.shape[1], 512):
            here = pl.ds(first, 512)
            row_grad_ref[:, here] = (
                dot_nt(gate_grads[...], gates[here, :]) + dot_nt(up_grads[...], ups[here, :])
            ).astype(bf16)
            returned_ref[:, here] = dot_nn(acted_rows[...], downs[:, here]).astype(bf16)


def expert_block(rows, upstream_rows, gate_weight, up_weight, down_weight, tile=256):
    count, width = rows.shape
    hidden = gate_weight.shape[1]
    shape = jax.ShapeDtypeStruct
    whole = pl.BlockSpec((count, width), lambda j: (0, 0))
    part = pl.BlockSpec((count, tile), lambda j: (0, j))
    return pl.pallas_call(
        expert_kernel,
        out_shape=[
            shape((count, hidden), bf16),
            shape((count, hidden), bf16),
            shape((count, hidden), bf16),
            shape((count, width), bf16),
            shape((count, width), bf16),
            shape((count, 1), f32),
        ],
        grid=(hidden // tile,),
        in_specs=[
            whole,
            whole,
            pl.BlockSpec((width, tile), lambda j: (0, j)),
            pl.BlockSpec((width, tile), lambda j: (0, j)),
            pl.BlockSpec((tile, width), lambda j: (j, 0)),
        ],
        out_specs=[part, part, part, whole, whole, pl.BlockSpec((count, 1), lambda j: (0, 0))],
        scratch_shapes=[
            pltpu.VMEM((width, hidden), bf16),
            pltpu.VMEM((width, hidden), bf16),
            pltpu.VMEM((hidden, width), bf16),
            pltpu.VMEM((count, hidden), bf16),
            pltpu.VMEM((count, hidden), bf16),
            pltpu.VMEM((count, hidden), bf16),
        ],
        compiler_params=pltpu.CompilerParams(vmem_limit_bytes=60 * 2**20),
        cost_estimate=pl.CostEstimate(flops=1000, bytes_accessed=1000, transcendentals=0),
        name="expert_block",
    )(rows, upstream_rows, gate_weight, up_weight, down_weight)


def local(
    inputs,
    expert_ids,
    positions,
    cotangent,
    attn_gain,
    query_proj,
    key_projection,
    value_projection,
    query_norm_gain,
    key_norm_gain,
    out_proj,
    moe_gain,
    router,
    gate_proj,
    up_proj,
    down_proj,
):
    tokens, width = inputs.shape
    head_size = query_norm_gain.shape[0]
    choices = expert_ids.shape[1]
    experts = router.shape[1]
    capacity = tokens * choices * 5 // (4 * experts)
    columns = lax.axis_size("col")
    peers = lax.axis_size("dp") * lax.axis_size("exp")
    col = lax.axis_index("col")
    here = lax.axis_index("dp") * lax.axis_size("exp") + lax.axis_index("exp")
    col_array = jnp.reshape(col, (1,)).astype(jnp.int32)
    heads = query_proj.shape[1] // head_size
    assert key_projection.shape[1] == head_size and experts == peers * columns
    assert columns == 4 and tokens % 32 == 0
    middle = tokens // 2

    def shifted(block, by):
        return lax.ppermute(block, "col", [(i, (i + by) % columns) for i in range(columns)])

    def up(block):
        return shifted(block, 1)

    def down(block):
        return shifted(block, -1)

    def gather_near(block):
        return up(block), down(block)

    def gather_far(former, latter):
        return jnp.concatenate([up(former[:middle]), down(latter[middle:])], axis=0)

    def scatter_first(up_rows, down_rows, *_):
        return up(up_rows), down(down_rows)

    def scatter_second(first, up_rest, down_rest):
        return (
            up((up_rest + first[0][:middle].astype(f32)).astype(bf16)),
            down((down_rest + first[1][middle:].astype(f32)).astype(bf16)),
        )

    def scatter_own(own, first, second):
        return own + jnp.concatenate(
            [
                second[0].astype(f32) + first[1][:middle].astype(f32),
                first[0][middle:].astype(f32) + second[1].astype(f32),
            ],
            axis=0,
        )

    def swap(rows):
        return lax.all_to_all(
            rows.reshape(peers, rows.shape[0] // peers, *rows.shape[1:]), plane, 0, 0, tiled=True
        ).reshape(rows.shape)

    def swap_all(values):
        return lax.all_to_all(values, everyone, 0, 0, tiled=True)

    def after(value, *others):
        return lax.optimization_barrier((value, others))[0]

    def exchange_plane(values, steps):
        parts = {}
        for step in steps:
            part = lax.dynamic_index_in_dim(values, lax.rem(here + step, peers), 0, keepdims=False)
            pairs = [(i, (i + step) % peers) for i in range(peers)]
            parts[step] = lax.ppermute(part, plane, pairs) if step else part
        return parts

    def joined(parts):
        order = lax.rem(here - jnp.arange(peers, dtype=jnp.int32) + peers, peers)
        return jnp.take(jnp.stack([parts[step] for step in range(peers)]), order, axis=0)

    early_steps, late_steps = range(peers // 2), range(peers // 2, peers)

    def exchange_columns(values):
        parts = [values[:, 0], *[shifted(values[:, s], -s) for s in range(1, columns)]]
        return jnp.stack([parts[0], *parts[:0:-1]], axis=1)

    to_ring = lax.rem(col - jnp.arange(columns, dtype=jnp.int32) + columns, columns)

    earlier = (
        lax.broadcasted_iota(jnp.int32, (tokens, tokens), 0)
        < lax.broadcasted_iota(jnp.int32, (tokens, tokens), 1)
    ).astype(bf16)
    all_experts = jnp.arange(experts, dtype=jnp.int32)
    plane_experts = jnp.arange(peers, dtype=jnp.int32) * columns + col

    def chosen_in(ids, named):
        return jnp.any(ids[None, :, :] == named[:, None, None], axis=1)

    def slots_of(ids, named):
        chosen = chosen_in(ids, named)
        rank = dot_nn(chosen.astype(bf16), earlier)
        code = jnp.where(chosen, rank, -1.0)
        place = lax.broadcasted_iota(jnp.int32, (1, capacity, 1), 1).astype(f32)
        return chosen, code[:, None, :] == place

    def slot_mat(ids):
        return slots_of(ids, plane_experts)[1].astype(bf16).reshape(peers * capacity, tokens)

    def pick(step, block):
        return product(slot_mats[step], block)

    def gates_of(chosen, block):
        logits = jnp.where(chosen, dot_general_t(router, block), -1e30)
        exponent = jnp.exp(logits - jnp.max(logits, axis=0, keepdims=True))
        exponent = jnp.where(chosen, exponent, 0.0)
        return exponent / jnp.sum(exponent, axis=0, keepdims=True)

    def weighted_mat(step, block_gates):
        gates_here = block_gates.reshape(peers, columns, 1, tokens)
        gates_here = lax.dynamic_index_in_dim(gates_here, col, 1, keepdims=False)
        mat = slot_mats[step].reshape(peers, capacity, tokens) * gates_here
        return mat.astype(bf16).reshape(peers * capacity, tokens)

    def collect(back, step, addend=None, out_type=bf16):
        return product(weighted_mats[step], back[step], addend, out_type, transposed=True)

    near_inputs = gather_near(inputs)
    local_qkv = jnp.concatenate([query_proj, key_projection, value_projection], axis=1)
    full_qkv = lax.all_gather(local_qkv, "exp", axis=0, tiled=True)
    full_out = lax.all_gather(out_proj, "exp", axis=0, tiled=True)
    own_ids = expert_ids.T
    slot_mats = [slot_mat(own_ids)]
    cotangent_rows = [swap(pick(0, cotangent)), None, None, None]
    near_inputs, full_qkv = after((near_inputs, full_qkv))

    far_inputs = gather_far(*near_inputs)
    def project(block):
        rows = block.astype(f32)
        unit = rows * inverse_rms(rows)
        low = (unit * attn_gain).astype(bf16)
        return unit, low, dot_nn(low, full_qkv)

    projected = [project(inputs), project(near_inputs[0]), None, project(near_inputs[1])]
    cosine, sine = rotary_tables(positions, head_size)
    far_inputs, cotangent_rows[0], cosine, sine = after(
        (far_inputs, cotangent_rows[0], cosine, sine),
        [projected[s][2] for s in (0, 1, 3)],
    )

    near_cotangent = gather_near(after(cotangent, far_inputs))
    later_ids = after(own_ids, far_inputs)
    ids_blocks = [own_ids, *[shifted(later_ids, step) for step in range(1, columns)]]
    projected[2] = project(far_inputs)
    units, normed, qkv = zip(*projected)
    query_gain, key_gain = query_norm_gain[None, :], key_norm_gain[None, :]
    attended = attention_forward(col_array, qkv, cosine, sine, query_gain, key_gain, heads)
    shares = spread(attended, full_out)
    slot_mats += [slot_mat(ids_blocks[s]) for s in (1, 2, 3)]
    near_cotangent, shares, slot_mats = after((near_cotangent, shares, slot_mats))

    up_rows, down_rows, up_rest, down_rest, own_share = shares
    first_up = up(up_rows)
    far_cotangent = gather_far(*near_cotangent)
    cotangent_rows[1] = swap(pick(1, near_cotangent[0]))
    chosen_all, slots_all = slots_of(own_ids, all_experts)
    picked = pick(3, near_cotangent[1])
    first_up, far_cotangent, cotangent_rows[1], chosen_all, slots_all, down_rows, picked = after(
        (first_up, far_cotangent, cotangent_rows[1], chosen_all, slots_all, down_rows, picked)
    )
    first_down = down(down_rows)
    second_up = up((up_rest + first_up[:middle].astype(f32)).astype(bf16))
    cotangent_rows[3] = swap(picked)
    picked = pick(2, far_cotangent)
    first_down, second_up, cotangent_rows[3], picked = after(
        (first_down, second_up, cotangent_rows[3], picked)
    )

    second_down = down((down_rest + first_down[middle:].astype(f32)).astype(bf16))
    cotangent_rows[2] = swap(picked)
    gate_weight, up_weight, down_weight = gate_proj[0], up_proj[0], down_proj[0]
    branch_first, branch_second = (first_up, first_down), (second_up, second_down)
    hidden = inputs.astype(f32) + scatter_own(own_share, branch_first, branch_second)
    inverse_hidden = inverse_rms(hidden)
    routed = (hidden * inverse_hidden * moe_gain).astype(bf16)
    own_rows = after(pick(0, routed), cotangent_rows[2])

    acted_rows, gate_grads, up_grads, row_grads, returned, gate_dots = [], [], [], [], [], []

    def run_expert(step, rows):
        results = expert_block(rows, cotangent_rows[step], gate_weight, up_weight, down_weight)
        for held, result in zip((acted_rows, gate_grads, up_grads, row_grads, returned), results):
            held.append(result)
        gate_dots.append(results[5].reshape(peers, capacity))

    def block_mat(step):
        block_gates = gates_of(chosen_in(ids_blocks[step], all_experts), routed_blocks[step])
        return weighted_mat(step, block_gates)

    routed_blocks, arrived, weighted_mats = [routed], [], {}
    rows, next_rows = own_rows, None
    slot_parts = {}
    for step in range(columns):
        rows = swap(rows)
        coming = None
        if step < columns - 1:
            coming = up(routed_blocks[step])
            next_rows = pick(step + 1, coming)
        if step:
            run_expert(step - 1, arrived[step - 1])
        if step == 0:
            gates = gates_of(chosen_all, routed)
            gate_slots = jnp.sum(jnp.where(slots_all, gates[:, None, :], 0.0), axis=2)
            gate_slots = jnp.take(gate_slots.reshape(peers, columns, capacity), to_ring, axis=1)
            weighted_mats[0] = weighted_mat(0, gates)
            slot_parts = exchange_plane(gate_slots, early_steps)
        elif step == 1:
            slot_parts.update(exchange_plane(gate_slots, late_steps))
        elif step == 2:
            gate_slots = exchange_columns(joined(slot_parts))
            slot_parts = {}
        state = (rows, next_rows, coming, gate_slots, weighted_mats, slot_parts)
        rows, next_rows, coming, gate_slots, weighted_mats, slot_parts = after(state, row_grads)
        arrived.append(rows)
        routed_blocks.append(coming)
        rows = next_rows
    row_weights = [gate_slots[:, step].reshape(peers * capacity, 1) for step in range(columns)]

    row_grads = after(row_grads, arrived[3])
    grad_back = {1: swap(row_grads[1])}
    run_expert(3, arrived[3])
    weighted_mats[1] = block_mat(1)
    grad_back[1], row_grads, gate_dots, weighted_mats = after(
        (grad_back[1], row_grads, gate_dots, weighted_mats)
    )
    grad_back[2] = swap(row_grads[2])
    running = up(collect(grad_back, 1))
    dots = jnp.stack(gate_dots, axis=1)
    dot_parts = exchange_plane(dots, early_steps)
    weighted_mats[2] = block_mat(2)
    running, grad_back[2], dot_parts, weighted_mats = after(
        (running, grad_back[2], dot_parts, weighted_mats)
    )
    grad_back[3] = swap(after(row_grads[3], running))
    running = up(collect(grad_back, 2, running))
    dot_parts.update(exchange_plane(after(dots, grad_back[2]), late_steps))
    weighted_mats[3] = block_mat(3)
    running, grad_back[3], dot_parts, weighted_mats = after(
        (running, grad_back[3], dot_parts, weighted_mats)
    )
    grad_back[0] = swap(after(row_grads[0], running))
    running = up(collect(grad_back, 3, running))
    dots = jnp.take(exchange_columns(joined(dot_parts)), to_ring, axis=1).reshape(experts, capacity)
    running, grad_back[0], dots = after((running, grad_back[0], dots))

    grad_gates = jnp.sum(jnp.where(slots_all, dots[:, :, None], 0.0), axis=1)
    grad_logits = (
        gates * (grad_gates - jnp.sum(gates * grad_gates, axis=0, keepdims=True))
    ).astype(bf16)
    grad_routed = collect(grad_back, 0, running, f32) + lax.dot_general(
        grad_logits, router, (((0,), (1,)), ((), ())), preferred_element_type=f32
    )
    scaled = grad_routed * moe_gain
    grad_hidden = (
        cotangent.astype(f32)
        + scaled * inverse_hidden
        - hidden * (jnp.mean(hidden * scaled, axis=-1, keepdims=True) * inverse_hidden**3)
    )
    grad_moe_gain = jnp.sum(grad_routed * hidden * inverse_hidden, axis=0)
    grad_router = dot_general_t(routed, grad_logits)

    grad_low = grad_hidden.astype(bf16)
    near_gradient = gather_near(grad_low)
    output_back = {1: swap(after(returned[1], grad_low))}
    grad_attended = {0: product(grad_low, full_out)}
    grad_gate_weight, grad_up_weight = weight_gradients(
        after(arrived, grad_low), [gate_grads, up_grads], f32, row_weights
    )
    near_gradient, output_back[1], grad_gate_weight, grad_attended = after(
        (near_gradient, output_back[1], grad_gate_weight, grad_attended)
    )

    far_gradient = gather_far(*near_gradient)
    output_back[2] = swap(after(returned[2], near_gradient))
    grad_attended.update({1: product(near_gradient[0], full_out), 3: product(near_gradient[1], full_out)})
    output_part = collect(output_back, 1)
    router_sums = grad_router.reshape(1, columns, width // columns * experts)
    router_sums = jnp.take(after(router_sums, near_gradient), to_ring, axis=1)
    router_sums = jnp.sum(exchange_columns(router_sums)[0], axis=0)
    far_gradient, output_back[2], grad_attended, output_part, router_sums = after(
        (far_gradient, output_back[2], grad_attended, output_part, router_sums)
    )

    grad_sequence = [grad_low, near_gradient[0], far_gradient, near_gradient[1]]
    running = up(output_part)
    output_back[3] = swap(after(returned[3], output_back[2]))
    grad_attended[2] = product(far_gradient, full_out)
    grad_attended = [grad_attended[s] for s in range(columns)]
    half = heads // 2
    arguments = (col_array, qkv, grad_attended, cosine, sine, query_gain, key_gain, heads)
    first_half = attention_backward(*arguments, 0, half)
    first_half, running = after((first_half, running))
    running = up(collect(output_back, 2, running))
    *grad_qkv, grad_query_gain, grad_key_gain, _, _ = attention_backward(
        *arguments, half, heads - half, first_half
    )
    grad_query_gain, grad_key_gain = grad_query_gain[0], grad_key_gain[0]

    *shares, attn_gain_sums = spread(grad_qkv, full_qkv, units)
    up_rows, down_rows, up_rest, down_rest, own_share = shares
    first_up, first_down = up(up_rows), down(down_rows)
    output_part = collect(after(output_back, attn_gain_sums), 3, running)
    output_back[0] = swap(after(returned[0], output_back[3], attn_gain_sums))
    (grad_down,) = weight_gradients(
        after(acted_rows, attn_gain_sums), [cotangent_rows], f32, row_weights
    )
    first_up, grad_down, output_part = after((first_up, grad_down, output_part))

    second_up = up((up_rest + first_up[:middle].astype(f32)).astype(bf16))
    running = up(output_part)
    dp, exp = lax.axis_size("dp"), lax.axis_size("exp")
    tile = min(256, width // (dp * exp))
    in_order = tile % 128 == 0
    order = (lambda i: i % exp * dp + i // exp) if in_order else None

    def weight_sums(lefts, right):
        (grads,) = weight_gradients(lefts, [right], bf16, tile=tile if in_order else 256, order=order)
        rows, wide = width // (dp * exp), grads.shape[1]
        if not in_order:
            grads = grads.reshape(dp, exp, rows, wide).transpose(1, 0, 2, 3)
        grads = grads.reshape(exp, dp * rows, wide)
        mine = lax.axis_index("exp")
        total = lax.dynamic_index_in_dim(grads, mine, 0, keepdims=False).astype(f32)
        for step in range(1, exp):
            part = lax.dynamic_index_in_dim(grads, lax.rem(mine + step, exp), 0, keepdims=False)
            part = lax.ppermute(part, "exp", [(i, (i + step) % exp) for i in range(exp)])
            total = total + part.astype(f32)
        return total.astype(bf16)

    out_sums = weight_sums(after(grad_sequence, first_up), attended)
    reduced_out = lax.psum_scatter(out_sums, "dp", scatter_dimension=0, tiled=True).astype(f32)
    qkv_sums = weight_sums(normed, after(grad_qkv, out_sums))

    small = jnp.concatenate([attn_gain_sums[0], grad_query_gain, grad_key_gain, grad_moe_gain])
    cuts = [0, width, width + head_size, width + 2 * head_size, 2 * (width + head_size)]
    small = jnp.concatenate([small, router_sums])
    small = swap(after(jnp.broadcast_to(small, (peers, small.shape[0])), output_back[0]))
    first_down, second_up, qkv_sums, small = after((first_down, second_up, qkv_sums, small))

    second_down = down((down_rest + first_down[middle:].astype(f32)).astype(bf16))
    qkv_parts = lax.all_to_all(
        qkv_sums.reshape(dp, -1, qkv_sums.shape[1]), "dp", 0, 0, tiled=True
    )
    reduced_qkv = jnp.sum(qkv_parts.astype(f32), axis=0)
    outputs = (hidden + collect(output_back, 0, running, f32)).astype(bf16)
    small = jnp.sum(small, axis=0)
    small = jnp.stack([small, *[shifted(small, step) for step in range(1, columns)]])
    to_true = lax.rem(col - jnp.arange(columns, dtype=jnp.int32) + columns, columns)
    grad_router = jnp.take(small[:, cuts[-1] :], to_true, axis=0).reshape(width, experts)
    small = jnp.sum(small[:, : cuts[-1]], axis=0)
    shared = [small[i:j] for i, j in zip(cuts, cuts[1:])]

    grad_normed = scatter_own(own_share, (first_up, first_down), (second_up, second_down))
    input_rows = inputs.astype(f32)
    inverse_own = inverse_rms(input_rows)
    scaled_in = grad_normed * attn_gain
    grad_inputs = (
        grad_hidden
        + scaled_in * inverse_own
        - input_rows * (jnp.mean(input_rows * scaled_in, axis=-1, keepdims=True) * inverse_own**3)
    ).astype(bf16)

    split = heads * head_size
    return (
        outputs,
        grad_inputs,
        shared[0],
        reduced_qkv[:, :split],
        reduced_qkv[:, split : split + head_size],
        reduced_qkv[:, split + head_size :],
        shared[1],
        shared[2],
        reduced_out,
        shared[3],
        grad_router,
        grad_gate_weight[None],
        grad_up_weight[None],
        grad_down[None],
    )


def dot_general_t(a, b):
    contract = (((0,), (1,)), ((), ()))
    return lax.dot_general(a, b, contract, preferred_element_type=f32)


def solution(mesh):
    return jax.shard_map(
        local,
        mesh=mesh,
        in_specs=(
            P(("dp", "exp", "col"), None),
            P(("dp", "exp", "col"), None),
            P(("dp", "exp")),
            P(("dp", "exp", "col"), None),
            P(),
            P("exp", "col"),
            P("exp", "col"),
            P("exp", "col"),
            P(),
            P(),
            P("exp", "col"),
            P(),
            P(),
            P(("dp", "exp", "col"), None, None),
            P(("dp", "exp", "col"), None, None),
            P(("dp", "exp", "col"), None, None),
        ),
        out_specs=(
            P(("dp", "exp", "col"), None),
            P(("dp", "exp", "col"), None),
            P(),
            P(("dp", "exp"), "col"),
            P(("dp", "exp"), "col"),
            P(("dp", "exp"), "col"),
            P(),
            P(),
            P(("dp", "exp"), "col"),
            P(),
            P(),
            P(("dp", "exp", "col"), None, None),
            P(("dp", "exp", "col"), None, None),
            P(("dp", "exp", "col"), None, None),
        ),
        check_vma=False,
    )
```

time: 1130 us -> 953 us (0.84)
  Pallas kernels: 63.6 us -> 332 us
  matrix products: 267 us -> 25.9 us
  waiting for transfers between devices: 472 us -> 290 us
  blocking collectives: 123 us -> 0 us
  starting transfers between devices: 84.3 us -> 166 us
  other arithmetic: 59.4 us -> 73.5 us
  local copies, waits for them, and re-layouts: 25.7 us -> 38.2 us
    pallas_call x2 -> x33, Pallas kernels: 63.6 us -> 332 us  [the longest x20 88.5 us: product(): pl.pallas_call(functools.partial(product_kernel, transposed), out_shape=j...]
    dot_general x30 -> x0, matrix products: 156 us -> none  [the longest x13 85.1 us: dot_tn(): lax.dot_general(a, b, (((0,), (0,)), ((), ())), preferred_element_type=f32)]
    all_to_all x16 -> x17, waiting for transfers between devices: 139 us -> 30.5 us  [swap(): lax.all_to_all(rows.reshape(peers, rows.shape[0] // peers, *rows.shape[1:...]
    dot_general x27 -> x9, matrix products: 106 us -> 14 us  [dot_nn(): lax.dot_general(a, b, (((1,), (0,)), ((), ())), preferred_element_type=f32)]
    ppermute x24 -> x60, waiting for transfers between devices: 326 us -> 244 us  [the longest x44 209 us: shifted(): lax.ppermute(block, 'col', [(i, (i + by) % columns) for i in range(column...]
    ppermute x24 -> x60, starting transfers between devices: 6.59 us -> 85.7 us  [the longest x44 64.9 us: shifted(): lax.ppermute(block, 'col', [(i, (i + by) % columns) for i in range(column...]
    psum x1 -> x0, blocking collectives: 63.1 us -> none  [local(): lax.psum((grad_attn_gain, grad_query_gain[0], grad_key_gain[0], grad_moe_...]
    all_gather x1 -> x0, blocking collectives: 51.2 us -> none  [local(): gathered_ids = lax.all_gather(expert_ids, 'col', axis=0)]
  transfers between devices with their start and end apart: 46 -> 81, of which waited for: 30 -> 31; matrix products, arithmetic and copies ran while one was open for 27% -> 12% of each run, Pallas kernels for 6% -> 33%
where the time goes in v2:
time: 953 us; the launch traced here: 941 us
  Pallas kernels  332 us (35%)
  waiting for transfers between devices  290 us (30%)
  starting transfers between devices  166 us (17%)
  other arithmetic  73.5 us (8%)
  local copies, waits for them, and re-layouts  38.2 us (4%)
  matrix products  25.9 us (3%)
  between operations  15.2 us (2%)
    ppermute x44, waiting for transfers between devices, shifted(): lax.ppermute(block, 'col', [(i, (i + by) % columns) for i in range(column...  209 us
    pallas_call x20, Pallas kernels, product(): pl.pallas_call(functools.partial(product_kernel, transposed), out_shape=j...  88.5 us
    pallas_call x4, Pallas kernels, expert_block(): pl.pallas_call(expert_kernel, out_shape=[shape((count, hidden), bf16), sh...  83.7 us
    all_to_all x17, starting transfers between devices, swap(): lax.all_to_all(rows.reshape(peers, rows.shape[0] // peers, *rows.shape[1:...  75.9 us
    pallas_call x4, Pallas kernels, weight_gradients(): pl.pallas_call(functools.partial(weight_kernel, blocks, len(rights), weig...  68.1 us
    ppermute x44, starting transfers between devices, shifted(): lax.ppermute(block, 'col', [(i, (i + by) % columns) for i in range(column...  64.9 us
    pallas_call x2, Pallas kernels, attention_backward(): pl.pallas_call(functools.partial(backward_kernel, blocks, head_size ** (-...  44.9 us
    ppermute x14, waiting for transfers between devices, exchange_plane(): parts[step] = lax.ppermute(part, plane, pairs) if step else part  34.8 us
  transfers between devices with their start and end apart: 81, of which 31 were waited for; matrix products, arithmetic and copies ran while one was open for 12% of the time, Pallas kernels for 33%

profile of v2, /device:TPU:0, one launch (start us, length us, event | category | flops | bytes accessed | tf_op | source)
XLA Modules:
  0.0 941.4 jit_solution(16660587463705472614)
XLA Ops:
  41.1 21.0 %collective-permute-done.1 = bf16[256,2048]{1,0:T(8,128)(2,1)S(1)} collective-permute-done((bf16[256,2048]{1,0:T(8,128)(2,1)S(1)}, bf16[256,2048]{1,0:T(8,128)(2,1)S(1)}, u32[]{:S(2)}, u32[]{:S(2)}) %collective-permute-start.1) | collective-permute-done | bytes 1048608 | tf_op jit(solution)/shard_map/ppermute | solution.py:559
  104.5 27.2 %attention_forward.1 = (bf16[256,1024]{1,0:T(8,128)(2,1)}, bf16[256,1024]{1,0:T(8,128)(2,1)}, bf16[256,1024]{1,0:T(8,128)(2,1)}, bf16[256,1024]{1,0:T(8,128)(2,1)}) custom-call(s32[1]{0:T(128)} %bitcast.4.col_ref, f32[256,1280]{1,0:T(8,128)} %fusion.52.refs_0_.refs_4_.refs_8_, f32[256,1280]{1,0:T(8,128)} %fusion.53.refs_1_.refs_5_.refs_9_, ...), custom_call_target="tpu_custom_call" | custom-call | flops 1000 | bytes 1000 | tf_op jit(solution)/shard_map/attention_forward/pallas_call | solution.py:131
  162.8 26.9 %collective-permute-done.10 = bf16[128,2048]{1,0:T(8,128)(2,1)S(1)} collective-permute-done((bf16[128,2048]{1,0:T(8,128)(2,1)S(1)}, bf16[128,2048]{1,0:T(8,128)(2,1)S(1)}, u32[]{:S(2)}, u32[]{:S(2)}) %collective-permute-start.10) | collective-permute-done | bytes 524320 | tf_op jit(solution)/shard_map/ppermute | solution.py:559
  189.8 10.7 %collective-permute-done.11 = bf16[128,2048]{1,0:T(8,128)(2,1)} collective-permute-done((bf16[128,2048]{1,0:T(8,128)(2,1)S(1)}, bf16[128,2048]{1,0:T(8,128)(2,1)}, u32[]{:S(2)}, u32[]{:S(2)}) %collective-permute-start.11) | collective-permute-done | bytes 524320 | tf_op jit(solution)/shard_map/ppermute | solution.py:559
  213.8 30.3 %collective-permute-done.13 = bf16[128,2048]{1,0:T(8,128)(2,1)S(1)} collective-permute-done((bf16[128,2048]{1,0:T(8,128)(2,1)S(1)}, bf16[128,2048]{1,0:T(8,128)(2,1)S(1)}, u32[]{:S(2)}, u32[]{:S(2)}) %collective-permute-start.13) | collective-permute-done | bytes 524320 | tf_op jit(solution)/shard_map/ppermute | solution.py:559
  252.9 12.5 %collective-permute-done.14 = bf16[128,2048]{1,0:T(8,128)(2,1)S(1)} collective-permute-done((bf16[128,2048]{1,0:T(8,128)(2,1)S(1)}, bf16[128,2048]{1,0:T(8,128)(2,1)S(1)}, u32[]{:S(2)}, u32[]{:S(2)}) %collective-permute-start.14) | collective-permute-done | bytes 524320 | tf_op jit(solution)/shard_map/ppermute | solution.py:559
  271.8 9.9 %all-to-all-done.3 = bf16[8,80,2048]{2,1,0:T(8,128)(2,1)} async-done(((bf16[8,80,2048]{2,1,0:T(8,128)(2,1)}), bf16[8,80,2048]{2,1,0:T(8,128)(2,1)}, u32[]{:S(2)}, u32[]{:S(2)}) %all-to-all-start.3) | async-done | bytes 2621472 | tf_op jit(solution)/shard_map/all_to_all | solution.py:592
  297.6 16.8 %collective-permute-done.15.right_ref = bf16[256,2048]{1,0:T(8,128)(2,1)} collective-permute-done((bf16[256,2048]{1,0:T(8,128)(2,1)}, bf16[256,2048]{1,0:T(8,128)(2,1)}, u32[]{:S(2)}, u32[]{:S(2)}) %collective-permute-start.15) | collective-permute-done | bytes 1048608 | tf_op jit(solution)/shard_map/ppermute | solution.py:559
  329.1 20.9 %expert_block.4 = (bf16[640,768]{1,0:T(8,128)(2,1)}, bf16[640,768]{1,0:T(8,128)(2,1)}, bf16[640,768]{1,0:T(8,128)(2,1)}, bf16[640,2048]{1,0:T(8,128)(2,1)}, bf16[640,2048]{1,0:T(8,128)(2,1)}, /*index=5*/f32[640,1]{1,0:T(8,128)}) custom-call(bf16[640,2048]{1,0:T(8,128)(2,1)} %bitcast.17.rows_ref.refs_0_, bf16[640,2048]{1,0:T(8,128)(2,1)} %bitcast.3.upstream_ref.refs_4_, ...), custom_call_target="tpu_custom_call" | custom-call | flops 1000 | bytes 1000 | tf_op jit(solution)/shard_map/expert_block/pallas_call | solution.py:492
  367.2 20.9 %expert_block.5 = (bf16[640,768]{1,0:T(8,128)(2,1)}, bf16[640,768]{1,0:T(8,128)(2,1)}, bf16[640,768]{1,0:T(8,128)(2,1)}, bf16[640,2048]{1,0:T(8,128)(2,1)}, bf16[640,2048]{1,0:T(8,128)(2,1)}, /*index=5*/f32[640,1]{1,0:T(8,128)}) custom-call(bf16[640,2048]{1,0:T(8,128)(2,1)} %bitcast.30.rows_ref.refs_1_, bf16[640,2048]{1,0:T(8,128)(2,1)} %bitcast.11.upstream_ref.refs_5_, ...), custom_call_target="tpu_custom_call" | custom-call | flops 1000 | bytes 1000 | tf_op jit(solution)/shard_map/expert_block/pallas_call | solution.py:492
  397.3 20.9 %expert_block.6 = (bf16[640,768]{1,0:T(8,128)(2,1)}, bf16[640,768]{1,0:T(8,128)(2,1)}, bf16[640,768]{1,0:T(8,128)(2,1)}, bf16[640,2048]{1,0:T(8,128)(2,1)}, bf16[640,2048]{1,0:T(8,128)(2,1)}, /*index=5*/f32[640,1]{1,0:T(8,128)}) custom-call(bf16[640,2048]{1,0:T(8,128)(2,1)} %bitcast.36.rows_ref.refs_2_, bf16[640,2048]{1,0:T(8,128)(2,1)} %bitcast.15.upstream_ref.refs_6_, ...), custom_call_target="tpu_custom_call" | custom-call | flops 1000 | bytes 1000 | tf_op jit(solution)/shard_map/expert_block/pallas_call | solution.py:492
  418.2 11.4 %all-to-all-done.7 = bf16[8,80,2048]{2,1,0:T(8,128)(2,1)} async-done(((bf16[8,80,2048]{2,1,0:T(8,128)(2,1)}), bf16[8,80,2048]{2,1,0:T(8,128)(2,1)}, u32[]{:S(2)}, u32[]{:S(2)}) %all-to-all-start.7) | async-done | bytes 2621472 | tf_op jit(solution)/shard_map/all_to_all | solution.py:592
  441.7 20.9 %expert_block.7 = (bf16[640,768]{1,0:T(8,128)(2,1)}, bf16[640,768]{1,0:T(8,128)(2,1)}, bf16[640,768]{1,0:T(8,128)(2,1)}, bf16[640,2048]{1,0:T(8,128)(2,1)}, bf16[640,2048]{1,0:T(8,128)(2,1)}, /*index=5*/f32[640,1]{1,0:T(8,128)}) custom-call(bf16[640,2048]{1,0:T(8,128)(2,1)} %bitcast.52.rows_ref.refs_3_, bf16[640,2048]{1,0:T(8,128)(2,1)} %bitcast.13.upstream_ref.refs_7_, ...), custom_call_target="tpu_custom_call" | custom-call | flops 1000 | bytes 1000 | tf_op jit(solution)/shard_map/expert_block/pallas_call | solution.py:492
  484.7 18.2 %collective-permute-done.29 = f32[4,80]{1,0:T(4,128)S(1)} collective-permute-done((f32[4,80]{1,0:T(4,128)S(1)}, f32[4,80]{1,0:T(4,128)S(1)}, u32[]{:S(2)}, u32[]{:S(2)}) %collective-permute-start.29) | collective-permute-done | bytes 1312 | tf_op jit(solution)/shard_map/ppermute | solution.py:607
  557.2 19.9 %collective-permute-done.38 = f32[8,80]{1,0:T(8,128)S(1)} collective-permute-done((f32[8,80]{1,0:T(8,128)S(1)}, f32[8,80]{1,0:T(8,128)S(1)}, u32[]{:S(2)}, u32[]{:S(2)}) %collective-permute-start.38) | collective-permute-done | bytes 2592 | tf_op jit(solution)/shard_map/ppermute | solution.py:559
  602.3 28.1 %weight_gradients.4 = (f32[2048,768]{1,0:T(8,128)}, f32[2048,768]{1,0:T(8,128)}) custom-call(bf16[640,2048]{1,0:T(8,128)(2,1)} %bitcast.17.rows_ref.refs_0_, bf16[640,2048]{1,0:T(8,128)(2,1)} %bitcast.30.rows_ref.refs_1_, bf16[640,2048]{1,0:T(8,128)(2,1)} %bitcast.36.rows_ref.refs_2_, bf16[640,2048]{1,0:T(8,128)(2,1)} %bitcast.52.rows_ref.refs_3_, ...), custom_call_target="tpu_custom_call" | custom-call | flops 1000 | bytes 1000 | tf_op jit(solution)/shard_map/weight_gradients/pallas_call | solution.py:332
  698.5 21.8 %attention_backward.2 = (bf16[256,1280]{1,0:T(8,128)(2,1)}, bf16[256,1280]{1,0:T(8,128)(2,1)}, bf16[256,1280]{1,0:T(8,128)(2,1)}, bf16[256,1280]{1,0:T(8,128)(2,...) custom-call(s32[1]{0:T(128)} %bitcast.4.col_ref, ...), custom_call_target="tpu_custom_call" | custom-call | flops 1000 | bytes 1000 | tf_op jit(solution)/shard_map/attention_backward/pallas_call | solution.py:262
  725.5 23.1 %attention_backward.3 = (bf16[256,1280]{1,0:T(8,128)(2,1)}, bf16[256,1280]{1,0:T(8,128)(2,1)}, bf16[256,1280]{1,0:T(8,128)(2,1)}, bf16[256,1280]{1,0:T(8,128)(2,...) custom-call(s32[1]{0:T(128)} %bitcast.4.col_ref, ...), custom_call_target="tpu_custom_call", output_to_operand_aliasing={{0}: (21, {}), {1}: (22, {}), {2}: (23, {}), {3}: (24, {})} | custom-call | flops 1000 | bytes 1000 | tf_op jit(solution)/shard_map/attention_backward/pallas_call | solution.py:262
  748.6 11.3 %spread.3 = (bf16[256,2048]{1,0:T(8,128)(2,1)}, bf16[256,2048]{1,0:T(8,128)(2,1)}, f32[128,2048]{1,0:T(8,128)}, f32[128,2048]{1,0:T(8,128)}, f32[256,2048]{1,0:T(8,128)}, /*index=5*/f32[8,2048]{1,0:T(8,128)}) custom-call(bf16[256,1280]{1,0:T(8,128)(2,1)} %get-tuple-element.418.refs_0_.refs_4_, bf16[256,1280]{1,0:T(8,128)(2,1)} %get-tuple-element.419.refs_1_.refs_5_, ...), custom_call_target="tpu_custom_call" | custom-call | flops 1000 | bytes 1000 | tf_op jit(solution)/shard_map/spread/pallas_call | solution.py:380
  761.5 18.5 %weight_gradients.5 = f32[768,2048]{1,0:T(8,128)} custom-call(bf16[640,768]{1,0:T(8,128)(2,1)} %get-tuple-element.402.refs_0_, bf16[640,768]{1,0:T(8,128)(2,1)} %get-tuple-element.403.refs_1_, bf16[640,768]{1,0:T(8,128)(2,1)} %get-tuple-element.404.refs_2_, bf16[640,768]{1,0:T(8,128)(2,1)} %get-tuple-element.405.refs_3_, ...), custom_call_target="tpu_custom_call" | custom-call | flops 1000 | bytes 1000 | tf_op jit(solution)/shard_map/weight_gradients/pallas_call | solution.py:332
  787.1 10.3 %weight_gradients.6 = bf16[2048,1024]{1,0:T(8,128)(2,1)} custom-call(bf16[256,2048]{1,0:T(8,128)(2,1)} %get-tuple-element.414.left_ref.refs_0_, bf16[256,2048]{1,0:T(8,128)(2,1)} %collective-permute-done.41.left_ref.refs_1_, bf16[256,2048]{1,0:T(8,128)(2,1)} %pad_maximum_fusion.3.left_ref.refs_2_, ...), custom_call_target="tpu_custom_call" | custom-call | flops 1000 | bytes 1000 | tf_op jit(solution)/shard_map/weight_gradients/pallas_call | solution.py:332
  809.6 11.3 %weight_gradients.7 = bf16[2048,1280]{1,0:T(8,128)(2,1)} custom-call(bf16[256,2048]{1,0:T(8,128)(2,1)} %get-tuple-element.508.refs_0_, bf16[256,2048]{1,0:T(8,128)(2,1)} %copy-done.9, bf16[256,2048]{1,0:T(8,128)(2,1)} %copy-done.7, bf16[256,2048]{1,0:T(8,128)(2,1)} %copy-done.8, bf16[256,1280]{1,0:T(8,128)(2,1)} %get-tuple-element.418.refs_0_.refs_4_, ...), custom_call_target="tpu_custom_call" | custom-call | flops 1000 | bytes 1000 | tf_op jit(solution)/shard_map/weight_gradients/pallas_call | solution.py:332
  842.7 32.1 %collective-permute-done.51.refs_0_ = bf16[256,2048]{1,0:T(8,128)(2,1)} collective-permute-done((bf16[256,2048]{1,0:T(8,128)(2,1)}, bf16[256,2048]{1,0:T(8,128)(2,1)}, u32[]{:S(2)}, u32[]{:S(2)}) %collective-permute-start.51) | collective-permute-done | bytes 1048608 | tf_op jit(solution)/shard_map/ppermute | solution.py:559
  915.7 14.8 %all-to-all-done.17 = bf16[4,256,1280]{2,1,0:T(8,128)(2,1)} async-done(((bf16[4,256,1280]{2,1,0:T(8,128)(2,1)}), bf16[4,256,1280]{2,1,0:T(8,128)(2,1)}, u32[]{:S(2)}, u32[]{:S(2)}) %all-to-all-start.17) | async-done | bytes 2621472 | tf_op jit(solution)/shard_map/all_to_all | solution.py:883
  (431 shorter events, 466.5 us)
Async XLA Ops:
  7.2 54.9 %all-gather.3.cloned.1.call-start = ((), (), s32[]{:S(2)}) async-start(), calls=%async_computation.19 | async-start | bytes 7864320 | tf_op jit(solution)/shard_map/all_gather | solution.py:662
  15.0 47.1 %collective-permute-start.1 = (bf16[256,2048]{1,0:T(8,128)(2,1)S(1)}, bf16[256,2048]{1,0:T(8,128)(2,1)S(1)}, u32[]{:S(2)}, u32[]{:S(2)}) collective-permute-start(bf16[256,2048]{1,0:T(8,128)(2,1)S(1)} %copy-done.2), channel_id=1, source_target_pairs={{0,3},{1,0},{2,1},{3,2},{4,7},{5,4},{6,5},{7,6},{8,11},{9,8},{10,9... | collective-permute-start | bytes 3145736 | tf_op jit(solution)/shard_map/ppermute | solution.py:559
  22.7 66.1 %all-to-all-start = ((bf16[8,80,2048]{2,1,0:T(8,128)(2,1)}), bf16[8,80,2048]{2,1,0:T(8,128)(2,1)}, u32[]{:S(2)}, u32[]{:S(2)}) async-start(bf16[8,80,2048]{2,1,0:T(8,128)(2,1)} %bitcast.275), calls=%async_computation | async-start | bytes 5242880 | tf_op jit(solution)/shard_map/all_to_all | solution.py:592
  27.3 104.4 %all-gather.5.cloned.1.call-start = ((), (), s32[]{:S(2)}) async-start(), calls=%async_computation.20 | async-start | bytes 6291456 | tf_op jit(solution)/shard_map/all_gather | solution.py:663
  88.9 50.9 %collective-permute-start.6 = (s32[8,256]{1,0:T(8,128)S(1)}, s32[8,256]{1,0:T(8,128)S(1)}, u32[]{:S(2)}, u32[]{:S(2)}) collective-permute-start(s32[8,256]{1,0:T(8,128)S(1)} %bitcast.299), channel_id=1, source_target_pairs={{0,1},{1,2},{2,3},{3,0},{4,5},{5,6},{6,7},{7,4},{8,9},{9,10},{10,1... | collective-permute-start | bytes 24584 | tf_op jit(solution)/shard_map/ppermute | solution.py:559
  89.3 50.5 %collective-permute-start.7 = (s32[8,256]{1,0:T(8,128)S(1)}, s32[8,256]{1,0:T(8,128)S(1)}, u32[]{:S(2)}, u32[]{:S(2)}) collective-permute-start(s32[8,256]{1,0:T(8,128)S(1)} %bitcast.300), channel_id=1, source_target_pairs={{0,2},{1,3},{2,0},{3,1},{4,6},{5,7},{6,4},{7,5},{8,10},{9,11},{10,... | collective-permute-start | bytes 24584 | tf_op jit(solution)/shard_map/ppermute | solution.py:559
  91.6 48.2 %collective-permute-start.8 = (s32[8,256]{1,0:T(8,128)S(1)}, s32[8,256]{1,0:T(8,128)S(1)}, u32[]{:S(2)}, u32[]{:S(2)}) collective-permute-start(s32[8,256]{1,0:T(8,128)S(1)} %bitcast.301), channel_id=1, source_target_pairs={{0,3},{1,0},{2,1},{3,2},{4,7},{5,4},{6,5},{7,6},{8,11},{9,8},{10,9... | collective-permute-start | bytes 24584 | tf_op jit(solution)/shard_map/ppermute | solution.py:559
  92.8 48.8 %collective-permute-start.4 = (bf16[256,2048]{1,0:T(8,128)(2,1)}, bf16[256,2048]{1,0:T(8,128)(2,1)}, u32[]{:S(2)}, u32[]{:S(2)}) collective-permute-start(bf16[256,2048]{1,0:T(8,128)(2,1)} %right_ref.1), channel_id=1, source_target_pairs={{0,1},{1,2},{2,3},{3,0},{4,5},{5,6},{6,7},{7,4},{8,9},{9,10},{10,1... | collective-permute-start | bytes 3145736 | tf_op jit(solution)/shard_map/ppermute | solution.py:559
  93.6 48.0 %collective-permute-start.5 = (bf16[256,2048]{1,0:T(8,128)(2,1)}, bf16[256,2048]{1,0:T(8,128)(2,1)}, u32[]{:S(2)}, u32[]{:S(2)}) collective-permute-start(bf16[256,2048]{1,0:T(8,128)(2,1)} %right_ref.1), channel_id=1, source_target_pairs={{0,3},{1,0},{2,1},{3,2},{4,7},{5,4},{6,5},{7,6},{8,11},{9,8},{10,9... | collective-permute-start | bytes 3145736 | tf_op jit(solution)/shard_map/ppermute | solution.py:559
  146.0 56.6 %all-to-all-start.1 = ((bf16[8,80,2048]{2,1,0:T(8,128)(2,1)}), bf16[8,80,2048]{2,1,0:T(8,128)(2,1)}, u32[]{:S(2)}, u32[]{:S(2)}) async-start(bf16[8,80,2048]{2,1,0:T(8,128)(2,1)} %bitcast.278), calls=%async_computation.1 | async-start | bytes 5242880 | tf_op jit(solution)/shard_map/all_to_all | solution.py:592
  150.4 52.2 %collective-permute-start.9 = (bf16[256,2048]{1,0:T(8,128)(2,1)}, bf16[256,2048]{1,0:T(8,128)(2,1)S(1)}, u32[]{:S(2)}, u32[]{:S(2)}) collective-permute-start(bf16[256,2048]{1,0:T(8,128)(2,1)} %get-tuple-element.243), channel_id=1, source_target_pairs={{0,1},{1,2},{2,3},{3,0},{4,5},{5,6},{6,7},{7,4},{8,9},{9,10},{10,1... | collective-permute-start | bytes 3145736 | tf_op jit(solution)/shard_map/ppermute | solution.py:559
  153.7 46.8 %collective-permute-start.11 = (bf16[128,2048]{1,0:T(8,128)(2,1)S(1)}, bf16[128,2048]{1,0:T(8,128)(2,1)}, u32[]{:S(2)}, u32[]{:S(2)}) collective-permute-start(bf16[128,2048]{1,0:T(8,128)(2,1)S(1)} %slice.129), channel_id=1, source_target_pairs={{0,3},{1,0},{2,1},{3,2},{4,7},{5,4},{6,5},{7,6},{8,11},{9,8},{10,9... | collective-permute-start | bytes 1572872 | tf_op jit(solution)/shard_map/ppermute | solution.py:559
  202.6 41.5 %all-to-all-start.2 = ((bf16[8,80,2048]{2,1,0:T(8,128)(2,1)}), bf16[8,80,2048]{2,1,0:T(8,128)(2,1)}, u32[]{:S(2)}, u32[]{:S(2)}) async-start(bf16[8,80,2048]{2,1,0:T(8,128)(2,1)} %bitcast.277), calls=%async_computation.2 | async-start | bytes 5242880 | tf_op jit(solution)/shard_map/all_to_all | solution.py:592
  590.5 53.3 %all-to-all-start.12 = ((bf16[8,80,2048]{2,1,0:T(8,128)(2,1)}), bf16[8,80,2048]{2,1,0:T(8,128)(2,1)}, u32[]{:S(2)}, u32[]{:S(2)}) async-start(bf16[8,80,2048]{2,1,0:T(8,128)(2,1)} %bitcast.288), calls=%async_computation.12 | async-start | bytes 5242880 | tf_op jit(solution)/shard_map/all_to_all | solution.py:592
  594.9 43.9 %collective-permute-start.41 = (bf16[256,2048]{1,0:T(8,128)(2,1)}, bf16[256,2048]{1,0:T(8,128)(2,1)}, u32[]{:S(2)}, u32[]{:S(2)}) collective-permute-start(bf16[256,2048]{1,0:T(8,128)(2,1)} %get-tuple-element.414.left_ref.refs_0_), channel_id=1, source_target_pairs={{0,1},{1,2},{2,3},{3,0},{4,5},{5,6},{6,7},{7,4},{8,9},{9,10},{10,1... | collective-permute-start | bytes 3145736 | tf_op jit(solution)/shard_map/ppermute | solution.py:559
  595.5 48.2 %collective-permute-start.42 = (bf16[256,2048]{1,0:T(8,128)(2,1)}, bf16[256,2048]{1,0:T(8,128)(2,1)}, u32[]{:S(2)}, u32[]{:S(2)}) collective-permute-start(bf16[256,2048]{1,0:T(8,128)(2,1)} %get-tuple-element.414.left_ref.refs_0_), channel_id=1, source_target_pairs={{0,3},{1,0},{2,1},{3,2},{4,7},{5,4},{6,5},{7,6},{8,11},{9,8},{10,9... | collective-permute-start | bytes 3145736 | tf_op jit(solution)/shard_map/ppermute | solution.py:559
  688.5 91.5 %all-to-all-start.14 = ((bf16[8,80,2048]{2,1,0:T(8,128)(2,1)}), bf16[8,80,2048]{2,1,0:T(8,128)(2,1)}, u32[]{:S(2)}, u32[]{:S(2)}) async-start(bf16[8,80,2048]{2,1,0:T(8,128)(2,1)} %bitcast.285), calls=%async_computation.14 | async-start | bytes 5242880 | tf_op jit(solution)/shard_map/all_to_all | solution.py:592
  725.1 54.9 %collective-permute-start.50 = (bf16[256,2048]{1,0:T(8,128)(2,1)}, bf16[256,2048]{1,0:T(8,128)(2,1)}, u32[]{:S(2)}, u32[]{:S(2)}) collective-permute-start(bf16[256,2048]{1,0:T(8,128)(2,1)} %product.37), channel_id=1, source_target_pairs={{0,1},{1,2},{2,3},{3,0},{4,5},{5,6},{6,7},{7,4},{8,9},{9,10},{10,1... | collective-permute-start | bytes 3145736 | tf_op jit(solution)/shard_map/ppermute | solution.py:559
  804.9 108.7 %reduce-scatter.2.cloned.1.call-start = ((), (), s32[]{:S(2)}) async-start(), calls=%async_computation.21 | async-start | bytes 2621440 | tf_op jit(solution)/shard_map/reduce_scatter | solution.py:873
  824.5 59.2 %collective-permute-start.55 = (bf16[1024,1280]{1,0:T(8,128)(2,1)}, bf16[1024,1280]{1,0:T(8,128)(2,1)}, u32[]{:S(2)}, u32[]{:S(2)}) collective-permute-start(bf16[1024,1280]{1,0:T(8,128)(2,1)} %dynamic-slice_bitcast_fusion), channel_id=1, source_target_pairs={{0,4},{4,0},{1,5},{5,1},{2,6},{6,2},{3,7},{7,3},{8,12},{12,8},{9,1... | collective-permute-start | bytes 7864328 | tf_op jit(solution)/shard_map/ppermute | solution.py:868
  825.8 62.6 %collective-permute-start.52 = (bf16[256,2048]{1,0:T(8,128)(2,1)}, bf16[256,2048]{1,0:T(8,128)(2,1)}, u32[]{:S(2)}, u32[]{:S(2)}) collective-permute-start(bf16[256,2048]{1,0:T(8,128)(2,1)} %get-tuple-element.411), channel_id=1, source_target_pairs={{0,3},{1,0},{2,1},{3,2},{4,7},{5,4},{6,5},{7,6},{8,11},{9,8},{10,9... | collective-permute-start | bytes 3145736 | tf_op jit(solution)/shard_map/ppermute | solution.py:559
  827.5 47.3 %collective-permute-start.51 = (bf16[256,2048]{1,0:T(8,128)(2,1)}, bf16[256,2048]{1,0:T(8,128)(2,1)}, u32[]{:S(2)}, u32[]{:S(2)}) collective-permute-start(bf16[256,2048]{1,0:T(8,128)(2,1)} %product.38), channel_id=1, source_target_pairs={{0,1},{1,2},{2,3},{3,0},{4,5},{5,6},{6,7},{7,4},{8,9},{9,10},{10,1... | collective-permute-start | bytes 3145736 | tf_op jit(solution)/shard_map/ppermute | solution.py:559
  831.3 57.1 %collective-permute-start.53 = (bf16[128,2048]{1,0:T(8,128)(2,1)}, bf16[128,2048]{1,0:T(8,128)(2,1)}, u32[]{:S(2)}, u32[]{:S(2)}) collective-permute-start(bf16[128,2048]{1,0:T(8,128)(2,1)} %add_convert_fusion.2), channel_id=1, source_target_pairs={{0,1},{1,2},{2,3},{3,0},{4,5},{5,6},{6,7},{7,4},{8,9},{9,10},{10,1... | collective-permute-start | bytes 1572872 | tf_op jit(solution)/shard_map/ppermute | solution.py:559
  838.5 44.0 %all-to-all-start.16 = ((f32[8,1,20736]{2,1,0:T(1,128)}), f32[8,1,20736]{2,1,0:T(1,128)}, u32[]{:S(2)}, u32[]{:S(2)}) async-start(f32[8,1,20736]{2,1,0:T(1,128)} %reshape.441), calls=%async_computation.16 | async-start | bytes 1327104 | tf_op jit(solution)/shard_map/all_to_all | solution.py:592
  (91 other events, 2231.9 us)
Sparse Core Ops, SparseCore 0:
  10.9 18.3 all-gather.2
  30.8 14.8 all-gather.4
  831.4 44.0 reduce-scatter.1

commit v3 on v2

--- a/solution.py
+++ b/solution.py
@@ -1,4 +1,5 @@
 import functools
+import math
 
 import jax
 import jax.numpy as jnp
@@ -66,23 +67,13 @@
         ref[...] = held[pl.ds(place_of(col_ref, len(refs), tokens, step), tokens), :].astype(ref.dtype)
 
 
-def softmax_rows(query, keys_ref, first, tokens, scale):
-    diagonal = dot_nt(query, keys_ref[pl.ds(first, tokens), :])
-    row = lax.broadcasted_iota(jnp.int32, diagonal.shape, 0)
-    column = lax.broadcasted_iota(jnp.int32, diagonal.shape, 1)
-    diagonal = jnp.where(row >= column, diagonal * scale, -1e30)
-    peak = jnp.max(diagonal, axis=1, keepdims=True)
-    if first:
-        former = dot_nt(query, keys_ref[pl.ds(0, first), :]) * scale
-        peak = jnp.maximum(peak, jnp.max(former, axis=1, keepdims=True))
-        former = jnp.exp(former - peak)
-        diagonal = jnp.exp(diagonal - peak)
-        inverse = 1.0 / (
-            jnp.sum(former, axis=1, keepdims=True) + jnp.sum(diagonal, axis=1, keepdims=True)
-        )
-        return former * inverse, diagonal * inverse
-    diagonal = jnp.exp(diagonal - peak)
-    return None, diagonal / jnp.sum(diagonal, axis=1, keepdims=True)
+def scores_of(keys, query, first, scale):
+    count = query.shape[0]
+    scores = dot_nt(keys[pl.ds(0, first + count), :], query) * (scale * math.log2(math.e))
+    row = lax.broadcasted_iota(jnp.int32, (count, count), 0)
+    column = lax.broadcasted_iota(jnp.int32, (count, count), 1)
+    last = jnp.where(row <= column, scores[first:], -1e30)
+    return jnp.concatenate([scores[:first], last], axis=0) if first else last
 
 
 def prepare_keys(col_ref, k_refs, v_refs, cos_ref, sin_ref, kg_ref, raw_rows, keys, values):
@@ -100,7 +91,7 @@
     q_refs, k_refs, v_refs = refs[:blocks], refs[blocks : 2 * blocks], refs[2 * blocks : 3 * blocks]
     cos_ref, sin_ref, qg_ref, kg_ref = refs[3 * blocks : 3 * blocks + 4]
     out_refs = refs[3 * blocks + 4 : 4 * blocks + 4]
-    raw_rows, keys, values, mixed_rows = refs[4 * blocks + 4 :]
+    level_ref, raw_rows, keys, values, mixed_rows = refs[4 * blocks + 4 :]
     tokens = q_refs[0].shape[0]
 
     @pl.when(pl.program_id(0) == 0)
@@ -114,11 +105,13 @@
         raw = raw_rows[there, :]
         rows = raw * inverse_rms(raw) * qg_ref[...]
         query = turn(rows, cos_ref[there, :], sin_ref[there, :]).astype(bf16)
-        former, diagonal = softmax_rows(query, keys, first, tokens, scale)
-        mixed = dot_nn(diagonal.astype(bf16), values[there, :])
-        if first:
-            mixed = mixed + dot_nn(former.astype(bf16), values[pl.ds(0, first), :])
-        mixed_rows[there, :] = mixed.astype(bf16)
+        scores = scores_of(keys, query, first, scale)
+        peak = jnp.max(scores, axis=0, keepdims=True)
+        probs = jnp.exp2(scores - peak)
+        total = jnp.sum(probs, axis=0, keepdims=True)
+        level_ref[0, :, there] = peak + jnp.log2(total)
+        probs = (probs * (1.0 / total)).astype(bf16)
+        mixed_rows[there, :] = dot_tn(probs, values[pl.ds(0, first + tokens), :]).astype(bf16)
     out_of_order(col_ref, mixed_rows, out_refs)
 
 
@@ -130,7 +123,10 @@
     gain = pl.BlockSpec((1, head_size), lambda h, c: (0, 0))
     return pl.pallas_call(
         functools.partial(forward_kernel, blocks, head_size ** (-0.5)),
-        out_shape=[jax.ShapeDtypeStruct((tokens, heads * head_size), bf16)] * blocks,
+        out_shape=[
+            *[jax.ShapeDtypeStruct((tokens, heads * head_size), bf16)] * blocks,
+            jax.ShapeDtypeStruct((heads, 1, seq_len), f32),
+        ],
         grid_spec=pltpu.PrefetchScalarGridSpec(
             num_scalar_prefetch=1,
             grid=(heads,),
@@ -143,7 +139,10 @@
                 gain,
                 gain,
             ],
-            out_specs=column(lambda h, c: (0, h)),
+            out_specs=[
+                *column(lambda h, c: (0, h)),
+                pl.BlockSpec((1, 1, seq_len), lambda h, c: (h, 0, 0)),
+            ],
             scratch_shapes=[
                 pltpu.VMEM((seq_len, head_size), f32),
                 pltpu.VMEM((seq_len, head_size), bf16),
@@ -159,8 +158,8 @@
 
 def backward_kernel(blocks, scale, first_head, heads, final, col_ref, *refs):
     q_refs, k_refs, v_refs, g_refs = (refs[i * blocks : (i + 1) * blocks] for i in range(4))
-    cos_ref, sin_ref, qg_ref, kg_ref = refs[4 * blocks : 4 * blocks + 4]
-    refs = refs[4 * blocks + 4 :]
+    cos_ref, sin_ref, qg_ref, kg_ref, level_ref = refs[4 * blocks : 4 * blocks + 5]
+    refs = refs[4 * blocks + 5 :]
     if first_head:
         refs = refs[blocks:]
         held_refs, refs = refs[:4], refs[4:]
@@ -202,22 +201,14 @@
             unit = raw * inverse
             query = turn(unit * qg_ref[...], cos_ref[there, :], sin_ref[there, :]).astype(bf16)
             grad_mixed = mixed_rows[there, :]
-            former, diagonal = softmax_rows(query, keys, first, tokens, scale)
-            grad_diagonal = dot_nt(grad_mixed, values[there, :])
-            inner = jnp.sum(diagonal * grad_diagonal, axis=1, keepdims=True)
-            if first:
-                before = pl.ds(0, first)
-                grad_former = dot_nt(grad_mixed, values[before, :])
-                inner = inner + jnp.sum(former * grad_former, axis=1, keepdims=True)
-                score_former = (former * (grad_former - inner)).astype(bf16)
-                grad_keys[before, :] += dot_tn(score_former, query)
-                grad_values[before, :] += dot_tn(former.astype(bf16), grad_mixed)
-            score_diagonal = (diagonal * (grad_diagonal - inner)).astype(bf16)
-            grad_keys[there, :] += dot_tn(score_diagonal, query)
-            grad_values[there, :] += dot_tn(diagonal.astype(bf16), grad_mixed)
-            grad_query = dot_nn(score_diagonal, keys[there, :])
-            if first:
-                grad_query = grad_query + dot_nn(score_former, keys[before, :])
+            upto = pl.ds(0, first + tokens)
+            probs = jnp.exp2(scores_of(keys, query, first, scale) - level_ref[0, :, there])
+            grad_probs = dot_nt(values[upto, :], grad_mixed)
+            inner = jnp.sum(probs * grad_probs, axis=0, keepdims=True)
+            grad_scores = (probs * (grad_probs - inner)).astype(bf16)
+            grad_values[upto, :] += dot_nn(probs.astype(bf16), grad_mixed)
+            grad_keys[upto, :] += dot_nn(grad_scores, query)
+            grad_query = dot_tn(grad_scores, keys[upto, :])
             grad_rows[there, :] = through_norm(
                 grad_query * scale, unit, inverse, there, qg_ref, qgain_ref
             ).astype(bf16)
@@ -248,10 +239,11 @@
 
 
 def attention_backward(
-    col, qkv, grad_attended, cosine, sine, query_gain, key_gain, all_heads, first, heads, former=None
+    col, qkv, grad_attended, cosine, sine, query_gain, key_gain, levels, first, heads, former=None
 ):
     blocks, tokens, head_size = len(qkv), qkv[0].shape[0], query_gain.shape[-1]
     seq_len = blocks * tokens
+    all_heads = levels.shape[0]
     final = first + heads == all_heads
     column = lambda index: [pl.BlockSpec((tokens, head_size), index)] * blocks
     whole = pl.BlockSpec((seq_len, head_size), lambda h, c: (0, 0))
@@ -280,6 +272,7 @@
                 whole,
                 gain,
                 gain,
+                pl.BlockSpec((1, 1, seq_len), lambda h, c: (jnp.minimum(h + first, last), 0, 0)),
                 *([] if former is None else [pl.BlockSpec(memory_space=pl.ANY)] * blocks),
                 *([] if former is None else [gain_out, gain_out, whole, whole]),
             ],
@@ -294,11 +287,11 @@
                 pltpu.VMEM((seq_len, head_size), f32),
             ],
         ),
-        input_output_aliases={} if former is None else {1 + 4 * blocks + 4 + i: i for i in range(blocks)},
+        input_output_aliases={} if former is None else {1 + 4 * blocks + 5 + i: i for i in range(blocks)},
         compiler_params=pltpu.CompilerParams(vmem_limit_bytes=60 * 2**20),
         cost_estimate=pl.CostEstimate(flops=1000, bytes_accessed=1000, transcendentals=0),
         name="attention_backward",
-    )(col, *qkv, *qkv, *qkv, *grad_attended, cosine, sine, query_gain, key_gain, *held)
+    )(col, *qkv, *qkv, *qkv, *grad_attended, cosine, sine, query_gain, key_gain, levels, *held)
 
 
 def weight_kernel(blocks, rights, weighted, *refs):
@@ -324,8 +317,7 @@
         out_ref[...] = total.astype(out_ref.dtype)
 
 
-def weight_gradients(lefts, rights, out_type, weights=None, tile=256, order=None):
-    order = order or (lambda i: i)
+def weight_gradients(lefts, rights, out_type, weights=None, tile=256):
     blocks, rows, tall = len(lefts), lefts[0].shape[0], lefts[0].shape[1]
     flat = [block for right in rights for block in right]
     fixed = lambda array: pl.BlockSpec(array.shape, lambda i: (0, 0))
@@ -339,7 +331,7 @@
             *([] if weights is None else [fixed(weight) for weight in weights]),
         ],
         out_specs=[
-            pl.BlockSpec((tile, right[0].shape[1]), lambda i: (order(i), 0)) for right in rights
+            pl.BlockSpec((tile, right[0].shape[1]), lambda i: (i, 0)) for right in rights
         ],
         scratch_shapes=[] if weights is None else [pltpu.VMEM(block.shape, bf16) for block in flat],
         compiler_params=pltpu.CompilerParams(vmem_limit_bytes=60 * 2**20),
@@ -348,20 +340,60 @@
     )(*lefts, *flat, *([] if weights is None else weights))
 
 
+def split_kernel(blocks, groups, mine_ref, *refs):
+    left_refs, right_refs, out_refs = refs[:blocks], refs[blocks : 2 * blocks], refs[2 * blocks :]
+    total = dot_tn(left_refs[0][...], right_refs[0][...])
+    for block in range(1, blocks):
+        total = total + dot_tn(left_refs[block][...], right_refs[block][...])
+    for index, out_ref in enumerate(out_refs):
+
+        @pl.when(pl.program_id(0) // groups == index)
+        def _():
+            out_ref[...] = total.astype(out_ref.dtype)
+
+
+def split_gradient(lefts, right, mine, devices, groups):
+    blocks, rows, tall = len(lefts), lefts[0].shape[0], lefts[0].shape[1]
+    tile, wide = tall // (devices * groups), right[0].shape[1]
+
+    def left_tile(i, mine_ref):
+        return (0, i % groups * devices + lax.rem(mine_ref[0] + i // groups, devices))
+
+    def out_tile(index):
+        return lambda i, mine_ref: (jnp.clip(i - index * groups, 0, groups - 1), 0)
+
+    return pl.pallas_call(
+        functools.partial(split_kernel, blocks, groups),
+        out_shape=[jax.ShapeDtypeStruct((groups * tile, wide), bf16)] * devices,
+        grid_spec=pltpu.PrefetchScalarGridSpec(
+            num_scalar_prefetch=1,
+            grid=(devices * groups,),
+            in_specs=[
+                *[pl.BlockSpec((rows, tile), left_tile)] * blocks,
+                *[pl.BlockSpec((rows, wide), lambda i, mine_ref: (0, 0))] * blocks,
+            ],
+            out_specs=[pl.BlockSpec((tile, wide), out_tile(index)) for index in range(devices)],
+        ),
+        compiler_params=pltpu.CompilerParams(vmem_limit_bytes=60 * 2**20),
+        cost_estimate=pl.CostEstimate(flops=1000, bytes_accessed=1000, transcendentals=0),
+        name="split_gradient",
+    )(mine, *lefts, *right)
+
+
 def spread_kernel(with_units, *refs):
     block_refs, weight_ref, refs = refs[:4], refs[4], refs[5:]
     if with_units:
         unit_refs, refs = refs[:4], refs[4:]
-    up_ref, down_ref, up_rest, down_rest, own_ref = refs[:5]
+    far_up, far_down, free_up, free_down, up_rest, down_rest, own_ref = refs[:7]
     weight = weight_ref[...]
     middle = own_ref.shape[0] // 2
     shares = {}
     for step in (2, 3, 1, 0):
         shares[step] = dot_nt(block_refs[step][...], weight)
-    up_ref[:middle, :] = shares[2][:middle].astype(bf16)
-    up_ref[middle:, :] = shares[3][middle:].astype(bf16)
-    down_ref[:middle, :] = shares[1][:middle].astype(bf16)
-    down_ref[middle:, :] = shares[2][middle:].astype(bf16)
+    far_up[...] = shares[2][:middle].astype(bf16)
+    far_down[...] = shares[2][middle:].astype(bf16)
+    free_up[...] = shares[3][middle:].astype(bf16)
+    free_down[...] = shares[1][:middle].astype(bf16)
     up_rest[...] = shares[3][:middle]
     down_rest[...] = shares[1][middle:]
     own_ref[...] = shares[0]
@@ -369,7 +401,7 @@
         total = sum(
             jnp.sum(shares[step] * unit_refs[step][...], axis=0, keepdims=True) for step in range(4)
         )
-        refs[5][...] = jnp.broadcast_to(total, refs[5].shape)
+        refs[7][...] = jnp.broadcast_to(total, refs[7].shape)
 
 
 def spread(blocks, weight, units=None, tile=512):
@@ -380,10 +412,8 @@
     return pl.pallas_call(
         functools.partial(spread_kernel, units is not None),
         out_shape=[
-            shape((tokens, width), bf16),
-            shape((tokens, width), bf16),
-            shape((tokens // 2, width), f32),
-            shape((tokens // 2, width), f32),
+            *[shape((tokens // 2, width), bf16)] * 4,
+            *[shape((tokens // 2, width), f32)] * 2,
             shape((tokens, width), f32),
             *([] if units is None else [shape((8, width), f32)]),
         ],
@@ -394,10 +424,7 @@
             *([] if units is None else [part(tokens)] * 4),
         ],
         out_specs=[
-            part(tokens),
-            part(tokens),
-            part(tokens // 2),
-            part(tokens // 2),
+            *[part(tokens // 2)] * 6,
             part(tokens),
             *([] if units is None else [part(8)]),
         ],
@@ -568,22 +595,16 @@
         return up(block), down(block)
 
     def gather_far(former, latter):
-        return jnp.concatenate([up(former[:middle]), down(latter[middle:])], axis=0)
-
-    def scatter_first(up_rows, down_rows, *_):
-        return up(up_rows), down(down_rows)
-
-    def scatter_second(first, up_rest, down_rest):
-        return (
-            up((up_rest + first[0][:middle].astype(f32)).astype(bf16)),
-            down((down_rest + first[1][middle:].astype(f32)).astype(bf16)),
-        )
-
-    def scatter_own(own, first, second):
+        return up(former[:middle]), down(latter[middle:])
+
+    def scatter_second(rest, far):
+        return (rest + far.astype(f32)).astype(bf16)
+
+    def scatter_own(own, second_up, second_down, free_up, free_down):
         return own + jnp.concatenate(
             [
-                second[0].astype(f32) + first[1][:middle].astype(f32),
-                first[0][middle:].astype(f32) + second[1].astype(f32),
+                second_up.astype(f32) + free_down.astype(f32),
+                free_up.astype(f32) + second_down.astype(f32),
             ],
             axis=0,
         )
@@ -666,7 +687,7 @@
     cotangent_rows = [swap(pick(0, cotangent)), None, None, None]
     near_inputs, full_qkv = after((near_inputs, full_qkv))
 
-    far_inputs = gather_far(*near_inputs)
+    far_inputs = jnp.concatenate(gather_far(*near_inputs), axis=0)
     def project(block):
         rows = block.astype(f32)
         unit = rows * inverse_rms(rows)
@@ -686,33 +707,39 @@
     projected[2] = project(far_inputs)
     units, normed, qkv = zip(*projected)
     query_gain, key_gain = query_norm_gain[None, :], key_norm_gain[None, :]
-    attended = attention_forward(col_array, qkv, cosine, sine, query_gain, key_gain, heads)
+    *attended, levels = attention_forward(col_array, qkv, cosine, sine, query_gain, key_gain, heads)
     shares = spread(attended, full_out)
+    ids_blocks = after(ids_blocks, attended)
     slot_mats += [slot_mat(ids_blocks[s]) for s in (1, 2, 3)]
-    near_cotangent, shares, slot_mats = after((near_cotangent, shares, slot_mats))
-
-    up_rows, down_rows, up_rest, down_rest, own_share = shares
-    first_up = up(up_rows)
-    far_cotangent = gather_far(*near_cotangent)
-    cotangent_rows[1] = swap(pick(1, near_cotangent[0]))
+    picked = pick(1, after(near_cotangent[0], attended))
+    near_cotangent, shares, slot_mats, picked = after((near_cotangent, shares, slot_mats, picked))
+
+    send_up, send_down, free_up, free_down, up_rest, down_rest, own_share = shares
+    cotangent_rows[1] = swap(picked)
+    first_up, first_down = up(send_up), down(send_down)
+    far_up = up(near_cotangent[0][:middle])
     chosen_all, slots_all = slots_of(own_ids, all_experts)
     picked = pick(3, near_cotangent[1])
-    first_up, far_cotangent, cotangent_rows[1], chosen_all, slots_all, down_rows, picked = after(
-        (first_up, far_cotangent, cotangent_rows[1], chosen_all, slots_all, down_rows, picked)
-    )
-    first_down = down(down_rows)
-    second_up = up((up_rest + first_up[:middle].astype(f32)).astype(bf16))
+    late_half = near_cotangent[1][middle:]
+    first_up, first_down, far_up, cotangent_rows[1], chosen_all, slots_all, picked, late_half, frees = after(
+        (
+            first_up, first_down, far_up, cotangent_rows[1], chosen_all, slots_all, picked, late_half,
+            (free_up, free_down),
+        )
+    )
     cotangent_rows[3] = swap(picked)
-    picked = pick(2, far_cotangent)
-    first_down, second_up, cotangent_rows[3], picked = after(
-        (first_down, second_up, cotangent_rows[3], picked)
-    )
-
-    second_down = down((down_rest + first_down[middle:].astype(f32)).astype(bf16))
+    far_down = down(late_half)
+    second_up = up(scatter_second(up_rest, first_up))
+    second_down = down(scatter_second(down_rest, first_down))
+    picked = pick(2, jnp.concatenate([far_up, far_down], axis=0))
+    second_up, second_down, picked, cotangent_rows[3], frees = after(
+        (second_up, second_down, picked, cotangent_rows[3], frees)
+    )
+
+    free_up, free_down = up(frees[0]), down(frees[1])
     cotangent_rows[2] = swap(picked)
     gate_weight, up_weight, down_weight = gate_proj[0], up_proj[0], down_proj[0]
-    branch_first, branch_second = (first_up, first_down), (second_up, second_down)
-    hidden = inputs.astype(f32) + scatter_own(own_share, branch_first, branch_second)
+    hidden = inputs.astype(f32) + scatter_own(own_share, second_up, second_down, free_up, free_down)
     inverse_hidden = inverse_rms(hidden)
     routed = (hidden * inverse_hidden * moe_gain).astype(bf16)
     own_rows = after(pick(0, routed), cotangent_rows[2])
@@ -803,24 +830,25 @@
 
     grad_low = grad_hidden.astype(bf16)
     near_gradient = gather_near(grad_low)
-    output_back = {1: swap(after(returned[1], grad_low))}
+    output_back = {1: swap(after(returned[1], grad_back[0]))}
     grad_attended = {0: product(grad_low, full_out)}
     grad_gate_weight, grad_up_weight = weight_gradients(
         after(arrived, grad_low), [gate_grads, up_grads], f32, row_weights
     )
-    near_gradient, output_back[1], grad_gate_weight, grad_attended = after(
-        (near_gradient, output_back[1], grad_gate_weight, grad_attended)
+    near_gradient, grad_gate_weight, grad_attended = after(
+        (near_gradient, grad_gate_weight, grad_attended)
     )
 
     far_gradient = gather_far(*near_gradient)
-    output_back[2] = swap(after(returned[2], near_gradient))
+    output_back[2] = swap(after(returned[2], output_back[1], grad_low))
     grad_attended.update({1: product(near_gradient[0], full_out), 3: product(near_gradient[1], full_out)})
     output_part = collect(output_back, 1)
+    far_gradient = jnp.concatenate(after(far_gradient, output_part), axis=0)
     router_sums = grad_router.reshape(1, columns, width // columns * experts)
     router_sums = jnp.take(after(router_sums, near_gradient), to_ring, axis=1)
     router_sums = jnp.sum(exchange_columns(router_sums)[0], axis=0)
-    far_gradient, output_back[2], grad_attended, output_part, router_sums = after(
-        (far_gradient, output_back[2], grad_attended, output_part, router_sums)
+    far_gradient, grad_attended, output_part, router_sums = after(
+        (far_gradient, grad_attended, output_part, router_sums)
     )
 
     grad_sequence = [grad_low, near_gradient[0], far_gradient, near_gradient[1]]
@@ -829,60 +857,72 @@
     grad_attended[2] = product(far_gradient, full_out)
     grad_attended = [grad_attended[s] for s in range(columns)]
     half = heads // 2
-    arguments = (col_array, qkv, grad_attended, cosine, sine, query_gain, key_gain, heads)
+    arguments = (col_array, qkv, grad_attended, cosine, sine, query_gain, key_gain, levels)
+    dp, exp = lax.axis_size("dp"), lax.axis_size("exp")
+    tile = width // (dp * exp)
+
+    def weight_parts(lefts, right):
+        mine = lax.axis_index("exp")
+        if tile % 128 == 0:
+            return split_gradient(lefts, right, jnp.reshape(mine, (1,)).astype(jnp.int32), exp, dp)
+        (grads,) = weight_gradients(lefts, [right], bf16)
+        grads = grads.reshape(dp, exp, tile, -1).transpose(1, 0, 2, 3).reshape(exp, dp * tile, -1)
+        return [
+            lax.dynamic_index_in_dim(grads, lax.rem(mine + step, exp), 0, keepdims=False)
+            for step in range(exp)
+        ]
+
+    def exchange_parts(parts):
+        return [
+            lax.ppermute(part, "exp", [(i, (i + step) % exp) for i in range(exp)]) if step else part
+            for step, part in enumerate(parts)
+        ]
+
+    def sum_of(parts):
+        return sum(part.astype(f32) for part in parts).astype(bf16)
+
+    def swap_parts(sums):
+        parts = sums.reshape(dp, -1, sums.shape[1])
+        return lax.all_to_all(parts, "dp", 0, 0, tiled=True)
+
+    out_parts = exchange_parts(weight_parts(grad_sequence, attended))
     first_half = attention_backward(*arguments, 0, half)
-    first_half, running = after((first_half, running))
-    running = up(collect(output_back, 2, running))
+    first_half, running, out_parts = after((first_half, running, out_parts))
+    out_sums = sum_of(out_parts)
+    out_sums = swap_parts(after(out_sums, output_back[3]))
+    output_part = collect(output_back, 2, running)
+    running = up(output_part)
     *grad_qkv, grad_query_gain, grad_key_gain, _, _ = attention_backward(
-        *arguments, half, heads - half, first_half
+        *arguments, half, heads - half, after(first_half, output_part)
     )
     grad_query_gain, grad_key_gain = grad_query_gain[0], grad_key_gain[0]
 
+    grad_qkv, out_sums = after((grad_qkv, out_sums))
     *shares, attn_gain_sums = spread(grad_qkv, full_qkv, units)
-    up_rows, down_rows, up_rest, down_rest, own_share = shares
-    first_up, first_down = up(up_rows), down(down_rows)
+    send_up, send_down, free_up, free_down, up_rest, down_rest, own_share = shares
+    first_up, first_down = up(send_up), down(send_down)
     output_part = collect(after(output_back, attn_gain_sums), 3, running)
-    output_back[0] = swap(after(returned[0], output_back[3], attn_gain_sums))
     (grad_down,) = weight_gradients(
         after(acted_rows, attn_gain_sums), [cotangent_rows], f32, row_weights
     )
-    first_up, grad_down, output_part = after((first_up, grad_down, output_part))
-
-    second_up = up((up_rest + first_up[:middle].astype(f32)).astype(bf16))
+    output_back[0] = swap(after(returned[0], out_sums))
+    free_up, free_down = up(free_up), down(free_down)
+    qkv_parts = weight_parts(normed, after(grad_qkv, attn_gain_sums))
+    first_up, first_down, free_up, free_down, grad_down, output_part, qkv_parts = after(
+        (first_up, first_down, free_up, free_down, grad_down, output_part, qkv_parts)
+    )
+
+    second_up = up(scatter_second(up_rest, first_up))
+    second_down = down(scatter_second(down_rest, first_down))
     running = up(output_part)
-    dp, exp = lax.axis_size("dp"), lax.axis_size("exp")
-    tile = min(256, width // (dp * exp))
-    in_order = tile % 128 == 0
-    order = (lambda i: i % exp * dp + i // exp) if in_order else None
-
-    def weight_sums(lefts, right):
-        (grads,) = weight_gradients(lefts, [right], bf16, tile=tile if in_order else 256, order=order)
-        rows, wide = width // (dp * exp), grads.shape[1]
-        if not in_order:
-            grads = grads.reshape(dp, exp, rows, wide).transpose(1, 0, 2, 3)
-        grads = grads.reshape(exp, dp * rows, wide)
-        mine = lax.axis_index("exp")
-        total = lax.dynamic_index_in_dim(grads, mine, 0, keepdims=False).astype(f32)
-        for step in range(1, exp):
-            part = lax.dynamic_index_in_dim(grads, lax.rem(mine + step, exp), 0, keepdims=False)
-            part = lax.ppermute(part, "exp", [(i, (i + step) % exp) for i in range(exp)])
-            total = total + part.astype(f32)
-        return total.astype(bf16)
-
-    out_sums = weight_sums(after(grad_sequence, first_up), attended)
-    reduced_out = lax.psum_scatter(out_sums, "dp", scatter_dimension=0, tiled=True).astype(f32)
-    qkv_sums = weight_sums(normed, after(grad_qkv, out_sums))
-
+    reduced_out = jnp.sum(out_sums.astype(f32), axis=0)
+    qkv_sums = sum_of(exchange_parts(qkv_parts))
+
+    qkv_parts = swap_parts(after(qkv_sums, output_back[0]))
     small = jnp.concatenate([attn_gain_sums[0], grad_query_gain, grad_key_gain, grad_moe_gain])
     cuts = [0, width, width + head_size, width + 2 * head_size, 2 * (width + head_size)]
     small = jnp.concatenate([small, router_sums])
-    small = swap(after(jnp.broadcast_to(small, (peers, small.shape[0])), output_back[0]))
-    first_down, second_up, qkv_sums, small = after((first_down, second_up, qkv_sums, small))
-
-    second_down = down((down_rest + first_down[middle:].astype(f32)).astype(bf16))
-    qkv_parts = lax.all_to_all(
-        qkv_sums.reshape(dp, -1, qkv_sums.shape[1]), "dp", 0, 0, tiled=True
-    )
+    small = swap(after(jnp.broadcast_to(small, (peers, small.shape[0])), qkv_parts))
     reduced_qkv = jnp.sum(qkv_parts.astype(f32), axis=0)
     outputs = (hidden + collect(output_back, 0, running, f32)).astype(bf16)
     small = jnp.sum(small, axis=0)
@@ -892,7 +932,7 @@
     small = jnp.sum(small[:, : cuts[-1]], axis=0)
     shared = [small[i:j] for i, j in zip(cuts, cuts[1:])]
 
-    grad_normed = scatter_own(own_share, (first_up, first_down), (second_up, second_down))
+    grad_normed = scatter_own(own_share, second_up, second_down, free_up, free_down)
     input_rows = inputs.astype(f32)
     inverse_own = inverse_rms(input_rows)
     scaled_in = grad_normed * attn_gain

time: 953 us -> 922 us (0.967)
  waiting for transfers between devices: 290 us -> 270 us
  Pallas kernels: 332 us -> 314 us
  starting transfers between devices: 166 us -> 182 us
    ppermute x44 -> x48, waiting for transfers between devices: 209 us -> 183 us  [shifted(): lax.ppermute(block, 'col', [(i, (i + by) % columns) for i in range(column...]
    pallas_call x0 -> x2, Pallas kernels: none -> 22.7 us  [split_gradient(): pl.pallas_call(functools.partial(split_kernel, blocks, groups), out_shape...]
    pallas_call x4 -> x2, Pallas kernels: 68.1 us -> 46.4 us  [weight_gradients(): pl.pallas_call(functools.partial(weight_kernel, blocks, len(rights), weig...]
    all_to_all x17, waiting for transfers between devices: 30.5 us -> 42.9 us  [swap(): lax.all_to_all(rows.reshape(peers, rows.shape[0] // peers, *rows.shape[1:...]
    ppermute x44 -> x48, starting transfers between devices: 64.9 us -> 76.9 us  [shifted(): lax.ppermute(block, 'col', [(i, (i + by) % columns) for i in range(column...]
    pallas_call x2, Pallas kernels: 44.9 us -> 33.7 us  [attention_backward(): pl.pallas_call(functools.partial(backward_kernel, blocks, head_size ** (-...]
  transfers between devices with their start and end apart: 81 -> 85, of which waited for: 31 -> 37; matrix products, arithmetic and copies ran while one was open for 12% -> 12% of each run, Pallas kernels for 33% -> 34%
where the time goes in v3:
time: 922 us; the launch traced here: 910 us
  Pallas kernels  314 us (34%)
  waiting for transfers between devices  270 us (29%)
  starting transfers between devices  182 us (20%)
  other arithmetic  73.2 us (8%)
  local copies, waits for them, and re-layouts  29.3 us (3%)
  matrix products  26 us (3%)
  between operations  15.6 us (2%)
    ppermute x48, waiting for transfers between devices, shifted(): lax.ppermute(block, 'col', [(i, (i + by) % columns) for i in range(column...  183 us
    pallas_call x20, Pallas kernels, product(): pl.pallas_call(functools.partial(product_kernel, transposed), out_shape=j...  88.5 us
    pallas_call x4, Pallas kernels, expert_block(): pl.pallas_call(expert_kernel, out_shape=[shape((count, hidden), bf16), sh...  83.6 us
    ppermute x48, starting transfers between devices, shifted(): lax.ppermute(block, 'col', [(i, (i + by) % columns) for i in range(column...  76.9 us
    all_to_all x17, starting transfers between devices, swap(): lax.all_to_all(rows.reshape(peers, rows.shape[0] // peers, *rows.shape[1:...  75.8 us
    pallas_call x2, Pallas kernels, weight_gradients(): pl.pallas_call(functools.partial(weight_kernel, blocks, len(rights), weig...  46.4 us
    all_to_all x17, waiting for transfers between devices, swap(): lax.all_to_all(rows.reshape(peers, rows.shape[0] // peers, *rows.shape[1:...  42.9 us
    ppermute x14, waiting for transfers between devices, exchange_plane(): parts[step] = lax.ppermute(part, plane, pairs) if step else part  36.7 us
  transfers between devices with their start and end apart: 85, of which 37 were waited for; matrix products, arithmetic and copies ran while one was open for 12% of the time, Pallas kernels for 34%

profile of v3, /device:TPU:0, one launch (start us, length us, event | category | flops | bytes accessed | tf_op | source)
XLA Modules:
  0.0 910.0 jit_solution(4168882263923994872)
XLA Ops:
  41.1 21.0 %collective-permute-done.1 = bf16[256,2048]{1,0:T(8,128)(2,1)S(1)} collective-permute-done((bf16[256,2048]{1,0:T(8,128)(2,1)S(1)}, bf16[256,2048]{1,0:T(8,128)(2,1)S(1)}, u32[]{:S(2)}, u32[]{:S(2)}) %collective-permute-start.1) | collective-permute-done | bytes 1048608 | tf_op jit(solution)/shard_map/ppermute | solution.py:586
  104.4 20.2 %attention_forward.1 = (bf16[256,1024]{1,0:T(8,128)(2,1)}, bf16[256,1024]{1,0:T(8,128)(2,1)}, bf16[256,1024]{1,0:T(8,128)(2,1)}, bf16[256,1024]{1,0:T(8,128)(2,1)}, f32[8,1,1024]{2,1,0:T(1,128)}) custom-call(s32[1]{0:T(128)} %bitcast.4.col_ref, f32[256,1280]{1,0:T(8,128)} %fusion.50.refs_0_.refs_4_.refs_8_, f32[256,1280]{1,0:T(8,128)} %fusion.51.refs_1_.refs_5_.refs_9_, ...), custom_call_target="tpu_custom_call" | custom-call | flops 1000 | bytes 1000 | tf_op jit(solution)/shard_map/attention_forward/pallas_call | solution.py:124
  162.4 11.1 %collective-permute-done.10 = bf16[128,2048]{1,0:T(8,128)(2,1)S(1)} collective-permute-done((bf16[128,2048]{1,0:T(8,128)(2,1)}, bf16[128,2048]{1,0:T(8,128)(2,1)S(1)}, u32[]{:S(2)}, u32[]{:S(2)}) %collective-permute-start.10) | collective-permute-done | bytes 524320 | tf_op jit(solution)/shard_map/ppermute | solution.py:586
  173.5 10.8 %collective-permute-done.9 = bf16[128,2048]{1,0:T(8,128)(2,1)S(1)} collective-permute-done((bf16[128,2048]{1,0:T(8,128)(2,1)}, bf16[128,2048]{1,0:T(8,128)(2,1)S(1)}, u32[]{:S(2)}, u32[]{:S(2)}) %collective-permute-start.9) | collective-permute-done | bytes 524320 | tf_op jit(solution)/shard_map/ppermute | solution.py:586
  216.9 12.8 %collective-permute-done.12 = bf16[128,2048]{1,0:T(8,128)(2,1)S(1)} collective-permute-done((bf16[128,2048]{1,0:T(8,128)(2,1)}, bf16[128,2048]{1,0:T(8,128)(2,1)S(1)}, u32[]{:S(2)}, u32[]{:S(2)}) %collective-permute-start.12) | collective-permute-done | bytes 524320 | tf_op jit(solution)/shard_map/ppermute | solution.py:586
  244.6 11.0 %collective-permute-done.16 = bf16[128,2048]{1,0:T(8,128)(2,1)S(1)} collective-permute-done((bf16[128,2048]{1,0:T(8,128)(2,1)}, bf16[128,2048]{1,0:T(8,128)(2,1)S(1)}, u32[]{:S(2)}, u32[]{:S(2)}) %collective-permute-start.16) | collective-permute-done | bytes 524320 | tf_op jit(solution)/shard_map/ppermute | solution.py:586
  283.8 17.2 %collective-permute-done.17.right_ref = bf16[256,2048]{1,0:T(8,128)(2,1)} collective-permute-done((bf16[256,2048]{1,0:T(8,128)(2,1)}, bf16[256,2048]{1,0:T(8,128)(2,1)}, u32[]{:S(2)}, u32[]{:S(2)}) %collective-permute-start.17) | collective-permute-done | bytes 1048608 | tf_op jit(solution)/shard_map/ppermute | solution.py:586
  315.9 20.9 %expert_block.4 = (bf16[640,768]{1,0:T(8,128)(2,1)}, bf16[640,768]{1,0:T(8,128)(2,1)}, bf16[640,768]{1,0:T(8,128)(2,1)}, bf16[640,2048]{1,0:T(8,128)(2,1)}, bf16[640,2048]{1,0:T(8,128)(2,1)}, /*index=5*/f32[640,1]{1,0:T(8,128)}) custom-call(bf16[640,2048]{1,0:T(8,128)(2,1)} %bitcast.17.rows_ref.refs_0_, bf16[640,2048]{1,0:T(8,128)(2,1)} %bitcast.3.upstream_ref.refs_4_, ...), custom_call_target="tpu_custom_call" | custom-call | flops 1000 | bytes 1000 | tf_op jit(solution)/shard_map/expert_block/pallas_call | solution.py:519
  354.1 20.9 %expert_block.5 = (bf16[640,768]{1,0:T(8,128)(2,1)}, bf16[640,768]{1,0:T(8,128)(2,1)}, bf16[640,768]{1,0:T(8,128)(2,1)}, bf16[640,2048]{1,0:T(8,128)(2,1)}, bf16[640,2048]{1,0:T(8,128)(2,1)}, /*index=5*/f32[640,1]{1,0:T(8,128)}) custom-call(bf16[640,2048]{1,0:T(8,128)(2,1)} %bitcast.30.rows_ref.refs_1_, bf16[640,2048]{1,0:T(8,128)(2,1)} %bitcast.11.upstream_ref.refs_5_, ...), custom_call_target="tpu_custom_call" | custom-call | flops 1000 | bytes 1000 | tf_op jit(solution)/shard_map/expert_block/pallas_call | solution.py:519
  384.1 20.9 %expert_block.6 = (bf16[640,768]{1,0:T(8,128)(2,1)}, bf16[640,768]{1,0:T(8,128)(2,1)}, bf16[640,768]{1,0:T(8,128)(2,1)}, bf16[640,2048]{1,0:T(8,128)(2,1)}, bf16[640,2048]{1,0:T(8,128)(2,1)}, /*index=5*/f32[640,1]{1,0:T(8,128)}) custom-call(bf16[640,2048]{1,0:T(8,128)(2,1)} %bitcast.36.rows_ref.refs_2_, bf16[640,2048]{1,0:T(8,128)(2,1)} %bitcast.15.upstream_ref.refs_6_, ...), custom_call_target="tpu_custom_call" | custom-call | flops 1000 | bytes 1000 | tf_op jit(solution)/shard_map/expert_block/pallas_call | solution.py:519
  405.0 11.4 %all-to-all-done.7 = bf16[8,80,2048]{2,1,0:T(8,128)(2,1)} async-done(((bf16[8,80,2048]{2,1,0:T(8,128)(2,1)}), bf16[8,80,2048]{2,1,0:T(8,128)(2,1)}, u32[]{:S(2)}, u32[]{:S(2)}) %all-to-all-start.7) | async-done | bytes 2621472 | tf_op jit(solution)/shard_map/all_to_all | solution.py:613
  428.6 20.9 %expert_block.7 = (bf16[640,768]{1,0:T(8,128)(2,1)}, bf16[640,768]{1,0:T(8,128)(2,1)}, bf16[640,768]{1,0:T(8,128)(2,1)}, bf16[640,2048]{1,0:T(8,128)(2,1)}, bf16[640,2048]{1,0:T(8,128)(2,1)}, /*index=5*/f32[640,1]{1,0:T(8,128)}) custom-call(bf16[640,2048]{1,0:T(8,128)(2,1)} %bitcast.52.rows_ref.refs_3_, bf16[640,2048]{1,0:T(8,128)(2,1)} %bitcast.13.upstream_ref.refs_7_, ...), custom_call_target="tpu_custom_call" | custom-call | flops 1000 | bytes 1000 | tf_op jit(solution)/shard_map/expert_block/pallas_call | solution.py:519
  470.6 19.1 %collective-permute-done.31 = f32[4,80]{1,0:T(4,128)S(1)} collective-permute-done((f32[4,80]{1,0:T(4,128)S(1)}, f32[4,80]{1,0:T(4,128)S(1)}, u32[]{:S(2)}, u32[]{:S(2)}) %collective-permute-start.31) | collective-permute-done | bytes 1312 | tf_op jit(solution)/shard_map/ppermute | solution.py:628
  509.0 10.0 %collective-permute-done.35 = f32[4,80]{1,0:T(4,128)S(1)} collective-permute-done((f32[4,80]{1,0:T(4,128)S(1)}, f32[4,80]{1,0:T(4,128)S(1)}, u32[]{:S(2)}, u32[]{:S(2)}) %collective-permute-start.35) | collective-permute-done | bytes 1312 | tf_op jit(solution)/shard_map/ppermute | solution.py:628
  544.0 19.8 %collective-permute-done.40 = f32[8,80]{1,0:T(8,128)S(1)} collective-permute-done((f32[8,80]{1,0:T(8,128)S(1)}, f32[8,80]{1,0:T(8,128)S(1)}, u32[]{:S(2)}, u32[]{:S(2)}) %collective-permute-start.40) | collective-permute-done | bytes 2592 | tf_op jit(solution)/shard_map/ppermute | solution.py:586
  587.8 28.1 %weight_gradients.2 = (f32[2048,768]{1,0:T(8,128)}, f32[2048,768]{1,0:T(8,128)}) custom-call(bf16[640,2048]{1,0:T(8,128)(2,1)} %bitcast.17.rows_ref.refs_0_, bf16[640,2048]{1,0:T(8,128)(2,1)} %bitcast.30.rows_ref.refs_1_, bf16[640,2048]{1,0:T(8,128)(2,1)} %bitcast.36.rows_ref.refs_2_, bf16[640,2048]{1,0:T(8,128)(2,1)} %bitcast.52.rows_ref.refs_3_, ...), custom_call_target="tpu_custom_call" | custom-call | flops 1000 | bytes 1000 | tf_op jit(solution)/shard_map/weight_gradients/pallas_call | solution.py:324
  665.3 10.8 %split_gradient.2 = (bf16[1024,1024]{1,0:T(8,128)(2,1)}, bf16[1024,1024]{1,0:T(8,128)(2,1)}) custom-call(s32[1]{0:T(128)} %bitcast.107.mine_ref, bf16[256,2048]{1,0:T(8,128)(2,1)} %get-tuple-element.565.left_ref.refs_0_, bf16[256,2048]{1,0:T(8,128)(2,1)} %collective-permute-done.43.left_ref.refs_1_, bf16[256,2048]{1,0:T(8,128)(2,1)} %pad_maximum_fusion.3.left_ref.refs_2_, ...), custom_call_target="tpu_custom_call" | custom-call | flops 1000 | bytes 1000 | tf_op jit(solution)/shard_map/split_gradient/pallas_call | solution.py:365
  686.6 16.1 %attention_backward.2 = (bf16[256,1280]{1,0:T(8,128)(2,1)}, bf16[256,1280]{1,0:T(8,128)(2,1)}, bf16[256,1280]{1,0:T(8,128)(2,1)}, bf16[256,1280]{1,0:T(8,128)(2,...) custom-call(s32[1]{0:T(128)} %bitcast.4.col_ref, ...), custom_call_target="tpu_custom_call" | custom-call | flops 1000 | bytes 1000 | tf_op jit(solution)/shard_map/attention_backward/pallas_call | solution.py:254
  723.5 17.5 %attention_backward.3 = (bf16[256,1280]{1,0:T(8,128)(2,1)}, bf16[256,1280]{1,0:T(8,128)(2,1)}, bf16[256,1280]{1,0:T(8,128)(2,1)}, bf16[256,1280]{1,0:T(8,128)(2,...) custom-call(s32[1]{0:T(128)} %bitcast.4.col_ref, ...), custom_call_target="tpu_custom_call", output_to_operand_aliasing={{0}: (22, {}), {1}: (23, {}), {2}: (24, {}), {3}: (25, {})} | custom-call | flops 1000 | bytes 1000 | tf_op jit(solution)/shard_map/attention_backward/pallas_call | solution.py:254
  742.5 11.2 %spread.3 = (bf16[128,2048]{1,0:T(8,128)(2,1)}, bf16[128,2048]{1,0:T(8,128)(2,1)}, bf16[128,2048]{1,0:T(8,128)(2,1)}, bf16[128,2048]{1,0:T(8,128)(2,1)}, f32[128...) custom-call(bf16[256,1280]{1,0:T(8,128)(2,1)} %get-tuple-element.480.refs_0_.refs_4_, ...), custom_call_target="tpu_custom_call" | custom-call | flops 1000 | bytes 1000 | tf_op jit(solution)/shard_map/spread/pallas_call | solution.py:412
  761.5 11.9 %split_gradient.3 = (bf16[1024,1280]{1,0:T(8,128)(2,1)}, bf16[1024,1280]{1,0:T(8,128)(2,1)}) custom-call(s32[1]{0:T(128)} %bitcast.107.mine_ref, bf16[256,2048]{1,0:T(8,128)(2,1)} %get-tuple-element.578.refs_0_, bf16[256,2048]{1,0:T(8,128)(2,1)} %copy-done.11, bf16[256,2048]{1,0:T(8,128)(2,1)} %copy-done.9, bf16[256,2048]{1,0:T(8,128)(2,1)} %copy-done.10, ...), custom_call_target="tpu_custom_call" | custom-call | flops 1000 | bytes 1000 | tf_op jit(solution)/shard_map/split_gradient/pallas_call | solution.py:365
  773.4 18.3 %weight_gradients.3 = f32[768,2048]{1,0:T(8,128)} custom-call(bf16[640,768]{1,0:T(8,128)(2,1)} %get-tuple-element.475.refs_0_, bf16[640,768]{1,0:T(8,128)(2,1)} %get-tuple-element.476.refs_1_, bf16[640,768]{1,0:T(8,128)(2,1)} %get-tuple-element.477.refs_2_, bf16[640,768]{1,0:T(8,128)(2,1)} %get-tuple-element.478.refs_3_, ...), custom_call_target="tpu_custom_call" | custom-call | flops 1000 | bytes 1000 | tf_op jit(solution)/shard_map/weight_gradients/pallas_call | solution.py:324
  822.6 15.7 %all-to-all-done.16 = bf16[8,80,2048]{2,1,0:T(8,128)(2,1)} async-done(((bf16[8,80,2048]{2,1,0:T(8,128)(2,1)}), bf16[8,80,2048]{2,1,0:T(8,128)(2,1)}, u32[]{:S(2)}, u32[]{:S(2)}) %all-to-all-start.16) | async-done | bytes 2621472 | tf_op jit(solution)/shard_map/all_to_all | solution.py:613
  848.9 14.0 %collective-permute-done.57.refs_0_ = bf16[256,2048]{1,0:T(8,128)(2,1)} collective-permute-done((bf16[256,2048]{1,0:T(8,128)(2,1)}, bf16[256,2048]{1,0:T(8,128)(2,1)}, u32[]{:S(2)}, u32[]{:S(2)}) %collective-permute-start.57) | collective-permute-done | bytes 1048608 | tf_op jit(solution)/shard_map/ppermute | solution.py:586
  (441 shorter events, 502.5 us)
Async XLA Ops:
  7.2 54.9 %all-gather.3.cloned.1.call-start = ((), (), s32[]{:S(2)}) async-start(), calls=%async_computation.19 | async-start | bytes 7864320 | tf_op jit(solution)/shard_map/all_gather | solution.py:683
  15.0 47.1 %collective-permute-start.1 = (bf16[256,2048]{1,0:T(8,128)(2,1)S(1)}, bf16[256,2048]{1,0:T(8,128)(2,1)S(1)}, u32[]{:S(2)}, u32[]{:S(2)}) collective-permute-start(bf16[256,2048]{1,0:T(8,128)(2,1)S(1)} %copy-done.2), channel_id=1, source_target_pairs={{0,3},{1,0},{2,1},{3,2},{4,7},{5,4},{6,5},{7,6},{8,11},{9,8},{10,9... | collective-permute-start | bytes 3145736 | tf_op jit(solution)/shard_map/ppermute | solution.py:586
  22.7 66.1 %all-to-all-start = ((bf16[8,80,2048]{2,1,0:T(8,128)(2,1)}), bf16[8,80,2048]{2,1,0:T(8,128)(2,1)}, u32[]{:S(2)}, u32[]{:S(2)}) async-start(bf16[8,80,2048]{2,1,0:T(8,128)(2,1)} %bitcast.257), calls=%async_computation | async-start | bytes 5242880 | tf_op jit(solution)/shard_map/all_to_all | solution.py:613
  27.3 97.4 %all-gather.5.cloned.1.call-start = ((), (), s32[]{:S(2)}) async-start(), calls=%async_computation.20 | async-start | bytes 6291456 | tf_op jit(solution)/shard_map/all_gather | solution.py:684
  88.9 43.8 %collective-permute-start.6 = (s32[8,256]{1,0:T(8,128)S(1)}, s32[8,256]{1,0:T(8,128)S(1)}, u32[]{:S(2)}, u32[]{:S(2)}) collective-permute-start(s32[8,256]{1,0:T(8,128)S(1)} %bitcast.282), channel_id=1, source_target_pairs={{0,1},{1,2},{2,3},{3,0},{4,5},{5,6},{6,7},{7,4},{8,9},{9,10},{10,1... | collective-permute-start | bytes 24584 | tf_op jit(solution)/shard_map/ppermute | solution.py:586
  89.3 43.4 %collective-permute-start.7 = (s32[8,256]{1,0:T(8,128)S(1)}, s32[8,256]{1,0:T(8,128)S(1)}, u32[]{:S(2)}, u32[]{:S(2)}) collective-permute-start(s32[8,256]{1,0:T(8,128)S(1)} %bitcast.283), channel_id=1, source_target_pairs={{0,2},{1,3},{2,0},{3,1},{4,6},{5,7},{6,4},{7,5},{8,10},{9,11},{10,... | collective-permute-start | bytes 24584 | tf_op jit(solution)/shard_map/ppermute | solution.py:586
  91.6 41.1 %collective-permute-start.8 = (s32[8,256]{1,0:T(8,128)S(1)}, s32[8,256]{1,0:T(8,128)S(1)}, u32[]{:S(2)}, u32[]{:S(2)}) collective-permute-start(s32[8,256]{1,0:T(8,128)S(1)} %bitcast.284), channel_id=1, source_target_pairs={{0,3},{1,0},{2,1},{3,2},{4,7},{5,4},{6,5},{7,6},{8,11},{9,8},{10,9... | collective-permute-start | bytes 24584 | tf_op jit(solution)/shard_map/ppermute | solution.py:586
  92.8 41.7 %collective-permute-start.4 = (bf16[256,2048]{1,0:T(8,128)(2,1)S(1)}, bf16[256,2048]{1,0:T(8,128)(2,1)}, u32[]{:S(2)}, u32[]{:S(2)}) collective-permute-start(bf16[256,2048]{1,0:T(8,128)(2,1)S(1)} %copy-done.6), channel_id=1, source_target_pairs={{0,1},{1,2},{2,3},{3,0},{4,5},{5,6},{6,7},{7,4},{8,9},{9,10},{10,1... | collective-permute-start | bytes 3145736 | tf_op jit(solution)/shard_map/ppermute | solution.py:586
  93.6 46.7 %collective-permute-start.5 = (bf16[256,2048]{1,0:T(8,128)(2,1)S(1)}, bf16[256,2048]{1,0:T(8,128)(2,1)}, u32[]{:S(2)}, u32[]{:S(2)}) collective-permute-start(bf16[256,2048]{1,0:T(8,128)(2,1)S(1)} %copy-done.6), channel_id=1, source_target_pairs={{0,3},{1,0},{2,1},{3,2},{4,7},{5,4},{6,5},{7,6},{8,11},{9,8},{10,9... | collective-permute-start | bytes 3145736 | tf_op jit(solution)/shard_map/ppermute | solution.py:586
  140.2 44.1 %all-to-all-start.1 = ((bf16[8,80,2048]{2,1,0:T(8,128)(2,1)}), bf16[8,80,2048]{2,1,0:T(8,128)(2,1)}, u32[]{:S(2)}, u32[]{:S(2)}) async-start(bf16[8,80,2048]{2,1,0:T(8,128)(2,1)} %bitcast.260), calls=%async_computation.1 | async-start | bytes 5242880 | tf_op jit(solution)/shard_map/all_to_all | solution.py:613
  185.1 44.6 %all-to-all-start.2 = ((bf16[8,80,2048]{2,1,0:T(8,128)(2,1)}), bf16[8,80,2048]{2,1,0:T(8,128)(2,1)}, u32[]{:S(2)}, u32[]{:S(2)}) async-start(bf16[8,80,2048]{2,1,0:T(8,128)(2,1)} %bitcast.258), calls=%async_computation.2 | async-start | bytes 5242880 | tf_op jit(solution)/shard_map/all_to_all | solution.py:613
  342.4 37.0 %all-to-all-start.6 = ((bf16[8,80,2048]{2,1,0:T(8,128)(2,1)}), bf16[8,80,2048]{2,1,0:T(8,128)(2,1)}, u32[]{:S(2)}, u32[]{:S(2)}) async-start(bf16[8,80,2048]{2,1,0:T(8,128)(2,1)} %bitcast.256), calls=%async_computation.6 | async-start | bytes 5242880 | tf_op jit(solution)/shard_map/all_to_all | solution.py:613
  416.4 37.2 %all-to-all-start.8 = ((bf16[8,80,2048]{2,1,0:T(8,128)(2,1)}), bf16[8,80,2048]{2,1,0:T(8,128)(2,1)}, u32[]{:S(2)}, u32[]{:S(2)}) async-start(bf16[8,80,2048]{2,1,0:T(8,128)(2,1)} %bitcast.274), calls=%async_computation.8 | async-start | bytes 5242880 | tf_op jit(solution)/shard_map/all_to_all | solution.py:613
  527.0 37.5 %all-to-all-start.11 = ((bf16[8,80,2048]{2,1,0:T(8,128)(2,1)}), bf16[8,80,2048]{2,1,0:T(8,128)(2,1)}, u32[]{:S(2)}, u32[]{:S(2)}) async-start(bf16[8,80,2048]{2,1,0:T(8,128)(2,1)} %bitcast.271), calls=%async_computation.11 | async-start | bytes 5242880 | tf_op jit(solution)/shard_map/all_to_all | solution.py:613
  576.0 48.3 %collective-permute-start.43 = (bf16[256,2048]{1,0:T(8,128)(2,1)}, bf16[256,2048]{1,0:T(8,128)(2,1)}, u32[]{:S(2)}, u32[]{:S(2)}) collective-permute-start(bf16[256,2048]{1,0:T(8,128)(2,1)} %get-tuple-element.565.left_ref.refs_0_), channel_id=1, source_target_pairs={{0,1},{1,2},{2,3},{3,0},{4,5},{5,6},{6,7},{7,4},{8,9},{9,10},{10,1... | collective-permute-start | bytes 3145736 | tf_op jit(solution)/shard_map/ppermute | solution.py:586
  576.6 47.7 %collective-permute-start.44 = (bf16[256,2048]{1,0:T(8,128)(2,1)}, bf16[256,2048]{1,0:T(8,128)(2,1)}, u32[]{:S(2)}, u32[]{:S(2)}) collective-permute-start(bf16[256,2048]{1,0:T(8,128)(2,1)} %get-tuple-element.565.left_ref.refs_0_), channel_id=1, source_target_pairs={{0,3},{1,0},{2,1},{3,2},{4,7},{5,4},{6,5},{7,6},{8,11},{9,8},{10,9... | collective-permute-start | bytes 3145736 | tf_op jit(solution)/shard_map/ppermute | solution.py:586
  583.4 51.1 %all-to-all-start.12 = ((bf16[8,80,2048]{2,1,0:T(8,128)(2,1)}), bf16[8,80,2048]{2,1,0:T(8,128)(2,1)}, u32[]{:S(2)}, u32[]{:S(2)}) async-start(bf16[8,80,2048]{2,1,0:T(8,128)(2,1)} %bitcast.270), calls=%async_computation.12 | async-start | bytes 5242880 | tf_op jit(solution)/shard_map/all_to_all | solution.py:613
  634.5 41.6 %all-to-all-start.13 = ((bf16[8,80,2048]{2,1,0:T(8,128)(2,1)}), bf16[8,80,2048]{2,1,0:T(8,128)(2,1)}, u32[]{:S(2)}, u32[]{:S(2)}) async-start(bf16[8,80,2048]{2,1,0:T(8,128)(2,1)} %bitcast.268), calls=%async_computation.13 | async-start | bytes 5242880 | tf_op jit(solution)/shard_map/all_to_all | solution.py:613
  722.2 69.6 %collective-permute-start.56 = (bf16[256,2048]{1,0:T(8,128)(2,1)}, bf16[256,2048]{1,0:T(8,128)(2,1)}, u32[]{:S(2)}, u32[]{:S(2)}) collective-permute-start(bf16[256,2048]{1,0:T(8,128)(2,1)} %product.37), channel_id=1, source_target_pairs={{0,1},{1,2},{2,3},{3,0},{4,5},{5,6},{6,7},{7,4},{8,9},{9,10},{10,1... | collective-permute-start | bytes 3145736 | tf_op jit(solution)/shard_map/ppermute | solution.py:586
  753.7 42.8 %collective-permute-start.52 = (bf16[128,2048]{1,0:T(8,128)(2,1)}, bf16[128,2048]{1,0:T(8,128)(2,1)}, u32[]{:S(2)}, u32[]{:S(2)}) collective-permute-start(bf16[128,2048]{1,0:T(8,128)(2,1)} %get-tuple-element.466), channel_id=1, source_target_pairs={{0,1},{1,2},{2,3},{3,0},{4,5},{5,6},{6,7},{7,4},{8,9},{9,10},{10,1... | collective-permute-start | bytes 1572872 | tf_op jit(solution)/shard_map/ppermute | solution.py:586
  754.3 42.2 %collective-permute-start.53 = (bf16[128,2048]{1,0:T(8,128)(2,1)}, bf16[128,2048]{1,0:T(8,128)(2,1)}, u32[]{:S(2)}, u32[]{:S(2)}) collective-permute-start(bf16[128,2048]{1,0:T(8,128)(2,1)} %get-tuple-element.467), channel_id=1, source_target_pairs={{0,3},{1,0},{2,1},{3,2},{4,7},{5,4},{6,5},{7,6},{8,11},{9,8},{10,9... | collective-permute-start | bytes 1572872 | tf_op jit(solution)/shard_map/ppermute | solution.py:586
  757.5 38.9 %collective-permute-start.54 = (bf16[128,2048]{1,0:T(8,128)(2,1)}, bf16[128,2048]{1,0:T(8,128)(2,1)}, u32[]{:S(2)}, u32[]{:S(2)}) collective-permute-start(bf16[128,2048]{1,0:T(8,128)(2,1)} %get-tuple-element.468), channel_id=1, source_target_pairs={{0,1},{1,2},{2,3},{3,0},{4,5},{5,6},{6,7},{7,4},{8,9},{9,10},{10,1... | collective-permute-start | bytes 1572872 | tf_op jit(solution)/shard_map/ppermute | solution.py:586
  757.6 43.1 %collective-permute-start.55 = (bf16[128,2048]{1,0:T(8,128)(2,1)}, bf16[128,2048]{1,0:T(8,128)(2,1)}, u32[]{:S(2)}, u32[]{:S(2)}) collective-permute-start(bf16[128,2048]{1,0:T(8,128)(2,1)} %get-tuple-element.469), channel_id=1, source_target_pairs={{0,3},{1,0},{2,1},{3,2},{4,7},{5,4},{6,5},{7,6},{8,11},{9,8},{10,9... | collective-permute-start | bytes 1572872 | tf_op jit(solution)/shard_map/ppermute | solution.py:586
  818.6 44.3 %collective-permute-start.57 = (bf16[256,2048]{1,0:T(8,128)(2,1)}, bf16[256,2048]{1,0:T(8,128)(2,1)}, u32[]{:S(2)}, u32[]{:S(2)}) collective-permute-start(bf16[256,2048]{1,0:T(8,128)(2,1)} %product.38), channel_id=1, source_target_pairs={{0,1},{1,2},{2,3},{3,0},{4,5},{5,6},{6,7},{7,4},{8,9},{9,10},{10,1... | collective-permute-start | bytes 3145736 | tf_op jit(solution)/shard_map/ppermute | solution.py:586
  (97 other events, 2339.4 us)
Sparse Core Ops, SparseCore 0:
  10.9 18.3 all-gather.2
  30.9 14.8 all-gather.4

commit v4 on v3

--- a/solution.py
+++ b/solution.py
@@ -711,16 +711,17 @@
     shares = spread(attended, full_out)
     ids_blocks = after(ids_blocks, attended)
     slot_mats += [slot_mat(ids_blocks[s]) for s in (1, 2, 3)]
-    picked = pick(1, after(near_cotangent[0], attended))
-    near_cotangent, shares, slot_mats, picked = after((near_cotangent, shares, slot_mats, picked))
+    first_rows = after(near_cotangent[0], attended)
+    picked = pick(1, first_rows)
+    late_cotangent, slot_mats = after((near_cotangent[1], slot_mats), shares)
 
     send_up, send_down, free_up, free_down, up_rest, down_rest, own_share = shares
     cotangent_rows[1] = swap(picked)
     first_up, first_down = up(send_up), down(send_down)
-    far_up = up(near_cotangent[0][:middle])
+    far_up = up(first_rows[:middle])
     chosen_all, slots_all = slots_of(own_ids, all_experts)
-    picked = pick(3, near_cotangent[1])
-    late_half = near_cotangent[1][middle:]
+    picked = pick(3, late_cotangent)
+    late_half = late_cotangent[middle:]
     first_up, first_down, far_up, cotangent_rows[1], chosen_all, slots_all, picked, late_half, frees = after(
         (
             first_up, first_down, far_up, cotangent_rows[1], chosen_all, slots_all, picked, late_half,
@@ -844,12 +845,7 @@
     grad_attended.update({1: product(near_gradient[0], full_out), 3: product(near_gradient[1], full_out)})
     output_part = collect(output_back, 1)
     far_gradient = jnp.concatenate(after(far_gradient, output_part), axis=0)
-    router_sums = grad_router.reshape(1, columns, width // columns * experts)
-    router_sums = jnp.take(after(router_sums, near_gradient), to_ring, axis=1)
-    router_sums = jnp.sum(exchange_columns(router_sums)[0], axis=0)
-    far_gradient, grad_attended, output_part, router_sums = after(
-        (far_gradient, grad_attended, output_part, router_sums)
-    )
+    far_gradient, grad_attended, output_part = after((far_gradient, grad_attended, output_part))
 
     grad_sequence = [grad_low, near_gradient[0], far_gradient, near_gradient[1]]
     running = up(output_part)
@@ -887,10 +883,14 @@
 
     out_parts = exchange_parts(weight_parts(grad_sequence, attended))
     first_half = attention_backward(*arguments, 0, half)
-    first_half, running, out_parts = after((first_half, running, out_parts))
+    first_half, out_parts = after((first_half, out_parts))
     out_sums = sum_of(out_parts)
+    running = after(running, out_sums)
     out_sums = swap_parts(after(out_sums, output_back[3]))
     output_part = collect(output_back, 2, running)
+    router_sums = grad_router.reshape(1, columns, width // columns * experts)
+    router_sums = jnp.take(after(router_sums, running), to_ring, axis=1)
+    router_sums = jnp.sum(exchange_columns(router_sums)[0], axis=0)
     running = up(output_part)
     *grad_qkv, grad_query_gain, grad_key_gain, _, _ = attention_backward(
         *arguments, half, heads - half, after(first_half, output_part)
@@ -908,8 +908,8 @@
     output_back[0] = swap(after(returned[0], out_sums))
     free_up, free_down = up(free_up), down(free_down)
     qkv_parts = weight_parts(normed, after(grad_qkv, attn_gain_sums))
-    first_up, first_down, free_up, free_down, grad_down, output_part, qkv_parts = after(
-        (first_up, first_down, free_up, free_down, grad_down, output_part, qkv_parts)
+    first_up, first_down, free_up, free_down, grad_down, output_part, qkv_parts, output_back[0] = after(
+        (first_up, first_down, free_up, free_down, grad_down, output_part, qkv_parts, output_back[0])
     )
 
     second_up = up(scatter_second(up_rest, first_up))

time: 922 us -> 973 us (1.055)
  waiting for transfers between devices: 270 us -> 336 us
  starting transfers between devices: 182 us -> 167 us
    ppermute x48, waiting for transfers between devices: 183 us -> 241 us  [shifted(): lax.ppermute(block, 'col', [(i, (i + by) % columns) for i in range(column...]
    all_to_all x17, waiting for transfers between devices: 42.9 us -> 56.7 us  [swap(): lax.all_to_all(rows.reshape(peers, rows.shape[0] // peers, *rows.shape[1:...]
    ppermute x48, starting transfers between devices: 76.9 us -> 64.1 us  [shifted(): lax.ppermute(block, 'col', [(i, (i + by) % columns) for i in range(column...]
  transfers between devices with their start and end apart: 85 -> 85, of which waited for: 37 -> 41; matrix products, arithmetic and copies ran while one was open for 12% -> 12% of each run, Pallas kernels for 34% -> 33%
where the time goes in v4:
time: 973 us; the launch traced here: 961 us
  waiting for transfers between devices  336 us (35%)
  Pallas kernels  314 us (32%)
  starting transfers between devices  167 us (17%)
  other arithmetic  70.4 us (7%)
  matrix products  28.5 us (3%)
  local copies, waits for them, and re-layouts  28.3 us (3%)
  between operations  15.9 us (2%)
    ppermute x48, waiting for transfers between devices, shifted(): lax.ppermute(block, 'col', [(i, (i + by) % columns) for i in range(column...  241 us
    pallas_call x20, Pallas kernels, product(): pl.pallas_call(functools.partial(product_kernel, transposed), out_shape=j...  88.5 us
    pallas_call x4, Pallas kernels, expert_block(): pl.pallas_call(expert_kernel, out_shape=[shape((count, hidden), bf16), sh...  83.6 us
    all_to_all x17, starting transfers between devices, swap(): lax.all_to_all(rows.reshape(peers, rows.shape[0] // peers, *rows.shape[1:...  76.8 us
    ppermute x48, starting transfers between devices, shifted(): lax.ppermute(block, 'col', [(i, (i + by) % columns) for i in range(column...  64.1 us
    all_to_all x17, waiting for transfers between devices, swap(): lax.all_to_all(rows.reshape(peers, rows.shape[0] // peers, *rows.shape[1:...  56.7 us
    pallas_call x2, Pallas kernels, weight_gradients(): pl.pallas_call(functools.partial(weight_kernel, blocks, len(rights), weig...  46.4 us
    ppermute x14, waiting for transfers between devices, exchange_plane(): parts[step] = lax.ppermute(part, plane, pairs) if step else part  37.7 us
  transfers between devices with their start and end apart: 85, of which 41 were waited for; matrix products, arithmetic and copies ran while one was open for 12% of the time, Pallas kernels for 33%

profile of v4, /device:TPU:0, one launch (start us, length us, event | category | flops | bytes accessed | tf_op | source)
XLA Modules:
  0.0 961.4 jit_solution(10632030085044697410)
XLA Ops:
  40.6 22.2 %collective-permute-done = bf16[256,2048]{1,0:T(8,128)(2,1)S(1)} collective-permute-done((bf16[256,2048]{1,0:T(8,128)(2,1)S(1)}, bf16[256,2048]{1,0:T(8,128)(2,1)S(1)}, u32[]{:S(2)}, u32[]{:S(2)}) %collective-permute-start) | collective-permute-done | bytes 1048608 | tf_op jit(solution)/shard_map/ppermute | solution.py:586
  101.4 20.2 %attention_forward.1 = (bf16[256,1024]{1,0:T(8,128)(2,1)}, bf16[256,1024]{1,0:T(8,128)(2,1)}, bf16[256,1024]{1,0:T(8,128)(2,1)}, bf16[256,1024]{1,0:T(8,128)(2,1)}, f32[8,1,1024]{2,1,0:T(1,128)}) custom-call(s32[1]{0:T(128)} %bitcast.col_ref, f32[256,1280]{1,0:T(8,128)} %fusion.50.refs_0_.refs_4_.refs_8_, f32[256,1280]{1,0:T(8,128)} %fusion.51.refs_1_.refs_5_.refs_9_, ...), custom_call_target="tpu_custom_call" | custom-call | flops 1000 | bytes 1000 | tf_op jit(solution)/shard_map/attention_forward/pallas_call | solution.py:124
  180.7 11.7 %collective-permute-done.7 = bf16[128,2048]{1,0:T(8,128)(2,1)} collective-permute-done((bf16[128,2048]{1,0:T(8,128)(2,1)S(1)}, bf16[128,2048]{1,0:T(8,128)(2,1)}, u32[]{:S(2)}, u32[]{:S(2)}) %collective-permute-start.7) | collective-permute-done | bytes 524320 | tf_op jit(solution)/shard_map/ppermute | solution.py:586
  290.4 17.7 %collective-permute-done.17.right_ref = bf16[256,2048]{1,0:T(8,128)(2,1)} collective-permute-done((bf16[256,2048]{1,0:T(8,128)(2,1)}, bf16[256,2048]{1,0:T(8,128)(2,1)}, u32[]{:S(2)}, u32[]{:S(2)}) %collective-permute-start.17) | collective-permute-done | bytes 1048608 | tf_op jit(solution)/shard_map/ppermute | solution.py:586
  322.0 21.0 %expert_block.4 = (bf16[640,768]{1,0:T(8,128)(2,1)}, bf16[640,768]{1,0:T(8,128)(2,1)}, bf16[640,768]{1,0:T(8,128)(2,1)}, bf16[640,2048]{1,0:T(8,128)(2,1)}, bf16[640,2048]{1,0:T(8,128)(2,1)}, /*index=5*/f32[640,1]{1,0:T(8,128)}) custom-call(bf16[640,2048]{1,0:T(8,128)(2,1)} %bitcast.17.rows_ref.refs_0_, bf16[640,2048]{1,0:T(8,128)(2,1)} %bitcast.4.upstream_ref.refs_4_, ...), custom_call_target="tpu_custom_call" | custom-call | flops 1000 | bytes 1000 | tf_op jit(solution)/shard_map/expert_block/pallas_call | solution.py:519
  359.2 20.8 %expert_block.5 = (bf16[640,768]{1,0:T(8,128)(2,1)}, bf16[640,768]{1,0:T(8,128)(2,1)}, bf16[640,768]{1,0:T(8,128)(2,1)}, bf16[640,2048]{1,0:T(8,128)(2,1)}, bf16[640,2048]{1,0:T(8,128)(2,1)}, /*index=5*/f32[640,1]{1,0:T(8,128)}) custom-call(bf16[640,2048]{1,0:T(8,128)(2,1)} %bitcast.30.rows_ref.refs_1_, bf16[640,2048]{1,0:T(8,128)(2,1)} %bitcast.9.upstream_ref.refs_5_, ...), custom_call_target="tpu_custom_call" | custom-call | flops 1000 | bytes 1000 | tf_op jit(solution)/shard_map/expert_block/pallas_call | solution.py:519
  390.5 20.9 %expert_block.6 = (bf16[640,768]{1,0:T(8,128)(2,1)}, bf16[640,768]{1,0:T(8,128)(2,1)}, bf16[640,768]{1,0:T(8,128)(2,1)}, bf16[640,2048]{1,0:T(8,128)(2,1)}, bf16[640,2048]{1,0:T(8,128)(2,1)}, /*index=5*/f32[640,1]{1,0:T(8,128)}) custom-call(bf16[640,2048]{1,0:T(8,128)(2,1)} %bitcast.36.rows_ref.refs_2_, bf16[640,2048]{1,0:T(8,128)(2,1)} %bitcast.15.upstream_ref.refs_6_, ...), custom_call_target="tpu_custom_call" | custom-call | flops 1000 | bytes 1000 | tf_op jit(solution)/shard_map/expert_block/pallas_call | solution.py:519
  411.4 11.4 %all-to-all-done.7 = bf16[8,80,2048]{2,1,0:T(8,128)(2,1)} async-done(((bf16[8,80,2048]{2,1,0:T(8,128)(2,1)}), bf16[8,80,2048]{2,1,0:T(8,128)(2,1)}, u32[]{:S(2)}, u32[]{:S(2)}) %all-to-all-start.7) | async-done | bytes 2621472 | tf_op jit(solution)/shard_map/all_to_all | solution.py:613
  434.8 20.9 %expert_block.7 = (bf16[640,768]{1,0:T(8,128)(2,1)}, bf16[640,768]{1,0:T(8,128)(2,1)}, bf16[640,768]{1,0:T(8,128)(2,1)}, bf16[640,2048]{1,0:T(8,128)(2,1)}, bf16[640,2048]{1,0:T(8,128)(2,1)}, /*index=5*/f32[640,1]{1,0:T(8,128)}) custom-call(bf16[640,2048]{1,0:T(8,128)(2,1)} %bitcast.52.rows_ref.refs_3_, bf16[640,2048]{1,0:T(8,128)(2,1)} %bitcast.13.upstream_ref.refs_7_, ...), custom_call_target="tpu_custom_call" | custom-call | flops 1000 | bytes 1000 | tf_op jit(solution)/shard_map/expert_block/pallas_call | solution.py:519
  476.3 20.2 %collective-permute-done.32 = f32[4,80]{1,0:T(4,128)S(1)} collective-permute-done((f32[4,80]{1,0:T(4,128)S(1)}, f32[4,80]{1,0:T(4,128)S(1)}, u32[]{:S(2)}, u32[]{:S(2)}) %collective-permute-start.32) | collective-permute-done | bytes 1312 | tf_op jit(solution)/shard_map/ppermute | solution.py:628
  514.7 17.5 %collective-permute-done.37 = f32[4,80]{1,0:T(4,128)S(1)} collective-permute-done((f32[4,80]{1,0:T(4,128)S(1)}, f32[4,80]{1,0:T(4,128)S(1)}, u32[]{:S(2)}, u32[]{:S(2)}) %collective-permute-start.37) | collective-permute-done | bytes 1312 | tf_op jit(solution)/shard_map/ppermute | solution.py:628
  547.7 22.3 %collective-permute-done.40 = f32[8,80]{1,0:T(8,128)S(1)} collective-permute-done((f32[8,80]{1,0:T(8,128)S(1)}, f32[8,80]{1,0:T(8,128)S(1)}, u32[]{:S(2)}, u32[]{:S(2)}) %collective-permute-start.40) | collective-permute-done | bytes 2592 | tf_op jit(solution)/shard_map/ppermute | solution.py:586
  587.1 20.8 %all-to-all-done.12 = bf16[8,80,2048]{2,1,0:T(8,128)(2,1)} async-done(((bf16[8,80,2048]{2,1,0:T(8,128)(2,1)}), bf16[8,80,2048]{2,1,0:T(8,128)(2,1)}, u32[]{:S(2)}, u32[]{:S(2)}) %all-to-all-start.12) | async-done | bytes 2621472 | tf_op jit(solution)/shard_map/all_to_all | solution.py:613
  618.0 28.1 %weight_gradients.2 = (f32[2048,768]{1,0:T(8,128)}, f32[2048,768]{1,0:T(8,128)}) custom-call(bf16[640,2048]{1,0:T(8,128)(2,1)} %bitcast.17.rows_ref.refs_0_, bf16[640,2048]{1,0:T(8,128)(2,1)} %bitcast.30.rows_ref.refs_1_, bf16[640,2048]{1,0:T(8,128)(2,1)} %bitcast.36.rows_ref.refs_2_, bf16[640,2048]{1,0:T(8,128)(2,1)} %bitcast.52.rows_ref.refs_3_, ...), custom_call_target="tpu_custom_call" | custom-call | flops 1000 | bytes 1000 | tf_op jit(solution)/shard_map/weight_gradients/pallas_call | solution.py:324
  650.1 10.5 %collective-permute-done.43.left_ref.refs_1_ = bf16[256,2048]{1,0:T(8,128)(2,1)} collective-permute-done((bf16[256,2048]{1,0:T(8,128)(2,1)}, bf16[256,2048]{1,0:T(8,128)(2,1)}, u32[]{:S(2)}, u32[]{:S(2)}) %collective-permute-start.43) | collective-permute-done | bytes 1048608 | tf_op jit(solution)/shard_map/ppermute | solution.py:586
  678.1 11.7 %collective-permute-done.45 = bf16[128,2048]{1,0:T(8,128)(2,1)} collective-permute-done((bf16[128,2048]{1,0:T(8,128)(2,1)S(1)}, bf16[128,2048]{1,0:T(8,128)(2,1)}, u32[]{:S(2)}, u32[]{:S(2)}) %collective-permute-start.45) | collective-permute-done | bytes 524320 | tf_op jit(solution)/shard_map/ppermute | solution.py:586
  692.1 10.8 %split_gradient.2 = (bf16[1024,1024]{1,0:T(8,128)(2,1)}, bf16[1024,1024]{1,0:T(8,128)(2,1)}) custom-call(s32[1]{0:T(128)} %bitcast.97.mine_ref, bf16[256,2048]{1,0:T(8,128)(2,1)} %get-tuple-element.547.left_ref.refs_0_, bf16[256,2048]{1,0:T(8,128)(2,1)} %collective-permute-done.43.left_ref.refs_1_, bf16[256,2048]{1,0:T(8,128)(2,1)} %pad_maximum_fusion.3.left_ref.refs_2_, ...), custom_call_target="tpu_custom_call" | custom-call | flops 1000 | bytes 1000 | tf_op jit(solution)/shard_map/split_gradient/pallas_call | solution.py:365
  711.5 16.2 %attention_backward.2 = (bf16[256,1280]{1,0:T(8,128)(2,1)}, bf16[256,1280]{1,0:T(8,128)(2,1)}, bf16[256,1280]{1,0:T(8,128)(2,1)}, bf16[256,1280]{1,0:T(8,128)(2,...) custom-call(s32[1]{0:T(128)} %bitcast.col_ref, ...), custom_call_target="tpu_custom_call" | custom-call | flops 1000 | bytes 1000 | tf_op jit(solution)/shard_map/attention_backward/pallas_call | solution.py:254
  749.4 19.1 %collective-permute-done.48.refs_0_ = bf16[256,2048]{1,0:T(8,128)(2,1)} collective-permute-done((bf16[256,2048]{1,0:T(8,128)(2,1)}, bf16[256,2048]{1,0:T(8,128)(2,1)}, u32[]{:S(2)}, u32[]{:S(2)}) %collective-permute-start.48) | collective-permute-done | bytes 1048608 | tf_op jit(solution)/shard_map/ppermute | solution.py:586
  774.7 17.5 %attention_backward.3 = (bf16[256,1280]{1,0:T(8,128)(2,1)}, bf16[256,1280]{1,0:T(8,128)(2,1)}, bf16[256,1280]{1,0:T(8,128)(2,1)}, bf16[256,1280]{1,0:T(8,128)(2,...) custom-call(s32[1]{0:T(128)} %bitcast.col_ref, ...), custom_call_target="tpu_custom_call", output_to_operand_aliasing={{0}: (22, {}), {1}: (23, {}), {2}: (24, {}), {3}: (25, {})} | custom-call | flops 1000 | bytes 1000 | tf_op jit(solution)/shard_map/attention_backward/pallas_call | solution.py:254
  797.3 11.2 %spread.3 = (bf16[128,2048]{1,0:T(8,128)(2,1)}, bf16[128,2048]{1,0:T(8,128)(2,1)}, bf16[128,2048]{1,0:T(8,128)(2,1)}, bf16[128,2048]{1,0:T(8,128)(2,1)}, f32[128...) custom-call(bf16[256,1280]{1,0:T(8,128)(2,1)} %get-tuple-element.458.refs_0_.refs_4_, ...), custom_call_target="tpu_custom_call" | custom-call | flops 1000 | bytes 1000 | tf_op jit(solution)/shard_map/spread/pallas_call | solution.py:412
  816.4 12.0 %split_gradient.3 = (bf16[1024,1280]{1,0:T(8,128)(2,1)}, bf16[1024,1280]{1,0:T(8,128)(2,1)}) custom-call(s32[1]{0:T(128)} %bitcast.97.mine_ref, bf16[256,2048]{1,0:T(8,128)(2,1)} %get-tuple-element.560.refs_0_, bf16[256,2048]{1,0:T(8,128)(2,1)} %copy-done.11, bf16[256,2048]{1,0:T(8,128)(2,1)} %copy-done.9, bf16[256,2048]{1,0:T(8,128)(2,1)} %copy-done.10, ...), custom_call_target="tpu_custom_call" | custom-call | flops 1000 | bytes 1000 | tf_op jit(solution)/shard_map/split_gradient/pallas_call | solution.py:365
  828.4 18.3 %weight_gradients.3 = f32[768,2048]{1,0:T(8,128)} custom-call(bf16[640,768]{1,0:T(8,128)(2,1)} %get-tuple-element.453.refs_0_, bf16[640,768]{1,0:T(8,128)(2,1)} %get-tuple-element.454.refs_1_, bf16[640,768]{1,0:T(8,128)(2,1)} %get-tuple-element.455.refs_2_, bf16[640,768]{1,0:T(8,128)(2,1)} %get-tuple-element.456.refs_3_, ...), custom_call_target="tpu_custom_call" | custom-call | flops 1000 | bytes 1000 | tf_op jit(solution)/shard_map/weight_gradients/pallas_call | solution.py:324
  902.9 17.1 %collective-permute-done.54.refs_0_ = bf16[256,2048]{1,0:T(8,128)(2,1)} collective-permute-done((bf16[256,2048]{1,0:T(8,128)(2,1)}, bf16[256,2048]{1,0:T(8,128)(2,1)}, u32[]{:S(2)}, u32[]{:S(2)}) %collective-permute-start.54) | collective-permute-done | bytes 1048608 | tf_op jit(solution)/shard_map/ppermute | solution.py:586
  (436 shorter events, 525.5 us)
Async XLA Ops:
  7.2 55.6 %all-gather.3.cloned.1.call-start = ((), (), s32[]{:S(2)}) async-start(), calls=%async_computation.19 | async-start | bytes 7864320 | tf_op jit(solution)/shard_map/all_gather | solution.py:683
  17.0 45.8 %collective-permute-start = (bf16[256,2048]{1,0:T(8,128)(2,1)S(1)}, bf16[256,2048]{1,0:T(8,128)(2,1)S(1)}, u32[]{:S(2)}, u32[]{:S(2)}) collective-permute-start(bf16[256,2048]{1,0:T(8,128)(2,1)S(1)} %copy-done.2), channel_id=1, source_target_pairs={{0,1},{1,2},{2,3},{3,0},{4,5},{5,6},{6,7},{7,4},{8,9},{9,10},{10,1... | collective-permute-start | bytes 3145736 | tf_op jit(solution)/shard_map/ppermute | solution.py:586
  22.7 65.1 %all-to-all-start = ((bf16[8,80,2048]{2,1,0:T(8,128)(2,1)}), bf16[8,80,2048]{2,1,0:T(8,128)(2,1)}, u32[]{:S(2)}, u32[]{:S(2)}) async-start(bf16[8,80,2048]{2,1,0:T(8,128)(2,1)} %bitcast.257), calls=%async_computation | async-start | bytes 5242880 | tf_op jit(solution)/shard_map/all_to_all | solution.py:613
  27.2 107.3 %all-gather.5.cloned.1.call-start = ((), (), s32[]{:S(2)}) async-start(), calls=%async_computation.20 | async-start | bytes 6291456 | tf_op jit(solution)/shard_map/all_gather | solution.py:684
  127.8 64.5 %all-to-all-start.1 = ((bf16[8,80,2048]{2,1,0:T(8,128)(2,1)}), bf16[8,80,2048]{2,1,0:T(8,128)(2,1)}, u32[]{:S(2)}, u32[]{:S(2)}) async-start(bf16[8,80,2048]{2,1,0:T(8,128)(2,1)} %bitcast.258), calls=%async_computation.1 | async-start | bytes 5242880 | tf_op jit(solution)/shard_map/all_to_all | solution.py:613
  142.5 38.2 %collective-permute-start.5 = (bf16[128,2048]{1,0:T(8,128)(2,1)}, bf16[128,2048]{1,0:T(8,128)(2,1)}, u32[]{:S(2)}, u32[]{:S(2)}) collective-permute-start(bf16[128,2048]{1,0:T(8,128)(2,1)} %get-tuple-element.264), channel_id=1, source_target_pairs={{0,3},{1,0},{2,1},{3,2},{4,7},{5,4},{6,5},{7,6},{8,11},{9,8},{10,9... | collective-permute-start | bytes 1572872 | tf_op jit(solution)/shard_map/ppermute | solution.py:586
  147.4 44.9 %collective-permute-start.7 = (bf16[128,2048]{1,0:T(8,128)(2,1)S(1)}, bf16[128,2048]{1,0:T(8,128)(2,1)}, u32[]{:S(2)}, u32[]{:S(2)}) collective-permute-start(bf16[128,2048]{1,0:T(8,128)(2,1)S(1)} %slice.104), channel_id=1, source_target_pairs={{0,1},{1,2},{2,3},{3,0},{4,5},{5,6},{6,7},{7,4},{8,9},{9,10},{10,1... | collective-permute-start | bytes 1572872 | tf_op jit(solution)/shard_map/ppermute | solution.py:586
  192.4 42.0 %all-to-all-start.2 = ((bf16[8,80,2048]{2,1,0:T(8,128)(2,1)}), bf16[8,80,2048]{2,1,0:T(8,128)(2,1)}, u32[]{:S(2)}, u32[]{:S(2)}) async-start(bf16[8,80,2048]{2,1,0:T(8,128)(2,1)} %bitcast.259), calls=%async_computation.2 | async-start | bytes 5242880 | tf_op jit(solution)/shard_map/all_to_all | solution.py:613
  275.4 37.0 %all-to-all-start.4 = ((bf16[8,80,2048]{2,1,0:T(8,128)(2,1)}), bf16[8,80,2048]{2,1,0:T(8,128)(2,1)}, u32[]{:S(2)}, u32[]{:S(2)}) async-start(bf16[8,80,2048]{2,1,0:T(8,128)(2,1)} %bitcast.254), calls=%async_computation.4 | async-start | bytes 5242880 | tf_op jit(solution)/shard_map/all_to_all | solution.py:613
  422.8 37.0 %all-to-all-start.8 = ((bf16[8,80,2048]{2,1,0:T(8,128)(2,1)}), bf16[8,80,2048]{2,1,0:T(8,128)(2,1)}, u32[]{:S(2)}, u32[]{:S(2)}) async-start(bf16[8,80,2048]{2,1,0:T(8,128)(2,1)} %bitcast.274), calls=%async_computation.8 | async-start | bytes 5242880 | tf_op jit(solution)/shard_map/all_to_all | solution.py:613
  533.2 37.6 %all-to-all-start.11 = ((bf16[8,80,2048]{2,1,0:T(8,128)(2,1)}), bf16[8,80,2048]{2,1,0:T(8,128)(2,1)}, u32[]{:S(2)}, u32[]{:S(2)}) async-start(bf16[8,80,2048]{2,1,0:T(8,128)(2,1)} %bitcast.269), calls=%async_computation.11 | async-start | bytes 5242880 | tf_op jit(solution)/shard_map/all_to_all | solution.py:613
  570.8 37.2 %all-to-all-start.12 = ((bf16[8,80,2048]{2,1,0:T(8,128)(2,1)}), bf16[8,80,2048]{2,1,0:T(8,128)(2,1)}, u32[]{:S(2)}, u32[]{:S(2)}) async-start(bf16[8,80,2048]{2,1,0:T(8,128)(2,1)} %bitcast.271), calls=%async_computation.12 | async-start | bytes 5242880 | tf_op jit(solution)/shard_map/all_to_all | solution.py:613
  608.0 94.9 %all-to-all-start.13 = ((bf16[8,80,2048]{2,1,0:T(8,128)(2,1)}), bf16[8,80,2048]{2,1,0:T(8,128)(2,1)}, u32[]{:S(2)}, u32[]{:S(2)}) async-start(bf16[8,80,2048]{2,1,0:T(8,128)(2,1)} %bitcast.268), calls=%async_computation.13 | async-start | bytes 5242880 | tf_op jit(solution)/shard_map/all_to_all | solution.py:613
  612.4 37.7 %collective-permute-start.44 = (bf16[256,2048]{1,0:T(8,128)(2,1)}, bf16[256,2048]{1,0:T(8,128)(2,1)}, u32[]{:S(2)}, u32[]{:S(2)}) collective-permute-start(bf16[256,2048]{1,0:T(8,128)(2,1)} %get-tuple-element.547.left_ref.refs_0_), channel_id=1, source_target_pairs={{0,3},{1,0},{2,1},{3,2},{4,7},{5,4},{6,5},{7,6},{8,11},{9,8},{10,9... | collective-permute-start | bytes 3145736 | tf_op jit(solution)/shard_map/ppermute | solution.py:586
  613.5 47.0 %collective-permute-start.43 = (bf16[256,2048]{1,0:T(8,128)(2,1)}, bf16[256,2048]{1,0:T(8,128)(2,1)}, u32[]{:S(2)}, u32[]{:S(2)}) collective-permute-start(bf16[256,2048]{1,0:T(8,128)(2,1)} %get-tuple-element.547.left_ref.refs_0_), channel_id=1, source_target_pairs={{0,1},{1,2},{2,3},{3,0},{4,5},{5,6},{6,7},{7,4},{8,9},{9,10},{10,1... | collective-permute-start | bytes 3145736 | tf_op jit(solution)/shard_map/ppermute | solution.py:586
  739.8 52.4 %all-to-all-start.15 = ((bf16[4,256,1024]{2,1,0:T(8,128)(2,1)}), bf16[4,256,1024]{2,1,0:T(8,128)(2,1)}, u32[]{:S(2)}, u32[]{:S(2)}) async-start(bf16[4,256,1024]{2,1,0:T(8,128)(2,1)} %bitcast.263), calls=%async_computation.15 | async-start | bytes 4194304 | tf_op jit(solution)/shard_map/all_to_all | solution.py:882
  774.7 72.1 %collective-permute-start.53 = (bf16[256,2048]{1,0:T(8,128)(2,1)}, bf16[256,2048]{1,0:T(8,128)(2,1)}, u32[]{:S(2)}, u32[]{:S(2)}) collective-permute-start(bf16[256,2048]{1,0:T(8,128)(2,1)} %product.37), channel_id=1, source_target_pairs={{0,1},{1,2},{2,3},{3,0},{4,5},{5,6},{6,7},{7,4},{8,9},{9,10},{10,1... | collective-permute-start | bytes 3145736 | tf_op jit(solution)/shard_map/ppermute | solution.py:586
  792.2 64.8 %all-to-all-start.16 = ((bf16[8,80,2048]{2,1,0:T(8,128)(2,1)}), bf16[8,80,2048]{2,1,0:T(8,128)(2,1)}, u32[]{:S(2)}, u32[]{:S(2)}) async-start(bf16[8,80,2048]{2,1,0:T(8,128)(2,1)} %bitcast.267), calls=%async_computation.16 | async-start | bytes 5242880 | tf_op jit(solution)/shard_map/all_to_all | solution.py:613
  808.5 42.9 %collective-permute-start.49 = (bf16[128,2048]{1,0:T(8,128)(2,1)}, bf16[128,2048]{1,0:T(8,128)(2,1)}, u32[]{:S(2)}, u32[]{:S(2)}) collective-permute-start(bf16[128,2048]{1,0:T(8,128)(2,1)} %get-tuple-element.444), channel_id=1, source_target_pairs={{0,1},{1,2},{2,3},{3,0},{4,5},{5,6},{6,7},{7,4},{8,9},{9,10},{10,1... | collective-permute-start | bytes 1572872 | tf_op jit(solution)/shard_map/ppermute | solution.py:586
  808.6 42.9 %collective-permute-start.50 = (bf16[128,2048]{1,0:T(8,128)(2,1)}, bf16[128,2048]{1,0:T(8,128)(2,1)}, u32[]{:S(2)}, u32[]{:S(2)}) collective-permute-start(bf16[128,2048]{1,0:T(8,128)(2,1)} %get-tuple-element.445), channel_id=1, source_target_pairs={{0,3},{1,0},{2,1},{3,2},{4,7},{5,4},{6,5},{7,6},{8,11},{9,8},{10,9... | collective-permute-start | bytes 1572872 | tf_op jit(solution)/shard_map/ppermute | solution.py:586
  812.4 39.0 %collective-permute-start.51 = (bf16[128,2048]{1,0:T(8,128)(2,1)}, bf16[128,2048]{1,0:T(8,128)(2,1)}, u32[]{:S(2)}, u32[]{:S(2)}) collective-permute-start(bf16[128,2048]{1,0:T(8,128)(2,1)} %get-tuple-element.446), channel_id=1, source_target_pairs={{0,1},{1,2},{2,3},{3,0},{4,5},{5,6},{6,7},{7,4},{8,9},{9,10},{10,1... | collective-permute-start | bytes 1572872 | tf_op jit(solution)/shard_map/ppermute | solution.py:586
  812.5 44.5 %collective-permute-start.52 = (bf16[128,2048]{1,0:T(8,128)(2,1)}, bf16[128,2048]{1,0:T(8,128)(2,1)}, u32[]{:S(2)}, u32[]{:S(2)}) collective-permute-start(bf16[128,2048]{1,0:T(8,128)(2,1)} %get-tuple-element.447), channel_id=1, source_target_pairs={{0,3},{1,0},{2,1},{3,2},{4,7},{5,4},{6,5},{7,6},{8,11},{9,8},{10,9... | collective-permute-start | bytes 1572872 | tf_op jit(solution)/shard_map/ppermute | solution.py:586
  876.0 43.9 %collective-permute-start.54 = (bf16[256,2048]{1,0:T(8,128)(2,1)}, bf16[256,2048]{1,0:T(8,128)(2,1)}, u32[]{:S(2)}, u32[]{:S(2)}) collective-permute-start(bf16[256,2048]{1,0:T(8,128)(2,1)} %product.38), channel_id=1, source_target_pairs={{0,1},{1,2},{2,3},{3,0},{4,5},{5,6},{6,7},{7,4},{8,9},{9,10},{10,1... | collective-permute-start | bytes 3145736 | tf_op jit(solution)/shard_map/ppermute | solution.py:586
  878.2 46.7 %all-to-all-start.17 = ((bf16[4,256,1280]{2,1,0:T(8,128)(2,1)}), bf16[4,256,1280]{2,1,0:T(8,128)(2,1)}, u32[]{:S(2)}, u32[]{:S(2)}) async-start(bf16[4,256,1280]{2,1,0:T(8,128)(2,1)} %bitcast.262), calls=%async_computation.17 | async-start | bytes 5242880 | tf_op jit(solution)/shard_map/all_to_all | solution.py:882
  (95 other events, 2423.4 us)
Sparse Core Ops, SparseCore 0:
  10.9 18.3 all-gather.2
  30.9 14.3 all-gather.4

commit v5 on v3

--- a/solution.py
+++ b/solution.py
@@ -830,7 +830,7 @@
 
     grad_low = grad_hidden.astype(bf16)
     near_gradient = gather_near(grad_low)
-    output_back = {1: swap(after(returned[1], grad_back[0]))}
+    output_back = {1: swap(after(returned[1], grad_low))}
     grad_attended = {0: product(grad_low, full_out)}
     grad_gate_weight, grad_up_weight = weight_gradients(
         after(arrived, grad_low), [gate_grads, up_grads], f32, row_weights
@@ -840,20 +840,15 @@
     )
 
     far_gradient = gather_far(*near_gradient)
-    output_back[2] = swap(after(returned[2], output_back[1], grad_low))
+    output_back[2] = swap(after(returned[2], output_back[1], near_gradient))
     grad_attended.update({1: product(near_gradient[0], full_out), 3: product(near_gradient[1], full_out)})
     output_part = collect(output_back, 1)
     far_gradient = jnp.concatenate(after(far_gradient, output_part), axis=0)
-    router_sums = grad_router.reshape(1, columns, width // columns * experts)
-    router_sums = jnp.take(after(router_sums, near_gradient), to_ring, axis=1)
-    router_sums = jnp.sum(exchange_columns(router_sums)[0], axis=0)
-    far_gradient, grad_attended, output_part, router_sums = after(
-        (far_gradient, grad_attended, output_part, router_sums)
-    )
+    far_gradient, grad_attended, output_part = after((far_gradient, grad_attended, output_part))
 
     grad_sequence = [grad_low, near_gradient[0], far_gradient, near_gradient[1]]
     running = up(output_part)
-    output_back[3] = swap(after(returned[3], output_back[2]))
+    output_back[3] = swap(after(returned[3], output_back[2], grad_attended))
     grad_attended[2] = product(far_gradient, full_out)
     grad_attended = [grad_attended[s] for s in range(columns)]
     half = heads // 2
@@ -887,7 +882,11 @@
 
     out_parts = exchange_parts(weight_parts(grad_sequence, attended))
     first_half = attention_backward(*arguments, 0, half)
-    first_half, running, out_parts = after((first_half, running, out_parts))
+    router_sums = grad_router.reshape(1, columns, width // columns * experts)
+    router_sums = jnp.take(after(router_sums, far_gradient), to_ring, axis=1)
+    router_sums = exchange_columns(router_sums)
+    first_half, running, out_parts, router_sums = after((first_half, running, out_parts, router_sums))
+    router_sums = jnp.sum(router_sums[0], axis=0)
     out_sums = sum_of(out_parts)
     out_sums = swap_parts(after(out_sums, output_back[3]))
     output_part = collect(output_back, 2, running)
@@ -908,8 +907,8 @@
     output_back[0] = swap(after(returned[0], out_sums))
     free_up, free_down = up(free_up), down(free_down)
     qkv_parts = weight_parts(normed, after(grad_qkv, attn_gain_sums))
-    first_up, first_down, free_up, free_down, grad_down, output_part, qkv_parts = after(
-        (first_up, first_down, free_up, free_down, grad_down, output_part, qkv_parts)
+    first_up, first_down, free_up, free_down, grad_down, output_part, qkv_parts, output_back[0] = after(
+        (first_up, first_down, free_up, free_down, grad_down, output_part, qkv_parts, output_back[0])
     )
 
     second_up = up(scatter_second(up_rest, first_up))

time: 922 us -> 950 us (1.030)
  waiting for transfers between devices: 270 us -> 312 us
  starting transfers between devices: 182 us -> 164 us
    ppermute x48, waiting for transfers between devices: 183 us -> 232 us  [shifted(): lax.ppermute(block, 'col', [(i, (i + by) % columns) for i in range(column...]
    ppermute x48, starting transfers between devices: 76.9 us -> 62.1 us  [shifted(): lax.ppermute(block, 'col', [(i, (i + by) % columns) for i in range(column...]
  transfers between devices with their start and end apart: 85 -> 85, of which waited for: 37 -> 40; matrix products, arithmetic and copies ran while one was open for 12% -> 12% of each run, Pallas kernels for 34% -> 33%
where the time goes in v5:
time: 950 us; the launch traced here: 938 us
  Pallas kernels  314 us (33%)
  waiting for transfers between devices  312 us (33%)
  starting transfers between devices  164 us (17%)
  other arithmetic  74.7 us (8%)
  local copies, waits for them, and re-layouts  29.9 us (3%)
  matrix products  27.3 us (3%)
  between operations  15.6 us (2%)
    ppermute x48, waiting for transfers between devices, shifted(): lax.ppermute(block, 'col', [(i, (i + by) % columns) for i in range(column...  232 us
    pallas_call x20, Pallas kernels, product(): pl.pallas_call(functools.partial(product_kernel, transposed), out_shape=j...  88.5 us
    pallas_call x4, Pallas kernels, expert_block(): pl.pallas_call(expert_kernel, out_shape=[shape((count, hidden), bf16), sh...  83.6 us
    all_to_all x17, starting transfers between devices, swap(): lax.all_to_all(rows.reshape(peers, rows.shape[0] // peers, *rows.shape[1:...  75.9 us
    ppermute x48, starting transfers between devices, shifted(): lax.ppermute(block, 'col', [(i, (i + by) % columns) for i in range(column...  62.1 us
    pallas_call x2, Pallas kernels, weight_gradients(): pl.pallas_call(functools.partial(weight_kernel, blocks, len(rights), weig...  46.4 us
    all_to_all x17, waiting for transfers between devices, swap(): lax.all_to_all(rows.reshape(peers, rows.shape[0] // peers, *rows.shape[1:...  39.3 us
    ppermute x14, waiting for transfers between devices, exchange_plane(): parts[step] = lax.ppermute(part, plane, pairs) if step else part  37.6 us
  transfers between devices with their start and end apart: 85, of which 40 were waited for; matrix products, arithmetic and copies ran while one was open for 12% of the time, Pallas kernels for 33%

profile of v5, /device:TPU:0, one launch (start us, length us, event | category | flops | bytes accessed | tf_op | source)
XLA Modules:
  0.0 938.3 jit_solution(3115153168937993756)
XLA Ops:
  40.6 22.2 %collective-permute-done = bf16[256,2048]{1,0:T(8,128)(2,1)S(1)} collective-permute-done((bf16[256,2048]{1,0:T(8,128)(2,1)S(1)}, bf16[256,2048]{1,0:T(8,128)(2,1)S(1)}, u32[]{:S(2)}, u32[]{:S(2)}) %collective-permute-start) | collective-permute-done | bytes 1048608 | tf_op jit(solution)/shard_map/ppermute | solution.py:586
  102.6 20.2 %attention_forward.1 = (bf16[256,1024]{1,0:T(8,128)(2,1)}, bf16[256,1024]{1,0:T(8,128)(2,1)}, bf16[256,1024]{1,0:T(8,128)(2,1)}, bf16[256,1024]{1,0:T(8,128)(2,1)}, f32[8,1,1024]{2,1,0:T(1,128)}) custom-call(s32[1]{0:T(128)} %bitcast.4.col_ref, f32[256,1280]{1,0:T(8,128)} %fusion.51.refs_0_.refs_4_.refs_8_, f32[256,1280]{1,0:T(8,128)} %fusion.52.refs_1_.refs_5_.refs_9_, ...), custom_call_target="tpu_custom_call" | custom-call | flops 1000 | bytes 1000 | tf_op jit(solution)/shard_map/attention_forward/pallas_call | solution.py:124
  166.2 11.1 %collective-permute-done.9 = bf16[128,2048]{1,0:T(8,128)(2,1)S(1)} collective-permute-done((bf16[128,2048]{1,0:T(8,128)(2,1)}, bf16[128,2048]{1,0:T(8,128)(2,1)S(1)}, u32[]{:S(2)}, u32[]{:S(2)}) %collective-permute-start.9) | collective-permute-done | bytes 524320 | tf_op jit(solution)/shard_map/ppermute | solution.py:586
  177.4 10.6 %collective-permute-done.10 = bf16[128,2048]{1,0:T(8,128)(2,1)S(1)} collective-permute-done((bf16[128,2048]{1,0:T(8,128)(2,1)}, bf16[128,2048]{1,0:T(8,128)(2,1)S(1)}, u32[]{:S(2)}, u32[]{:S(2)}) %collective-permute-start.10) | collective-permute-done | bytes 524320 | tf_op jit(solution)/shard_map/ppermute | solution.py:586
  200.5 20.8 %collective-permute-done.14 = bf16[128,2048]{1,0:T(8,128)(2,1)S(1)} collective-permute-done((bf16[128,2048]{1,0:T(8,128)(2,1)S(1)}, bf16[128,2048]{1,0:T(8,128)(2,1)S(1)}, u32[]{:S(2)}, u32[]{:S(2)}) %collective-permute-start.14) | collective-permute-done | bytes 524320 | tf_op jit(solution)/shard_map/ppermute | solution.py:586
  246.6 11.4 %collective-permute-done.16 = bf16[128,2048]{1,0:T(8,128)(2,1)S(1)} collective-permute-done((bf16[128,2048]{1,0:T(8,128)(2,1)}, bf16[128,2048]{1,0:T(8,128)(2,1)S(1)}, u32[]{:S(2)}, u32[]{:S(2)}) %collective-permute-start.16) | collective-permute-done | bytes 524320 | tf_op jit(solution)/shard_map/ppermute | solution.py:586
  285.0 18.0 %collective-permute-done.17.right_ref = bf16[256,2048]{1,0:T(8,128)(2,1)} collective-permute-done((bf16[256,2048]{1,0:T(8,128)(2,1)}, bf16[256,2048]{1,0:T(8,128)(2,1)}, u32[]{:S(2)}, u32[]{:S(2)}) %collective-permute-start.17) | collective-permute-done | bytes 1048608 | tf_op jit(solution)/shard_map/ppermute | solution.py:586
  317.2 20.9 %expert_block.4 = (bf16[640,768]{1,0:T(8,128)(2,1)}, bf16[640,768]{1,0:T(8,128)(2,1)}, bf16[640,768]{1,0:T(8,128)(2,1)}, bf16[640,2048]{1,0:T(8,128)(2,1)}, bf16[640,2048]{1,0:T(8,128)(2,1)}, /*index=5*/f32[640,1]{1,0:T(8,128)}) custom-call(bf16[640,2048]{1,0:T(8,128)(2,1)} %bitcast.17.rows_ref.refs_0_, bf16[640,2048]{1,0:T(8,128)(2,1)} %bitcast.3.upstream_ref.refs_4_, ...), custom_call_target="tpu_custom_call" | custom-call | flops 1000 | bytes 1000 | tf_op jit(solution)/shard_map/expert_block/pallas_call | solution.py:519
  354.4 20.8 %expert_block.5 = (bf16[640,768]{1,0:T(8,128)(2,1)}, bf16[640,768]{1,0:T(8,128)(2,1)}, bf16[640,768]{1,0:T(8,128)(2,1)}, bf16[640,2048]{1,0:T(8,128)(2,1)}, bf16[640,2048]{1,0:T(8,128)(2,1)}, /*index=5*/f32[640,1]{1,0:T(8,128)}) custom-call(bf16[640,2048]{1,0:T(8,128)(2,1)} %bitcast.30.rows_ref.refs_1_, bf16[640,2048]{1,0:T(8,128)(2,1)} %bitcast.11.upstream_ref.refs_5_, ...), custom_call_target="tpu_custom_call" | custom-call | flops 1000 | bytes 1000 | tf_op jit(solution)/shard_map/expert_block/pallas_call | solution.py:519
  385.7 20.9 %expert_block.6 = (bf16[640,768]{1,0:T(8,128)(2,1)}, bf16[640,768]{1,0:T(8,128)(2,1)}, bf16[640,768]{1,0:T(8,128)(2,1)}, bf16[640,2048]{1,0:T(8,128)(2,1)}, bf16[640,2048]{1,0:T(8,128)(2,1)}, /*index=5*/f32[640,1]{1,0:T(8,128)}) custom-call(bf16[640,2048]{1,0:T(8,128)(2,1)} %bitcast.36.rows_ref.refs_2_, bf16[640,2048]{1,0:T(8,128)(2,1)} %bitcast.15.upstream_ref.refs_6_, ...), custom_call_target="tpu_custom_call" | custom-call | flops 1000 | bytes 1000 | tf_op jit(solution)/shard_map/expert_block/pallas_call | solution.py:519
  406.6 11.4 %all-to-all-done.7 = bf16[8,80,2048]{2,1,0:T(8,128)(2,1)} async-done(((bf16[8,80,2048]{2,1,0:T(8,128)(2,1)}), bf16[8,80,2048]{2,1,0:T(8,128)(2,1)}, u32[]{:S(2)}, u32[]{:S(2)}) %all-to-all-start.7) | async-done | bytes 2621472 | tf_op jit(solution)/shard_map/all_to_all | solution.py:613
  430.2 20.9 %expert_block.7 = (bf16[640,768]{1,0:T(8,128)(2,1)}, bf16[640,768]{1,0:T(8,128)(2,1)}, bf16[640,768]{1,0:T(8,128)(2,1)}, bf16[640,2048]{1,0:T(8,128)(2,1)}, bf16[640,2048]{1,0:T(8,128)(2,1)}, /*index=5*/f32[640,1]{1,0:T(8,128)}) custom-call(bf16[640,2048]{1,0:T(8,128)(2,1)} %bitcast.52.rows_ref.refs_3_, bf16[640,2048]{1,0:T(8,128)(2,1)} %bitcast.13.upstream_ref.refs_7_, ...), custom_call_target="tpu_custom_call" | custom-call | flops 1000 | bytes 1000 | tf_op jit(solution)/shard_map/expert_block/pallas_call | solution.py:519
  471.8 20.1 %collective-permute-done.32 = f32[4,80]{1,0:T(4,128)S(1)} collective-permute-done((f32[4,80]{1,0:T(4,128)S(1)}, f32[4,80]{1,0:T(4,128)S(1)}, u32[]{:S(2)}, u32[]{:S(2)}) %collective-permute-start.32) | collective-permute-done | bytes 1312 | tf_op jit(solution)/shard_map/ppermute | solution.py:628
  510.2 17.5 %collective-permute-done.37 = f32[4,80]{1,0:T(4,128)S(1)} collective-permute-done((f32[4,80]{1,0:T(4,128)S(1)}, f32[4,80]{1,0:T(4,128)S(1)}, u32[]{:S(2)}, u32[]{:S(2)}) %collective-permute-start.37) | collective-permute-done | bytes 1312 | tf_op jit(solution)/shard_map/ppermute | solution.py:628
  543.3 22.2 %collective-permute-done.40 = f32[8,80]{1,0:T(8,128)S(1)} collective-permute-done((f32[8,80]{1,0:T(8,128)S(1)}, f32[8,80]{1,0:T(8,128)S(1)}, u32[]{:S(2)}, u32[]{:S(2)}) %collective-permute-start.40) | collective-permute-done | bytes 2592 | tf_op jit(solution)/shard_map/ppermute | solution.py:586
  587.7 28.1 %weight_gradients.2 = (f32[2048,768]{1,0:T(8,128)}, f32[2048,768]{1,0:T(8,128)}) custom-call(bf16[640,2048]{1,0:T(8,128)(2,1)} %bitcast.17.rows_ref.refs_0_, bf16[640,2048]{1,0:T(8,128)(2,1)} %bitcast.30.rows_ref.refs_1_, bf16[640,2048]{1,0:T(8,128)(2,1)} %bitcast.36.rows_ref.refs_2_, bf16[640,2048]{1,0:T(8,128)(2,1)} %bitcast.52.rows_ref.refs_3_, ...), custom_call_target="tpu_custom_call" | custom-call | flops 1000 | bytes 1000 | tf_op jit(solution)/shard_map/weight_gradients/pallas_call | solution.py:324
  662.7 10.8 %split_gradient.2 = (bf16[1024,1024]{1,0:T(8,128)(2,1)}, bf16[1024,1024]{1,0:T(8,128)(2,1)}) custom-call(s32[1]{0:T(128)} %bitcast.97.mine_ref, bf16[256,2048]{1,0:T(8,128)(2,1)} %get-tuple-element.567.left_ref.refs_0_, bf16[256,2048]{1,0:T(8,128)(2,1)} %collective-permute-done.43.left_ref.refs_1_, bf16[256,2048]{1,0:T(8,128)(2,1)} %pad_maximum_fusion.3.left_ref.refs_2_, ...), custom_call_target="tpu_custom_call" | custom-call | flops 1000 | bytes 1000 | tf_op jit(solution)/shard_map/split_gradient/pallas_call | solution.py:365
  676.1 12.4 %all-to-all-done.13 = bf16[8,80,2048]{2,1,0:T(8,128)(2,1)} async-done(((bf16[8,80,2048]{2,1,0:T(8,128)(2,1)}), bf16[8,80,2048]{2,1,0:T(8,128)(2,1)}, u32[]{:S(2)}, u32[]{:S(2)}) %all-to-all-start.13) | async-done | bytes 2621472 | tf_op jit(solution)/shard_map/all_to_all | solution.py:613
  704.5 16.2 %attention_backward.2 = (bf16[256,1280]{1,0:T(8,128)(2,1)}, bf16[256,1280]{1,0:T(8,128)(2,1)}, bf16[256,1280]{1,0:T(8,128)(2,1)}, bf16[256,1280]{1,0:T(8,128)(2,...) custom-call(s32[1]{0:T(128)} %bitcast.4.col_ref, ...), custom_call_target="tpu_custom_call" | custom-call | flops 1000 | bytes 1000 | tf_op jit(solution)/shard_map/attention_backward/pallas_call | solution.py:254
  739.9 17.5 %attention_backward.3 = (bf16[256,1280]{1,0:T(8,128)(2,1)}, bf16[256,1280]{1,0:T(8,128)(2,1)}, bf16[256,1280]{1,0:T(8,128)(2,1)}, bf16[256,1280]{1,0:T(8,128)(2,...) custom-call(s32[1]{0:T(128)} %bitcast.4.col_ref, ...), custom_call_target="tpu_custom_call", output_to_operand_aliasing={{0}: (22, {}), {1}: (23, {}), {2}: (24, {}), {3}: (25, {})} | custom-call | flops 1000 | bytes 1000 | tf_op jit(solution)/shard_map/attention_backward/pallas_call | solution.py:254
  764.8 11.2 %spread.3 = (bf16[128,2048]{1,0:T(8,128)(2,1)}, bf16[128,2048]{1,0:T(8,128)(2,1)}, bf16[128,2048]{1,0:T(8,128)(2,1)}, bf16[128,2048]{1,0:T(8,128)(2,1)}, f32[128...) custom-call(bf16[256,1280]{1,0:T(8,128)(2,1)} %get-tuple-element.478.refs_0_.refs_4_, ...), custom_call_target="tpu_custom_call" | custom-call | flops 1000 | bytes 1000 | tf_op jit(solution)/shard_map/spread/pallas_call | solution.py:412
  783.9 11.9 %split_gradient.3 = (bf16[1024,1280]{1,0:T(8,128)(2,1)}, bf16[1024,1280]{1,0:T(8,128)(2,1)}) custom-call(s32[1]{0:T(128)} %bitcast.97.mine_ref, bf16[256,2048]{1,0:T(8,128)(2,1)} %get-tuple-element.580.refs_0_, bf16[256,2048]{1,0:T(8,128)(2,1)} %copy-done.12, bf16[256,2048]{1,0:T(8,128)(2,1)} %copy-done.10, bf16[256,2048]{1,0:T(8,128)(2,1)} %copy-done.11, ...), custom_call_target="tpu_custom_call" | custom-call | flops 1000 | bytes 1000 | tf_op jit(solution)/shard_map/split_gradient/pallas_call | solution.py:365
  795.8 18.3 %weight_gradients.3 = f32[768,2048]{1,0:T(8,128)} custom-call(bf16[640,768]{1,0:T(8,128)(2,1)} %get-tuple-element.473.refs_0_, bf16[640,768]{1,0:T(8,128)(2,1)} %get-tuple-element.474.refs_1_, bf16[640,768]{1,0:T(8,128)(2,1)} %get-tuple-element.475.refs_2_, bf16[640,768]{1,0:T(8,128)(2,1)} %get-tuple-element.476.refs_3_, ...), custom_call_target="tpu_custom_call" | custom-call | flops 1000 | bytes 1000 | tf_op jit(solution)/shard_map/weight_gradients/pallas_call | solution.py:324
  878.3 17.6 %collective-permute-done.57.refs_0_ = bf16[256,2048]{1,0:T(8,128)(2,1)} collective-permute-done((bf16[256,2048]{1,0:T(8,128)(2,1)}, bf16[256,2048]{1,0:T(8,128)(2,1)}, u32[]{:S(2)}, u32[]{:S(2)}) %collective-permute-start.57) | collective-permute-done | bytes 1048608 | tf_op jit(solution)/shard_map/ppermute | solution.py:586
  (446 shorter events, 509.4 us)
Async XLA Ops:
  7.2 55.6 %all-gather.3.cloned.1.call-start = ((), (), s32[]{:S(2)}) async-start(), calls=%async_computation.19 | async-start | bytes 7864320 | tf_op jit(solution)/shard_map/all_gather | solution.py:683
  17.0 45.8 %collective-permute-start = (bf16[256,2048]{1,0:T(8,128)(2,1)S(1)}, bf16[256,2048]{1,0:T(8,128)(2,1)S(1)}, u32[]{:S(2)}, u32[]{:S(2)}) collective-permute-start(bf16[256,2048]{1,0:T(8,128)(2,1)S(1)} %copy-done.2), channel_id=1, source_target_pairs={{0,1},{1,2},{2,3},{3,0},{4,5},{5,6},{6,7},{7,4},{8,9},{9,10},{10,1... | collective-permute-start | bytes 3145736 | tf_op jit(solution)/shard_map/ppermute | solution.py:586
  22.7 64.9 %all-to-all-start = ((bf16[8,80,2048]{2,1,0:T(8,128)(2,1)}), bf16[8,80,2048]{2,1,0:T(8,128)(2,1)}, u32[]{:S(2)}, u32[]{:S(2)}) async-start(bf16[8,80,2048]{2,1,0:T(8,128)(2,1)} %bitcast.256), calls=%async_computation | async-start | bytes 5242880 | tf_op jit(solution)/shard_map/all_to_all | solution.py:613
  27.3 95.5 %all-gather.5.cloned.1.call-start = ((), (), s32[]{:S(2)}) async-start(), calls=%async_computation.20 | async-start | bytes 6291456 | tf_op jit(solution)/shard_map/all_gather | solution.py:684
  87.7 43.1 %collective-permute-start.8 = (s32[8,256]{1,0:T(8,128)S(1)}, s32[8,256]{1,0:T(8,128)S(1)}, u32[]{:S(2)}, u32[]{:S(2)}) collective-permute-start(s32[8,256]{1,0:T(8,128)S(1)} %bitcast.280), channel_id=1, source_target_pairs={{0,3},{1,0},{2,1},{3,2},{4,7},{5,4},{6,5},{7,6},{8,11},{9,8},{10,9... | collective-permute-start | bytes 24584 | tf_op jit(solution)/shard_map/ppermute | solution.py:586
  90.3 40.5 %collective-permute-start.7 = (s32[8,256]{1,0:T(8,128)S(1)}, s32[8,256]{1,0:T(8,128)S(1)}, u32[]{:S(2)}, u32[]{:S(2)}) collective-permute-start(s32[8,256]{1,0:T(8,128)S(1)} %bitcast.281), channel_id=1, source_target_pairs={{0,2},{1,3},{2,0},{3,1},{4,6},{5,7},{6,4},{7,5},{8,10},{9,11},{10,... | collective-permute-start | bytes 24584 | tf_op jit(solution)/shard_map/ppermute | solution.py:586
  90.9 39.9 %collective-permute-start.6 = (s32[8,256]{1,0:T(8,128)S(1)}, s32[8,256]{1,0:T(8,128)S(1)}, u32[]{:S(2)}, u32[]{:S(2)}) collective-permute-start(s32[8,256]{1,0:T(8,128)S(1)} %bitcast.282), channel_id=1, source_target_pairs={{0,1},{1,2},{2,3},{3,0},{4,5},{5,6},{6,7},{7,4},{8,9},{9,10},{10,1... | collective-permute-start | bytes 24584 | tf_op jit(solution)/shard_map/ppermute | solution.py:586
  92.2 51.8 %collective-permute-start.5 = (bf16[256,2048]{1,0:T(8,128)(2,1)S(1)}, bf16[256,2048]{1,0:T(8,128)(2,1)}, u32[]{:S(2)}, u32[]{:S(2)}) collective-permute-start(bf16[256,2048]{1,0:T(8,128)(2,1)S(1)} %copy-done.7), channel_id=1, source_target_pairs={{0,3},{1,0},{2,1},{3,2},{4,7},{5,4},{6,5},{7,6},{8,11},{9,8},{10,9... | collective-permute-start | bytes 3145736 | tf_op jit(solution)/shard_map/ppermute | solution.py:586
  94.7 44.9 %collective-permute-start.4 = (bf16[256,2048]{1,0:T(8,128)(2,1)S(1)}, bf16[256,2048]{1,0:T(8,128)(2,1)}, u32[]{:S(2)}, u32[]{:S(2)}) collective-permute-start(bf16[256,2048]{1,0:T(8,128)(2,1)S(1)} %copy-done.7), channel_id=1, source_target_pairs={{0,1},{1,2},{2,3},{3,0},{4,5},{5,6},{6,7},{7,4},{8,9},{9,10},{10,1... | collective-permute-start | bytes 3145736 | tf_op jit(solution)/shard_map/ppermute | solution.py:586
  144.0 44.0 %all-to-all-start.1 = ((bf16[8,80,2048]{2,1,0:T(8,128)(2,1)}), bf16[8,80,2048]{2,1,0:T(8,128)(2,1)}, u32[]{:S(2)}, u32[]{:S(2)}) async-start(bf16[8,80,2048]{2,1,0:T(8,128)(2,1)} %bitcast.259), calls=%async_computation.1 | async-start | bytes 5242880 | tf_op jit(solution)/shard_map/all_to_all | solution.py:613
  188.8 42.9 %all-to-all-start.2 = ((bf16[8,80,2048]{2,1,0:T(8,128)(2,1)}), bf16[8,80,2048]{2,1,0:T(8,128)(2,1)}, u32[]{:S(2)}, u32[]{:S(2)}) async-start(bf16[8,80,2048]{2,1,0:T(8,128)(2,1)} %bitcast.257), calls=%async_computation.2 | async-start | bytes 5242880 | tf_op jit(solution)/shard_map/all_to_all | solution.py:613
  577.7 69.6 %all-to-all-start.12 = ((bf16[8,80,2048]{2,1,0:T(8,128)(2,1)}), bf16[8,80,2048]{2,1,0:T(8,128)(2,1)}, u32[]{:S(2)}, u32[]{:S(2)}) async-start(bf16[8,80,2048]{2,1,0:T(8,128)(2,1)} %bitcast.269), calls=%async_computation.12 | async-start | bytes 5242880 | tf_op jit(solution)/shard_map/all_to_all | solution.py:613
  582.1 37.8 %collective-permute-start.44 = (bf16[256,2048]{1,0:T(8,128)(2,1)}, bf16[256,2048]{1,0:T(8,128)(2,1)}, u32[]{:S(2)}, u32[]{:S(2)}) collective-permute-start(bf16[256,2048]{1,0:T(8,128)(2,1)} %get-tuple-element.567.left_ref.refs_0_), channel_id=1, source_target_pairs={{0,3},{1,0},{2,1},{3,2},{4,7},{5,4},{6,5},{7,6},{8,11},{9,8},{10,9... | collective-permute-start | bytes 3145736 | tf_op jit(solution)/shard_map/ppermute | solution.py:586
  583.2 47.1 %collective-permute-start.43 = (bf16[256,2048]{1,0:T(8,128)(2,1)}, bf16[256,2048]{1,0:T(8,128)(2,1)}, u32[]{:S(2)}, u32[]{:S(2)}) collective-permute-start(bf16[256,2048]{1,0:T(8,128)(2,1)} %get-tuple-element.567.left_ref.refs_0_), channel_id=1, source_target_pairs={{0,1},{1,2},{2,3},{3,0},{4,5},{5,6},{6,7},{7,4},{8,9},{9,10},{10,1... | collective-permute-start | bytes 3145736 | tf_op jit(solution)/shard_map/ppermute | solution.py:586
  673.4 52.8 %collective-permute-start.48 = (bf16[1024,1024]{1,0:T(8,128)(2,1)}, bf16[1024,1024]{1,0:T(8,128)(2,1)}, u32[]{:S(2)}, u32[]{:S(2)}) collective-permute-start(bf16[1024,1024]{1,0:T(8,128)(2,1)} %get-tuple-element.429), channel_id=1, source_target_pairs={{0,4},{4,0},{1,5},{5,1},{2,6},{6,2},{3,7},{7,3},{8,12},{12,8},{9,1... | collective-permute-start | bytes 6291464 | tf_op jit(solution)/shard_map/ppermute | solution.py:872
  688.5 42.2 %all-to-all-start.14 = ((bf16[8,80,2048]{2,1,0:T(8,128)(2,1)}), bf16[8,80,2048]{2,1,0:T(8,128)(2,1)}, u32[]{:S(2)}, u32[]{:S(2)}) async-start(bf16[8,80,2048]{2,1,0:T(8,128)(2,1)} %bitcast.267), calls=%async_computation.14 | async-start | bytes 5242880 | tf_op jit(solution)/shard_map/all_to_all | solution.py:613
  760.3 76.9 %all-to-all-start.16 = ((bf16[8,80,2048]{2,1,0:T(8,128)(2,1)}), bf16[8,80,2048]{2,1,0:T(8,128)(2,1)}, u32[]{:S(2)}, u32[]{:S(2)}) async-start(bf16[8,80,2048]{2,1,0:T(8,128)(2,1)} %bitcast.266), calls=%async_computation.16 | async-start | bytes 5242880 | tf_op jit(solution)/shard_map/all_to_all | solution.py:613
  764.7 49.5 %collective-permute-start.56 = (bf16[256,2048]{1,0:T(8,128)(2,1)}, bf16[256,2048]{1,0:T(8,128)(2,1)}, u32[]{:S(2)}, u32[]{:S(2)}) collective-permute-start(bf16[256,2048]{1,0:T(8,128)(2,1)} %product.37), channel_id=1, source_target_pairs={{0,1},{1,2},{2,3},{3,0},{4,5},{5,6},{6,7},{7,4},{8,9},{9,10},{10,1... | collective-permute-start | bytes 3145736 | tf_op jit(solution)/shard_map/ppermute | solution.py:586
  776.0 42.8 %collective-permute-start.52 = (bf16[128,2048]{1,0:T(8,128)(2,1)}, bf16[128,2048]{1,0:T(8,128)(2,1)}, u32[]{:S(2)}, u32[]{:S(2)}) collective-permute-start(bf16[128,2048]{1,0:T(8,128)(2,1)} %get-tuple-element.464), channel_id=1, source_target_pairs={{0,1},{1,2},{2,3},{3,0},{4,5},{5,6},{6,7},{7,4},{8,9},{9,10},{10,1... | collective-permute-start | bytes 1572872 | tf_op jit(solution)/shard_map/ppermute | solution.py:586
  778.3 40.5 %collective-permute-start.53 = (bf16[128,2048]{1,0:T(8,128)(2,1)}, bf16[128,2048]{1,0:T(8,128)(2,1)}, u32[]{:S(2)}, u32[]{:S(2)}) collective-permute-start(bf16[128,2048]{1,0:T(8,128)(2,1)} %get-tuple-element.465), channel_id=1, source_target_pairs={{0,3},{1,0},{2,1},{3,2},{4,7},{5,4},{6,5},{7,6},{8,11},{9,8},{10,9... | collective-permute-start | bytes 1572872 | tf_op jit(solution)/shard_map/ppermute | solution.py:586
  780.1 46.6 %collective-permute-start.54 = (bf16[128,2048]{1,0:T(8,128)(2,1)}, bf16[128,2048]{1,0:T(8,128)(2,1)}, u32[]{:S(2)}, u32[]{:S(2)}) collective-permute-start(bf16[128,2048]{1,0:T(8,128)(2,1)} %get-tuple-element.466), channel_id=1, source_target_pairs={{0,1},{1,2},{2,3},{3,0},{4,5},{5,6},{6,7},{7,4},{8,9},{9,10},{10,1... | collective-permute-start | bytes 1572872 | tf_op jit(solution)/shard_map/ppermute | solution.py:586
  780.4 56.8 %collective-permute-start.55 = (bf16[128,2048]{1,0:T(8,128)(2,1)}, bf16[128,2048]{1,0:T(8,128)(2,1)}, u32[]{:S(2)}, u32[]{:S(2)}) collective-permute-start(bf16[128,2048]{1,0:T(8,128)(2,1)} %get-tuple-element.467), channel_id=1, source_target_pairs={{0,3},{1,0},{2,1},{3,2},{4,7},{5,4},{6,5},{7,6},{8,11},{9,8},{10,9... | collective-permute-start | bytes 1572872 | tf_op jit(solution)/shard_map/ppermute | solution.py:586
  851.5 44.4 %collective-permute-start.57 = (bf16[256,2048]{1,0:T(8,128)(2,1)}, bf16[256,2048]{1,0:T(8,128)(2,1)}, u32[]{:S(2)}, u32[]{:S(2)}) collective-permute-start(bf16[256,2048]{1,0:T(8,128)(2,1)} %product.38), channel_id=1, source_target_pairs={{0,1},{1,2},{2,3},{3,0},{4,5},{5,6},{6,7},{7,4},{8,9},{9,10},{10,1... | collective-permute-start | bytes 3145736 | tf_op jit(solution)/shard_map/ppermute | solution.py:586
  855.5 45.3 %all-to-all-start.17 = ((bf16[4,256,1280]{2,1,0:T(8,128)(2,1)}), bf16[4,256,1280]{2,1,0:T(8,128)(2,1)}, u32[]{:S(2)}, u32[]{:S(2)}) async-start(bf16[4,256,1280]{2,1,0:T(8,128)(2,1)} %bitcast.261), calls=%async_computation.17 | async-start | bytes 5242880 | tf_op jit(solution)/shard_map/all_to_all | solution.py:881
  (99 other events, 2398.0 us)
Sparse Core Ops, SparseCore 0:
  10.9 18.3 all-gather.2
  30.8 14.4 all-gather.4

commit v6 on v3

--- a/solution.py
+++ b/solution.py
@@ -905,11 +905,15 @@
     (grad_down,) = weight_gradients(
         after(acted_rows, attn_gain_sums), [cotangent_rows], f32, row_weights
     )
-    output_back[0] = swap(after(returned[0], out_sums))
     free_up, free_down = up(free_up), down(free_down)
     qkv_parts = weight_parts(normed, after(grad_qkv, attn_gain_sums))
-    first_up, first_down, free_up, free_down, grad_down, output_part, qkv_parts = after(
-        (first_up, first_down, free_up, free_down, grad_down, output_part, qkv_parts)
+    small = jnp.concatenate([attn_gain_sums[0], grad_query_gain, grad_key_gain, grad_moe_gain])
+    cuts = [0, width, width + head_size, width + 2 * head_size, 2 * (width + head_size)]
+    small = jnp.concatenate([small, router_sums])
+    small = swap(after(jnp.broadcast_to(small, (peers, small.shape[0])), out_sums))
+    output_back[0] = swap(after(returned[0], small))
+    first_up, first_down, free_up, free_down, grad_down, output_part, qkv_parts, small = after(
+        (first_up, first_down, free_up, free_down, grad_down, output_part, qkv_parts, small)
     )
 
     second_up = up(scatter_second(up_rest, first_up))
@@ -919,13 +923,9 @@
     qkv_sums = sum_of(exchange_parts(qkv_parts))
 
     qkv_parts = swap_parts(after(qkv_sums, output_back[0]))
-    small = jnp.concatenate([attn_gain_sums[0], grad_query_gain, grad_key_gain, grad_moe_gain])
-    cuts = [0, width, width + head_size, width + 2 * head_size, 2 * (width + head_size)]
-    small = jnp.concatenate([small, router_sums])
-    small = swap(after(jnp.broadcast_to(small, (peers, small.shape[0])), qkv_parts))
     reduced_qkv = jnp.sum(qkv_parts.astype(f32), axis=0)
     outputs = (hidden + collect(output_back, 0, running, f32)).astype(bf16)
-    small = jnp.sum(small, axis=0)
+    small = after(jnp.sum(small, axis=0), qkv_sums)
     small = jnp.stack([small, *[shifted(small, step) for step in range(1, columns)]])
     to_true = lax.rem(col - jnp.arange(columns, dtype=jnp.int32) + columns, columns)
     grad_router = jnp.take(small[:, cuts[-1] :], to_true, axis=0).reshape(width, experts)

time: 922 us -> 937 us (1.016)
  starting transfers between devices: 182 us -> 192 us
    all_to_all x17, waiting for transfers between devices: 42.9 us -> 21.2 us  [swap(): lax.all_to_all(rows.reshape(peers, rows.shape[0] // peers, *rows.shape[1:...]
    all_to_all x2, waiting for transfers between devices: 6.28 us -> 21.8 us  [swap_parts(): return lax.all_to_all(parts, 'dp', 0, 0, tiled=True)]
    ppermute x48, starting transfers between devices: 76.9 us -> 87.3 us  [shifted(): lax.ppermute(block, 'col', [(i, (i + by) % columns) for i in range(column...]
  transfers between devices with their start and end apart: 85 -> 85, of which waited for: 37 -> 38; matrix products, arithmetic and copies ran while one was open for 12% -> 12% of each run, Pallas kernels for 34% -> 33%
where the time goes in v6:
time: 937 us; the launch traced here: 925 us
  Pallas kernels  314 us (34%)
  waiting for transfers between devices  271 us (29%)
  starting transfers between devices  192 us (20%)
  other arithmetic  72.4 us (8%)
  local copies, waits for them, and re-layouts  33.2 us (4%)
  matrix products  26 us (3%)
  between operations  15.5 us (2%)
    ppermute x48, waiting for transfers between devices, shifted(): lax.ppermute(block, 'col', [(i, (i + by) % columns) for i in range(column...  191 us
    pallas_call x20, Pallas kernels, product(): pl.pallas_call(functools.partial(product_kernel, transposed), out_shape=j...  88.5 us
    ppermute x48, starting transfers between devices, shifted(): lax.ppermute(block, 'col', [(i, (i + by) % columns) for i in range(column...  87.3 us
    pallas_call x4, Pallas kernels, expert_block(): pl.pallas_call(expert_kernel, out_shape=[shape((count, hidden), bf16), sh...  83.6 us
    all_to_all x17, starting transfers between devices, swap(): lax.all_to_all(rows.reshape(peers, rows.shape[0] // peers, *rows.shape[1:...  76.4 us
    pallas_call x2, Pallas kernels, weight_gradients(): pl.pallas_call(functools.partial(weight_kernel, blocks, len(rights), weig...  46.4 us
    ppermute x14, waiting for transfers between devices, exchange_plane(): parts[step] = lax.ppermute(part, plane, pairs) if step else part  36.6 us
    pallas_call x2, Pallas kernels, attention_backward(): pl.pallas_call(functools.partial(backward_kernel, blocks, head_size ** (-...  33.7 us
  transfers between devices with their start and end apart: 85, of which 38 were waited for; matrix products, arithmetic and copies ran while one was open for 12% of the time, Pallas kernels for 33%

profile of v6, /device:TPU:0, one launch (start us, length us, event | category | flops | bytes accessed | tf_op | source)
XLA Modules:
  0.0 925.2 jit_solution(6897657925889971154)
XLA Ops:
  41.1 21.0 %collective-permute-done.1 = bf16[256,2048]{1,0:T(8,128)(2,1)S(1)} collective-permute-done((bf16[256,2048]{1,0:T(8,128)(2,1)S(1)}, bf16[256,2048]{1,0:T(8,128)(2,1)S(1)}, u32[]{:S(2)}, u32[]{:S(2)}) %collective-permute-start.1) | collective-permute-done | bytes 1048608 | tf_op jit(solution)/shard_map/ppermute | solution.py:586
  104.2 20.2 %attention_forward.1 = (bf16[256,1024]{1,0:T(8,128)(2,1)}, bf16[256,1024]{1,0:T(8,128)(2,1)}, bf16[256,1024]{1,0:T(8,128)(2,1)}, bf16[256,1024]{1,0:T(8,128)(2,1)}, f32[8,1,1024]{2,1,0:T(1,128)}) custom-call(s32[1]{0:T(128)} %bitcast.4.col_ref, f32[256,1280]{1,0:T(8,128)} %fusion.50.refs_0_.refs_4_.refs_8_, f32[256,1280]{1,0:T(8,128)} %fusion.51.refs_1_.refs_5_.refs_9_, ...), custom_call_target="tpu_custom_call" | custom-call | flops 1000 | bytes 1000 | tf_op jit(solution)/shard_map/attention_forward/pallas_call | solution.py:124
  162.2 11.1 %collective-permute-done.10 = bf16[128,2048]{1,0:T(8,128)(2,1)S(1)} collective-permute-done((bf16[128,2048]{1,0:T(8,128)(2,1)}, bf16[128,2048]{1,0:T(8,128)(2,1)S(1)}, u32[]{:S(2)}, u32[]{:S(2)}) %collective-permute-start.10) | collective-permute-done | bytes 524320 | tf_op jit(solution)/shard_map/ppermute | solution.py:586
  173.3 10.8 %collective-permute-done.9 = bf16[128,2048]{1,0:T(8,128)(2,1)S(1)} collective-permute-done((bf16[128,2048]{1,0:T(8,128)(2,1)}, bf16[128,2048]{1,0:T(8,128)(2,1)S(1)}, u32[]{:S(2)}, u32[]{:S(2)}) %collective-permute-start.9) | collective-permute-done | bytes 524320 | tf_op jit(solution)/shard_map/ppermute | solution.py:586
  216.9 12.8 %collective-permute-done.12 = bf16[128,2048]{1,0:T(8,128)(2,1)S(1)} collective-permute-done((bf16[128,2048]{1,0:T(8,128)(2,1)}, bf16[128,2048]{1,0:T(8,128)(2,1)S(1)}, u32[]{:S(2)}, u32[]{:S(2)}) %collective-permute-start.12) | collective-permute-done | bytes 524320 | tf_op jit(solution)/shard_map/ppermute | solution.py:586
  244.6 11.0 %collective-permute-done.16 = bf16[128,2048]{1,0:T(8,128)(2,1)S(1)} collective-permute-done((bf16[128,2048]{1,0:T(8,128)(2,1)}, bf16[128,2048]{1,0:T(8,128)(2,1)S(1)}, u32[]{:S(2)}, u32[]{:S(2)}) %collective-permute-start.16) | collective-permute-done | bytes 524320 | tf_op jit(solution)/shard_map/ppermute | solution.py:586
  283.9 17.2 %collective-permute-done.17.right_ref = bf16[256,2048]{1,0:T(8,128)(2,1)} collective-permute-done((bf16[256,2048]{1,0:T(8,128)(2,1)}, bf16[256,2048]{1,0:T(8,128)(2,1)}, u32[]{:S(2)}, u32[]{:S(2)}) %collective-permute-start.17) | collective-permute-done | bytes 1048608 | tf_op jit(solution)/shard_map/ppermute | solution.py:586
  316.3 20.9 %expert_block.4 = (bf16[640,768]{1,0:T(8,128)(2,1)}, bf16[640,768]{1,0:T(8,128)(2,1)}, bf16[640,768]{1,0:T(8,128)(2,1)}, bf16[640,2048]{1,0:T(8,128)(2,1)}, bf16[640,2048]{1,0:T(8,128)(2,1)}, /*index=5*/f32[640,1]{1,0:T(8,128)}) custom-call(bf16[640,2048]{1,0:T(8,128)(2,1)} %bitcast.17.rows_ref.refs_0_, bf16[640,2048]{1,0:T(8,128)(2,1)} %bitcast.3.upstream_ref.refs_4_, ...), custom_call_target="tpu_custom_call" | custom-call | flops 1000 | bytes 1000 | tf_op jit(solution)/shard_map/expert_block/pallas_call | solution.py:519
  354.4 20.8 %expert_block.5 = (bf16[640,768]{1,0:T(8,128)(2,1)}, bf16[640,768]{1,0:T(8,128)(2,1)}, bf16[640,768]{1,0:T(8,128)(2,1)}, bf16[640,2048]{1,0:T(8,128)(2,1)}, bf16[640,2048]{1,0:T(8,128)(2,1)}, /*index=5*/f32[640,1]{1,0:T(8,128)}) custom-call(bf16[640,2048]{1,0:T(8,128)(2,1)} %bitcast.30.rows_ref.refs_1_, bf16[640,2048]{1,0:T(8,128)(2,1)} %bitcast.11.upstream_ref.refs_5_, ...), custom_call_target="tpu_custom_call" | custom-call | flops 1000 | bytes 1000 | tf_op jit(solution)/shard_map/expert_block/pallas_call | solution.py:519
  384.3 20.9 %expert_block.6 = (bf16[640,768]{1,0:T(8,128)(2,1)}, bf16[640,768]{1,0:T(8,128)(2,1)}, bf16[640,768]{1,0:T(8,128)(2,1)}, bf16[640,2048]{1,0:T(8,128)(2,1)}, bf16[640,2048]{1,0:T(8,128)(2,1)}, /*index=5*/f32[640,1]{1,0:T(8,128)}) custom-call(bf16[640,2048]{1,0:T(8,128)(2,1)} %bitcast.36.rows_ref.refs_2_, bf16[640,2048]{1,0:T(8,128)(2,1)} %bitcast.15.upstream_ref.refs_6_, ...), custom_call_target="tpu_custom_call" | custom-call | flops 1000 | bytes 1000 | tf_op jit(solution)/shard_map/expert_block/pallas_call | solution.py:519
  405.2 11.4 %all-to-all-done.7 = bf16[8,80,2048]{2,1,0:T(8,128)(2,1)} async-done(((bf16[8,80,2048]{2,1,0:T(8,128)(2,1)}), bf16[8,80,2048]{2,1,0:T(8,128)(2,1)}, u32[]{:S(2)}, u32[]{:S(2)}) %all-to-all-start.7) | async-done | bytes 2621472 | tf_op jit(solution)/shard_map/all_to_all | solution.py:613
  428.6 20.9 %expert_block.7 = (bf16[640,768]{1,0:T(8,128)(2,1)}, bf16[640,768]{1,0:T(8,128)(2,1)}, bf16[640,768]{1,0:T(8,128)(2,1)}, bf16[640,2048]{1,0:T(8,128)(2,1)}, bf16[640,2048]{1,0:T(8,128)(2,1)}, /*index=5*/f32[640,1]{1,0:T(8,128)}) custom-call(bf16[640,2048]{1,0:T(8,128)(2,1)} %bitcast.52.rows_ref.refs_3_, bf16[640,2048]{1,0:T(8,128)(2,1)} %bitcast.13.upstream_ref.refs_7_, ...), custom_call_target="tpu_custom_call" | custom-call | flops 1000 | bytes 1000 | tf_op jit(solution)/shard_map/expert_block/pallas_call | solution.py:519
  470.6 19.1 %collective-permute-done.31 = f32[4,80]{1,0:T(4,128)S(1)} collective-permute-done((f32[4,80]{1,0:T(4,128)S(1)}, f32[4,80]{1,0:T(4,128)S(1)}, u32[]{:S(2)}, u32[]{:S(2)}) %collective-permute-start.31) | collective-permute-done | bytes 1312 | tf_op jit(solution)/shard_map/ppermute | solution.py:628
  509.0 10.0 %collective-permute-done.35 = f32[4,80]{1,0:T(4,128)S(1)} collective-permute-done((f32[4,80]{1,0:T(4,128)S(1)}, f32[4,80]{1,0:T(4,128)S(1)}, u32[]{:S(2)}, u32[]{:S(2)}) %collective-permute-start.35) | collective-permute-done | bytes 1312 | tf_op jit(solution)/shard_map/ppermute | solution.py:628
  541.3 14.6 %collective-permute-start.42 = (f32[8,80]{1,0:T(8,128)S(1)}, f32[8,80]{1,0:T(8,128)S(1)}, u32[]{:S(2)}, u32[]{:S(2)}) collective-permute-start(f32[8,80]{1,0:T(8,128)S(1)} %bitcast.316), channel_id=1, source_target_pairs={{0,3},{1,0},{2,1},{3,2},{4,7},{5,4},{6,5},{7,6},{8,11},{9,8},{10,9... | collective-permute-start | bytes 7688 | tf_op jit(solution)/shard_map/ppermute | solution.py:586
  587.9 28.1 %weight_gradients.2 = (f32[2048,768]{1,0:T(8,128)}, f32[2048,768]{1,0:T(8,128)}) custom-call(bf16[640,2048]{1,0:T(8,128)(2,1)} %bitcast.17.rows_ref.refs_0_, bf16[640,2048]{1,0:T(8,128)(2,1)} %bitcast.30.rows_ref.refs_1_, bf16[640,2048]{1,0:T(8,128)(2,1)} %bitcast.36.rows_ref.refs_2_, bf16[640,2048]{1,0:T(8,128)(2,1)} %bitcast.52.rows_ref.refs_3_, ...), custom_call_target="tpu_custom_call" | custom-call | flops 1000 | bytes 1000 | tf_op jit(solution)/shard_map/weight_gradients/pallas_call | solution.py:324
  665.4 10.8 %split_gradient.2 = (bf16[1024,1024]{1,0:T(8,128)(2,1)}, bf16[1024,1024]{1,0:T(8,128)(2,1)}) custom-call(s32[1]{0:T(128)} %bitcast.107.mine_ref, bf16[256,2048]{1,0:T(8,128)(2,1)} %get-tuple-element.569.left_ref.refs_0_, bf16[256,2048]{1,0:T(8,128)(2,1)} %collective-permute-done.43.left_ref.refs_1_, bf16[256,2048]{1,0:T(8,128)(2,1)} %pad_maximum_fusion.3.left_ref.refs_2_, ...), custom_call_target="tpu_custom_call" | custom-call | flops 1000 | bytes 1000 | tf_op jit(solution)/shard_map/split_gradient/pallas_call | solution.py:365
  686.2 16.2 %attention_backward.2 = (bf16[256,1280]{1,0:T(8,128)(2,1)}, bf16[256,1280]{1,0:T(8,128)(2,1)}, bf16[256,1280]{1,0:T(8,128)(2,1)}, bf16[256,1280]{1,0:T(8,128)(2,...) custom-call(s32[1]{0:T(128)} %bitcast.4.col_ref, ...), custom_call_target="tpu_custom_call" | custom-call | flops 1000 | bytes 1000 | tf_op jit(solution)/shard_map/attention_backward/pallas_call | solution.py:254
  723.8 17.5 %attention_backward.3 = (bf16[256,1280]{1,0:T(8,128)(2,1)}, bf16[256,1280]{1,0:T(8,128)(2,1)}, bf16[256,1280]{1,0:T(8,128)(2,1)}, bf16[256,1280]{1,0:T(8,128)(2,...) custom-call(s32[1]{0:T(128)} %bitcast.4.col_ref, ...), custom_call_target="tpu_custom_call", output_to_operand_aliasing={{0}: (22, {}), {1}: (23, {}), {2}: (24, {}), {3}: (25, {})} | custom-call | flops 1000 | bytes 1000 | tf_op jit(solution)/shard_map/attention_backward/pallas_call | solution.py:254
  742.3 11.2 %spread.3 = (bf16[128,2048]{1,0:T(8,128)(2,1)}, bf16[128,2048]{1,0:T(8,128)(2,1)}, bf16[128,2048]{1,0:T(8,128)(2,1)}, bf16[128,2048]{1,0:T(8,128)(2,1)}, f32[128...) custom-call(bf16[256,1280]{1,0:T(8,128)(2,1)} %get-tuple-element.486.refs_0_.refs_4_, ...), custom_call_target="tpu_custom_call" | custom-call | flops 1000 | bytes 1000 | tf_op jit(solution)/shard_map/spread/pallas_call | solution.py:412
  769.2 12.0 %split_gradient.3 = (bf16[1024,1280]{1,0:T(8,128)(2,1)}, bf16[1024,1280]{1,0:T(8,128)(2,1)}) custom-call(s32[1]{0:T(128)} %bitcast.107.mine_ref, bf16[256,2048]{1,0:T(8,128)(2,1)} %get-tuple-element.582.refs_0_, bf16[256,2048]{1,0:T(8,128)(2,1)} %copy-done.12, bf16[256,2048]{1,0:T(8,128)(2,1)} %copy-done.10, bf16[256,2048]{1,0:T(8,128)(2,1)} %copy-done.11, ...), custom_call_target="tpu_custom_call" | custom-call | flops 1000 | bytes 1000 | tf_op jit(solution)/shard_map/split_gradient/pallas_call | solution.py:365
  781.1 18.3 %weight_gradients.3 = f32[768,2048]{1,0:T(8,128)} custom-call(bf16[640,768]{1,0:T(8,128)(2,1)} %get-tuple-element.481.refs_0_, bf16[640,768]{1,0:T(8,128)(2,1)} %get-tuple-element.482.refs_1_, bf16[640,768]{1,0:T(8,128)(2,1)} %get-tuple-element.483.refs_2_, bf16[640,768]{1,0:T(8,128)(2,1)} %get-tuple-element.484.refs_3_, ...), custom_call_target="tpu_custom_call" | custom-call | flops 1000 | bytes 1000 | tf_op jit(solution)/shard_map/weight_gradients/pallas_call | solution.py:324
  849.9 17.5 %collective-permute-done.57.refs_0_ = bf16[256,2048]{1,0:T(8,128)(2,1)} collective-permute-done((bf16[256,2048]{1,0:T(8,128)(2,1)}, bf16[256,2048]{1,0:T(8,128)(2,1)}, u32[]{:S(2)}, u32[]{:S(2)}) %collective-permute-start.57) | collective-permute-done | bytes 1048608 | tf_op jit(solution)/shard_map/ppermute | solution.py:586
  895.3 20.8 %all-to-all-done.18 = bf16[4,256,1280]{2,1,0:T(8,128)(2,1)S(1)} async-done(((bf16[4,256,1280]{2,1,0:T(8,128)(2,1)}), bf16[4,256,1280]{2,1,0:T(8,128)(2,1)S(1)}, u32[]{:S(2)}, u32[]{:S(2)}) %all-to-all-start.18) | async-done | bytes 2621472 | tf_op jit(solution)/shard_map/all_to_all | solution.py:886
  (440 shorter events, 514.4 us)
Async XLA Ops:
  7.2 54.9 %all-gather.3.cloned.1.call-start = ((), (), s32[]{:S(2)}) async-start(), calls=%async_computation.19 | async-start | bytes 7864320 | tf_op jit(solution)/shard_map/all_gather | solution.py:683
  15.0 47.1 %collective-permute-start.1 = (bf16[256,2048]{1,0:T(8,128)(2,1)S(1)}, bf16[256,2048]{1,0:T(8,128)(2,1)S(1)}, u32[]{:S(2)}, u32[]{:S(2)}) collective-permute-start(bf16[256,2048]{1,0:T(8,128)(2,1)S(1)} %copy-done.2), channel_id=1, source_target_pairs={{0,3},{1,0},{2,1},{3,2},{4,7},{5,4},{6,5},{7,6},{8,11},{9,8},{10,9... | collective-permute-start | bytes 3145736 | tf_op jit(solution)/shard_map/ppermute | solution.py:586
  22.7 66.1 %all-to-all-start = ((bf16[8,80,2048]{2,1,0:T(8,128)(2,1)}), bf16[8,80,2048]{2,1,0:T(8,128)(2,1)}, u32[]{:S(2)}, u32[]{:S(2)}) async-start(bf16[8,80,2048]{2,1,0:T(8,128)(2,1)} %bitcast.260), calls=%async_computation | async-start | bytes 5242880 | tf_op jit(solution)/shard_map/all_to_all | solution.py:613
  27.3 97.2 %all-gather.5.cloned.1.call-start = ((), (), s32[]{:S(2)}) async-start(), calls=%async_computation.20 | async-start | bytes 6291456 | tf_op jit(solution)/shard_map/all_gather | solution.py:684
  88.9 43.6 %collective-permute-start.6 = (s32[8,256]{1,0:T(8,128)S(1)}, s32[8,256]{1,0:T(8,128)S(1)}, u32[]{:S(2)}, u32[]{:S(2)}) collective-permute-start(s32[8,256]{1,0:T(8,128)S(1)} %bitcast.286), channel_id=1, source_target_pairs={{0,1},{1,2},{2,3},{3,0},{4,5},{5,6},{6,7},{7,4},{8,9},{9,10},{10,1... | collective-permute-start | bytes 24584 | tf_op jit(solution)/shard_map/ppermute | solution.py:586
  89.3 43.2 %collective-permute-start.7 = (s32[8,256]{1,0:T(8,128)S(1)}, s32[8,256]{1,0:T(8,128)S(1)}, u32[]{:S(2)}, u32[]{:S(2)}) collective-permute-start(s32[8,256]{1,0:T(8,128)S(1)} %bitcast.287), channel_id=1, source_target_pairs={{0,2},{1,3},{2,0},{3,1},{4,6},{5,7},{6,4},{7,5},{8,10},{9,11},{10,... | collective-permute-start | bytes 24584 | tf_op jit(solution)/shard_map/ppermute | solution.py:586
  91.6 40.9 %collective-permute-start.8 = (s32[8,256]{1,0:T(8,128)S(1)}, s32[8,256]{1,0:T(8,128)S(1)}, u32[]{:S(2)}, u32[]{:S(2)}) collective-permute-start(s32[8,256]{1,0:T(8,128)S(1)} %bitcast.288), channel_id=1, source_target_pairs={{0,3},{1,0},{2,1},{3,2},{4,7},{5,4},{6,5},{7,6},{8,11},{9,8},{10,9... | collective-permute-start | bytes 24584 | tf_op jit(solution)/shard_map/ppermute | solution.py:586
  92.8 41.5 %collective-permute-start.4 = (bf16[256,2048]{1,0:T(8,128)(2,1)S(1)}, bf16[256,2048]{1,0:T(8,128)(2,1)}, u32[]{:S(2)}, u32[]{:S(2)}) collective-permute-start(bf16[256,2048]{1,0:T(8,128)(2,1)S(1)} %copy-done.7), channel_id=1, source_target_pairs={{0,1},{1,2},{2,3},{3,0},{4,5},{5,6},{6,7},{7,4},{8,9},{9,10},{10,1... | collective-permute-start | bytes 3145736 | tf_op jit(solution)/shard_map/ppermute | solution.py:586
  93.6 46.4 %collective-permute-start.5 = (bf16[256,2048]{1,0:T(8,128)(2,1)S(1)}, bf16[256,2048]{1,0:T(8,128)(2,1)}, u32[]{:S(2)}, u32[]{:S(2)}) collective-permute-start(bf16[256,2048]{1,0:T(8,128)(2,1)S(1)} %copy-done.7), channel_id=1, source_target_pairs={{0,3},{1,0},{2,1},{3,2},{4,7},{5,4},{6,5},{7,6},{8,11},{9,8},{10,9... | collective-permute-start | bytes 3145736 | tf_op jit(solution)/shard_map/ppermute | solution.py:586
  140.0 44.1 %all-to-all-start.1 = ((bf16[8,80,2048]{2,1,0:T(8,128)(2,1)}), bf16[8,80,2048]{2,1,0:T(8,128)(2,1)}, u32[]{:S(2)}, u32[]{:S(2)}) async-start(bf16[8,80,2048]{2,1,0:T(8,128)(2,1)} %bitcast.263), calls=%async_computation.1 | async-start | bytes 5242880 | tf_op jit(solution)/shard_map/all_to_all | solution.py:613
  184.9 44.8 %all-to-all-start.2 = ((bf16[8,80,2048]{2,1,0:T(8,128)(2,1)}), bf16[8,80,2048]{2,1,0:T(8,128)(2,1)}, u32[]{:S(2)}, u32[]{:S(2)}) async-start(bf16[8,80,2048]{2,1,0:T(8,128)(2,1)} %bitcast.261), calls=%async_computation.2 | async-start | bytes 5242880 | tf_op jit(solution)/shard_map/all_to_all | solution.py:613
  576.1 48.3 %collective-permute-start.43 = (bf16[256,2048]{1,0:T(8,128)(2,1)}, bf16[256,2048]{1,0:T(8,128)(2,1)}, u32[]{:S(2)}, u32[]{:S(2)}) collective-permute-start(bf16[256,2048]{1,0:T(8,128)(2,1)} %get-tuple-element.569.left_ref.refs_0_), channel_id=1, source_target_pairs={{0,1},{1,2},{2,3},{3,0},{4,5},{5,6},{6,7},{7,4},{8,9},{9,10},{10,1... | collective-permute-start | bytes 3145736 | tf_op jit(solution)/shard_map/ppermute | solution.py:586
  576.6 47.8 %collective-permute-start.44 = (bf16[256,2048]{1,0:T(8,128)(2,1)}, bf16[256,2048]{1,0:T(8,128)(2,1)}, u32[]{:S(2)}, u32[]{:S(2)}) collective-permute-start(bf16[256,2048]{1,0:T(8,128)(2,1)} %get-tuple-element.569.left_ref.refs_0_), channel_id=1, source_target_pairs={{0,3},{1,0},{2,1},{3,2},{4,7},{5,4},{6,5},{7,6},{8,11},{9,8},{10,9... | collective-permute-start | bytes 3145736 | tf_op jit(solution)/shard_map/ppermute | solution.py:586
  583.5 51.1 %all-to-all-start.12 = ((bf16[8,80,2048]{2,1,0:T(8,128)(2,1)}), bf16[8,80,2048]{2,1,0:T(8,128)(2,1)}, u32[]{:S(2)}, u32[]{:S(2)}) async-start(bf16[8,80,2048]{2,1,0:T(8,128)(2,1)} %bitcast.274), calls=%async_computation.12 | async-start | bytes 5242880 | tf_op jit(solution)/shard_map/all_to_all | solution.py:613
  634.6 41.6 %all-to-all-start.13 = ((bf16[8,80,2048]{2,1,0:T(8,128)(2,1)}), bf16[8,80,2048]{2,1,0:T(8,128)(2,1)}, u32[]{:S(2)}, u32[]{:S(2)}) async-start(bf16[8,80,2048]{2,1,0:T(8,128)(2,1)} %bitcast.272), calls=%async_computation.13 | async-start | bytes 5242880 | tf_op jit(solution)/shard_map/all_to_all | solution.py:613
  722.1 77.4 %collective-permute-start.56 = (bf16[256,2048]{1,0:T(8,128)(2,1)}, bf16[256,2048]{1,0:T(8,128)(2,1)}, u32[]{:S(2)}, u32[]{:S(2)}) collective-permute-start(bf16[256,2048]{1,0:T(8,128)(2,1)} %product.37), channel_id=1, source_target_pairs={{0,1},{1,2},{2,3},{3,0},{4,5},{5,6},{6,7},{7,4},{8,9},{9,10},{10,1... | collective-permute-start | bytes 3145736 | tf_op jit(solution)/shard_map/ppermute | solution.py:586
  757.2 47.0 %all-to-all-start.16 = ((f32[8,1,20736]{2,1,0:T(1,128)}), f32[8,1,20736]{2,1,0:T(1,128)}, u32[]{:S(2)}, u32[]{:S(2)}) async-start(f32[8,1,20736]{2,1,0:T(1,128)} %reshape.436), calls=%async_computation.16 | async-start | bytes 1327104 | tf_op jit(solution)/shard_map/all_to_all | solution.py:613
  761.4 44.8 %collective-permute-start.52 = (bf16[128,2048]{1,0:T(8,128)(2,1)}, bf16[128,2048]{1,0:T(8,128)(2,1)}, u32[]{:S(2)}, u32[]{:S(2)}) collective-permute-start(bf16[128,2048]{1,0:T(8,128)(2,1)} %get-tuple-element.473), channel_id=1, source_target_pairs={{0,1},{1,2},{2,3},{3,0},{4,5},{5,6},{6,7},{7,4},{8,9},{9,10},{10,1... | collective-permute-start | bytes 1572872 | tf_op jit(solution)/shard_map/ppermute | solution.py:586
  762.2 43.9 %collective-permute-start.53 = (bf16[128,2048]{1,0:T(8,128)(2,1)}, bf16[128,2048]{1,0:T(8,128)(2,1)}, u32[]{:S(2)}, u32[]{:S(2)}) collective-permute-start(bf16[128,2048]{1,0:T(8,128)(2,1)} %get-tuple-element.474), channel_id=1, source_target_pairs={{0,3},{1,0},{2,1},{3,2},{4,7},{5,4},{6,5},{7,6},{8,11},{9,8},{10,9... | collective-permute-start | bytes 1572872 | tf_op jit(solution)/shard_map/ppermute | solution.py:586
  765.3 40.9 %collective-permute-start.54 = (bf16[128,2048]{1,0:T(8,128)(2,1)}, bf16[128,2048]{1,0:T(8,128)(2,1)}, u32[]{:S(2)}, u32[]{:S(2)}) collective-permute-start(bf16[128,2048]{1,0:T(8,128)(2,1)} %get-tuple-element.475), channel_id=1, source_target_pairs={{0,1},{1,2},{2,3},{3,0},{4,5},{5,6},{6,7},{7,4},{8,9},{9,10},{10,1... | collective-permute-start | bytes 1572872 | tf_op jit(solution)/shard_map/ppermute | solution.py:586
  765.3 44.9 %collective-permute-start.55 = (bf16[128,2048]{1,0:T(8,128)(2,1)}, bf16[128,2048]{1,0:T(8,128)(2,1)}, u32[]{:S(2)}, u32[]{:S(2)}) collective-permute-start(bf16[128,2048]{1,0:T(8,128)(2,1)} %get-tuple-element.476), channel_id=1, source_target_pairs={{0,3},{1,0},{2,1},{3,2},{4,7},{5,4},{6,5},{7,6},{8,11},{9,8},{10,9... | collective-permute-start | bytes 1572872 | tf_op jit(solution)/shard_map/ppermute | solution.py:586
  810.1 62.3 %collective-permute-start.60 = (bf16[1024,1280]{1,0:T(8,128)(2,1)}, bf16[1024,1280]{1,0:T(8,128)(2,1)}, u32[]{:S(2)}, u32[]{:S(2)}) collective-permute-start(bf16[1024,1280]{1,0:T(8,128)(2,1)} %get-tuple-element.502), channel_id=1, source_target_pairs={{0,4},{4,0},{1,5},{5,1},{2,6},{6,2},{3,7},{7,3},{8,12},{12,8},{9,1... | collective-permute-start | bytes 7864328 | tf_op jit(solution)/shard_map/ppermute | solution.py:877
  810.1 57.3 %all-to-all-start.17 = ((bf16[8,80,2048]{2,1,0:T(8,128)(2,1)}), bf16[8,80,2048]{2,1,0:T(8,128)(2,1)}, u32[]{:S(2)}, u32[]{:S(2)}) async-start(bf16[8,80,2048]{2,1,0:T(8,128)(2,1)} %bitcast.271), calls=%async_computation.17 | async-start | bytes 5242880 | tf_op jit(solution)/shard_map/all_to_all | solution.py:613
  826.2 41.3 %collective-permute-start.57 = (bf16[256,2048]{1,0:T(8,128)(2,1)}, bf16[256,2048]{1,0:T(8,128)(2,1)}, u32[]{:S(2)}, u32[]{:S(2)}) collective-permute-start(bf16[256,2048]{1,0:T(8,128)(2,1)} %product.38), channel_id=1, source_target_pairs={{0,1},{1,2},{2,3},{3,0},{4,5},{5,6},{6,7},{7,4},{8,9},{9,10},{10,1... | collective-permute-start | bytes 3145736 | tf_op jit(solution)/shard_map/ppermute | solution.py:586
  (96 other events, 2387.2 us)
Sparse Core Ops, SparseCore 0:
  10.9 18.3 all-gather.2
  30.8 14.8 all-gather.4

commit v7 on v6

--- a/solution.py
+++ b/solution.py
@@ -910,7 +910,7 @@
     small = jnp.concatenate([attn_gain_sums[0], grad_query_gain, grad_key_gain, grad_moe_gain])
     cuts = [0, width, width + head_size, width + 2 * head_size, 2 * (width + head_size)]
     small = jnp.concatenate([small, router_sums])
-    small = swap(after(jnp.broadcast_to(small, (peers, small.shape[0])), out_sums))
+    small = swap(after(jnp.broadcast_to(small, (peers, small.shape[0])), out_sums, first_up))
     output_back[0] = swap(after(returned[0], small))
     first_up, first_down, free_up, free_down, grad_down, output_part, qkv_parts, small = after(
         (first_up, first_down, free_up, free_down, grad_down, output_part, qkv_parts, small)
@@ -924,7 +924,7 @@
 
     qkv_parts = swap_parts(after(qkv_sums, output_back[0]))
     reduced_qkv = jnp.sum(qkv_parts.astype(f32), axis=0)
-    outputs = (hidden + collect(output_back, 0, running, f32)).astype(bf16)
+    outputs = (hidden + collect(output_back, 0, after(running, qkv_sums), f32)).astype(bf16)
     small = after(jnp.sum(small, axis=0), qkv_sums)
     small = jnp.stack([small, *[shifted(small, step) for step in range(1, columns)]])
     to_true = lax.rem(col - jnp.arange(columns, dtype=jnp.int32) + columns, columns)

time: 937 us -> 922 us (0.984)
  starting transfers between devices: 192 us -> 178 us
    ppermute x48, starting transfers between devices: 87.3 us -> 72.4 us  [shifted(): lax.ppermute(block, 'col', [(i, (i + by) % columns) for i in range(column...]
  transfers between devices with their start and end apart: 85 -> 85, of which waited for: 38 -> 37; matrix products, arithmetic and copies ran while one was open for 12% -> 12% of each run, Pallas kernels for 33% -> 34%
where the time goes in v7:
time: 922 us; the launch traced here: 910 us
  Pallas kernels  314 us (34%)
  waiting for transfers between devices  272 us (30%)
  starting transfers between devices  178 us (19%)
  other arithmetic  72.8 us (8%)
  local copies, waits for them, and re-layouts  31.6 us (3%)
  matrix products  26 us (3%)
  between operations  15.6 us (2%)
    ppermute x48, waiting for transfers between devices, shifted(): lax.ppermute(block, 'col', [(i, (i + by) % columns) for i in range(column...  190 us
    pallas_call x20, Pallas kernels, product(): pl.pallas_call(functools.partial(product_kernel, transposed), out_shape=j...  88.6 us
    pallas_call x4, Pallas kernels, expert_block(): pl.pallas_call(expert_kernel, out_shape=[shape((count, hidden), bf16), sh...  83.6 us
    all_to_all x17, starting transfers between devices, swap(): lax.all_to_all(rows.reshape(peers, rows.shape[0] // peers, *rows.shape[1:...  76.2 us
    ppermute x48, starting transfers between devices, shifted(): lax.ppermute(block, 'col', [(i, (i + by) % columns) for i in range(column...  72.4 us
    pallas_call x2, Pallas kernels, weight_gradients(): pl.pallas_call(functools.partial(weight_kernel, blocks, len(rights), weig...  46.4 us
    ppermute x14, waiting for transfers between devices, exchange_plane(): parts[step] = lax.ppermute(part, plane, pairs) if step else part  36.7 us
    pallas_call x2, Pallas kernels, attention_backward(): pl.pallas_call(functools.partial(backward_kernel, blocks, head_size ** (-...  33.7 us
  transfers between devices with their start and end apart: 85, of which 37 were waited for; matrix products, arithmetic and copies ran while one was open for 12% of the time, Pallas kernels for 34%

profile of v7, /device:TPU:0, one launch (start us, length us, event | category | flops | bytes accessed | tf_op | source)
XLA Modules:
  0.0 910.4 jit_solution(7663195835736831478)
XLA Ops:
  41.1 21.0 %collective-permute-done.1 = bf16[256,2048]{1,0:T(8,128)(2,1)S(1)} collective-permute-done((bf16[256,2048]{1,0:T(8,128)(2,1)S(1)}, bf16[256,2048]{1,0:T(8,128)(2,1)S(1)}, u32[]{:S(2)}, u32[]{:S(2)}) %collective-permute-start.1) | collective-permute-done | bytes 1048608 | tf_op jit(solution)/shard_map/ppermute | solution.py:586
  104.3 20.2 %attention_forward.1 = (bf16[256,1024]{1,0:T(8,128)(2,1)}, bf16[256,1024]{1,0:T(8,128)(2,1)}, bf16[256,1024]{1,0:T(8,128)(2,1)}, bf16[256,1024]{1,0:T(8,128)(2,1)}, f32[8,1,1024]{2,1,0:T(1,128)}) custom-call(s32[1]{0:T(128)} %bitcast.4.col_ref, f32[256,1280]{1,0:T(8,128)} %fusion.50.refs_0_.refs_4_.refs_8_, f32[256,1280]{1,0:T(8,128)} %fusion.51.refs_1_.refs_5_.refs_9_, ...), custom_call_target="tpu_custom_call" | custom-call | flops 1000 | bytes 1000 | tf_op jit(solution)/shard_map/attention_forward/pallas_call | solution.py:124
  162.2 11.1 %collective-permute-done.10 = bf16[128,2048]{1,0:T(8,128)(2,1)S(1)} collective-permute-done((bf16[128,2048]{1,0:T(8,128)(2,1)}, bf16[128,2048]{1,0:T(8,128)(2,1)S(1)}, u32[]{:S(2)}, u32[]{:S(2)}) %collective-permute-start.10) | collective-permute-done | bytes 524320 | tf_op jit(solution)/shard_map/ppermute | solution.py:586
  173.4 10.8 %collective-permute-done.9 = bf16[128,2048]{1,0:T(8,128)(2,1)S(1)} collective-permute-done((bf16[128,2048]{1,0:T(8,128)(2,1)}, bf16[128,2048]{1,0:T(8,128)(2,1)S(1)}, u32[]{:S(2)}, u32[]{:S(2)}) %collective-permute-start.9) | collective-permute-done | bytes 524320 | tf_op jit(solution)/shard_map/ppermute | solution.py:586
  216.9 12.8 %collective-permute-done.12 = bf16[128,2048]{1,0:T(8,128)(2,1)S(1)} collective-permute-done((bf16[128,2048]{1,0:T(8,128)(2,1)}, bf16[128,2048]{1,0:T(8,128)(2,1)S(1)}, u32[]{:S(2)}, u32[]{:S(2)}) %collective-permute-start.12) | collective-permute-done | bytes 524320 | tf_op jit(solution)/shard_map/ppermute | solution.py:586
  244.6 11.0 %collective-permute-done.16 = bf16[128,2048]{1,0:T(8,128)(2,1)S(1)} collective-permute-done((bf16[128,2048]{1,0:T(8,128)(2,1)}, bf16[128,2048]{1,0:T(8,128)(2,1)S(1)}, u32[]{:S(2)}, u32[]{:S(2)}) %collective-permute-start.16) | collective-permute-done | bytes 524320 | tf_op jit(solution)/shard_map/ppermute | solution.py:586
  283.9 17.2 %collective-permute-done.17.right_ref = bf16[256,2048]{1,0:T(8,128)(2,1)} collective-permute-done((bf16[256,2048]{1,0:T(8,128)(2,1)}, bf16[256,2048]{1,0:T(8,128)(2,1)}, u32[]{:S(2)}, u32[]{:S(2)}) %collective-permute-start.17) | collective-permute-done | bytes 1048608 | tf_op jit(solution)/shard_map/ppermute | solution.py:586
  316.3 20.9 %expert_block.4 = (bf16[640,768]{1,0:T(8,128)(2,1)}, bf16[640,768]{1,0:T(8,128)(2,1)}, bf16[640,768]{1,0:T(8,128)(2,1)}, bf16[640,2048]{1,0:T(8,128)(2,1)}, bf16[640,2048]{1,0:T(8,128)(2,1)}, /*index=5*/f32[640,1]{1,0:T(8,128)}) custom-call(bf16[640,2048]{1,0:T(8,128)(2,1)} %bitcast.17.rows_ref.refs_0_, bf16[640,2048]{1,0:T(8,128)(2,1)} %bitcast.3.upstream_ref.refs_4_, ...), custom_call_target="tpu_custom_call" | custom-call | flops 1000 | bytes 1000 | tf_op jit(solution)/shard_map/expert_block/pallas_call | solution.py:519
  354.4 20.8 %expert_block.5 = (bf16[640,768]{1,0:T(8,128)(2,1)}, bf16[640,768]{1,0:T(8,128)(2,1)}, bf16[640,768]{1,0:T(8,128)(2,1)}, bf16[640,2048]{1,0:T(8,128)(2,1)}, bf16[640,2048]{1,0:T(8,128)(2,1)}, /*index=5*/f32[640,1]{1,0:T(8,128)}) custom-call(bf16[640,2048]{1,0:T(8,128)(2,1)} %bitcast.30.rows_ref.refs_1_, bf16[640,2048]{1,0:T(8,128)(2,1)} %bitcast.11.upstream_ref.refs_5_, ...), custom_call_target="tpu_custom_call" | custom-call | flops 1000 | bytes 1000 | tf_op jit(solution)/shard_map/expert_block/pallas_call | solution.py:519
  384.3 20.9 %expert_block.6 = (bf16[640,768]{1,0:T(8,128)(2,1)}, bf16[640,768]{1,0:T(8,128)(2,1)}, bf16[640,768]{1,0:T(8,128)(2,1)}, bf16[640,2048]{1,0:T(8,128)(2,1)}, bf16[640,2048]{1,0:T(8,128)(2,1)}, /*index=5*/f32[640,1]{1,0:T(8,128)}) custom-call(bf16[640,2048]{1,0:T(8,128)(2,1)} %bitcast.36.rows_ref.refs_2_, bf16[640,2048]{1,0:T(8,128)(2,1)} %bitcast.15.upstream_ref.refs_6_, ...), custom_call_target="tpu_custom_call" | custom-call | flops 1000 | bytes 1000 | tf_op jit(solution)/shard_map/expert_block/pallas_call | solution.py:519
  405.2 11.4 %all-to-all-done.7 = bf16[8,80,2048]{2,1,0:T(8,128)(2,1)} async-done(((bf16[8,80,2048]{2,1,0:T(8,128)(2,1)}), bf16[8,80,2048]{2,1,0:T(8,128)(2,1)}, u32[]{:S(2)}, u32[]{:S(2)}) %all-to-all-start.7) | async-done | bytes 2621472 | tf_op jit(solution)/shard_map/all_to_all | solution.py:613
  428.8 20.9 %expert_block.7 = (bf16[640,768]{1,0:T(8,128)(2,1)}, bf16[640,768]{1,0:T(8,128)(2,1)}, bf16[640,768]{1,0:T(8,128)(2,1)}, bf16[640,2048]{1,0:T(8,128)(2,1)}, bf16[640,2048]{1,0:T(8,128)(2,1)}, /*index=5*/f32[640,1]{1,0:T(8,128)}) custom-call(bf16[640,2048]{1,0:T(8,128)(2,1)} %bitcast.52.rows_ref.refs_3_, bf16[640,2048]{1,0:T(8,128)(2,1)} %bitcast.13.upstream_ref.refs_7_, ...), custom_call_target="tpu_custom_call" | custom-call | flops 1000 | bytes 1000 | tf_op jit(solution)/shard_map/expert_block/pallas_call | solution.py:519
  470.8 19.1 %collective-permute-done.31 = f32[4,80]{1,0:T(4,128)S(1)} collective-permute-done((f32[4,80]{1,0:T(4,128)S(1)}, f32[4,80]{1,0:T(4,128)S(1)}, u32[]{:S(2)}, u32[]{:S(2)}) %collective-permute-start.31) | collective-permute-done | bytes 1312 | tf_op jit(solution)/shard_map/ppermute | solution.py:628
  509.2 10.0 %collective-permute-done.35 = f32[4,80]{1,0:T(4,128)S(1)} collective-permute-done((f32[4,80]{1,0:T(4,128)S(1)}, f32[4,80]{1,0:T(4,128)S(1)}, u32[]{:S(2)}, u32[]{:S(2)}) %collective-permute-start.35) | collective-permute-done | bytes 1312 | tf_op jit(solution)/shard_map/ppermute | solution.py:628
  544.3 19.7 %collective-permute-done.40 = f32[8,80]{1,0:T(8,128)S(1)} collective-permute-done((f32[8,80]{1,0:T(8,128)S(1)}, f32[8,80]{1,0:T(8,128)S(1)}, u32[]{:S(2)}, u32[]{:S(2)}) %collective-permute-start.40) | collective-permute-done | bytes 2592 | tf_op jit(solution)/shard_map/ppermute | solution.py:586
  588.0 28.1 %weight_gradients.2 = (f32[2048,768]{1,0:T(8,128)}, f32[2048,768]{1,0:T(8,128)}) custom-call(bf16[640,2048]{1,0:T(8,128)(2,1)} %bitcast.17.rows_ref.refs_0_, bf16[640,2048]{1,0:T(8,128)(2,1)} %bitcast.30.rows_ref.refs_1_, bf16[640,2048]{1,0:T(8,128)(2,1)} %bitcast.36.rows_ref.refs_2_, bf16[640,2048]{1,0:T(8,128)(2,1)} %bitcast.52.rows_ref.refs_3_, ...), custom_call_target="tpu_custom_call" | custom-call | flops 1000 | bytes 1000 | tf_op jit(solution)/shard_map/weight_gradients/pallas_call | solution.py:324
  665.6 10.8 %split_gradient.2 = (bf16[1024,1024]{1,0:T(8,128)(2,1)}, bf16[1024,1024]{1,0:T(8,128)(2,1)}) custom-call(s32[1]{0:T(128)} %bitcast.107.mine_ref, bf16[256,2048]{1,0:T(8,128)(2,1)} %get-tuple-element.571.left_ref.refs_0_, bf16[256,2048]{1,0:T(8,128)(2,1)} %collective-permute-done.43.left_ref.refs_1_, bf16[256,2048]{1,0:T(8,128)(2,1)} %pad_maximum_fusion.3.left_ref.refs_2_, ...), custom_call_target="tpu_custom_call" | custom-call | flops 1000 | bytes 1000 | tf_op jit(solution)/shard_map/split_gradient/pallas_call | solution.py:365
  686.6 16.2 %attention_backward.2 = (bf16[256,1280]{1,0:T(8,128)(2,1)}, bf16[256,1280]{1,0:T(8,128)(2,1)}, bf16[256,1280]{1,0:T(8,128)(2,1)}, bf16[256,1280]{1,0:T(8,128)(2,...) custom-call(s32[1]{0:T(128)} %bitcast.4.col_ref, ...), custom_call_target="tpu_custom_call" | custom-call | flops 1000 | bytes 1000 | tf_op jit(solution)/shard_map/attention_backward/pallas_call | solution.py:254
  723.7 17.5 %attention_backward.3 = (bf16[256,1280]{1,0:T(8,128)(2,1)}, bf16[256,1280]{1,0:T(8,128)(2,1)}, bf16[256,1280]{1,0:T(8,128)(2,1)}, bf16[256,1280]{1,0:T(8,128)(2,...) custom-call(s32[1]{0:T(128)} %bitcast.4.col_ref, ...), custom_call_target="tpu_custom_call", output_to_operand_aliasing={{0}: (22, {}), {1}: (23, {}), {2}: (24, {}), {3}: (25, {})} | custom-call | flops 1000 | bytes 1000 | tf_op jit(solution)/shard_map/attention_backward/pallas_call | solution.py:254
  742.7 11.2 %spread.3 = (bf16[128,2048]{1,0:T(8,128)(2,1)}, bf16[128,2048]{1,0:T(8,128)(2,1)}, bf16[128,2048]{1,0:T(8,128)(2,1)}, bf16[128,2048]{1,0:T(8,128)(2,1)}, f32[128...) custom-call(bf16[256,1280]{1,0:T(8,128)(2,1)} %get-tuple-element.487.refs_0_.refs_4_, ...), custom_call_target="tpu_custom_call" | custom-call | flops 1000 | bytes 1000 | tf_op jit(solution)/shard_map/spread/pallas_call | solution.py:412
  757.1 13.0 %collective-permute-done.52 = bf16[128,2048]{1,0:T(8,128)(2,1)} collective-permute-done((bf16[128,2048]{1,0:T(8,128)(2,1)}, bf16[128,2048]{1,0:T(8,128)(2,1)}, u32[]{:S(2)}, u32[]{:S(2)}) %collective-permute-start.52) | collective-permute-done | bytes 524320 | tf_op jit(solution)/shard_map/ppermute | solution.py:586
  779.8 12.0 %split_gradient.3 = (bf16[1024,1280]{1,0:T(8,128)(2,1)}, bf16[1024,1280]{1,0:T(8,128)(2,1)}) custom-call(s32[1]{0:T(128)} %bitcast.107.mine_ref, bf16[256,2048]{1,0:T(8,128)(2,1)} %get-tuple-element.584.refs_0_, bf16[256,2048]{1,0:T(8,128)(2,1)} %copy-done.11, bf16[256,2048]{1,0:T(8,128)(2,1)} %copy-done.9, bf16[256,2048]{1,0:T(8,128)(2,1)} %copy-done.10, ...), custom_call_target="tpu_custom_call" | custom-call | flops 1000 | bytes 1000 | tf_op jit(solution)/shard_map/split_gradient/pallas_call | solution.py:365
  791.7 18.3 %weight_gradients.3 = f32[768,2048]{1,0:T(8,128)} custom-call(bf16[640,768]{1,0:T(8,128)(2,1)} %get-tuple-element.482.refs_0_, bf16[640,768]{1,0:T(8,128)(2,1)} %get-tuple-element.483.refs_1_, bf16[640,768]{1,0:T(8,128)(2,1)} %get-tuple-element.484.refs_2_, bf16[640,768]{1,0:T(8,128)(2,1)} %get-tuple-element.485.refs_3_, ...), custom_call_target="tpu_custom_call" | custom-call | flops 1000 | bytes 1000 | tf_op jit(solution)/shard_map/weight_gradients/pallas_call | solution.py:324
  882.2 17.1 %all-to-all-done.18 = bf16[4,256,1280]{2,1,0:T(8,128)(2,1)} async-done(((bf16[4,256,1280]{2,1,0:T(8,128)(2,1)}), bf16[4,256,1280]{2,1,0:T(8,128)(2,1)}, u32[]{:S(2)}, u32[]{:S(2)}) %all-to-all-start.18) | async-done | bytes 2621472 | tf_op jit(solution)/shard_map/all_to_all | solution.py:886
  (440 shorter events, 502.5 us)
Async XLA Ops:
  7.2 54.9 %all-gather.3.cloned.1.call-start = ((), (), s32[]{:S(2)}) async-start(), calls=%async_computation.19 | async-start | bytes 7864320 | tf_op jit(solution)/shard_map/all_gather | solution.py:683
  15.0 47.1 %collective-permute-start.1 = (bf16[256,2048]{1,0:T(8,128)(2,1)S(1)}, bf16[256,2048]{1,0:T(8,128)(2,1)S(1)}, u32[]{:S(2)}, u32[]{:S(2)}) collective-permute-start(bf16[256,2048]{1,0:T(8,128)(2,1)S(1)} %copy-done.2), channel_id=1, source_target_pairs={{0,3},{1,0},{2,1},{3,2},{4,7},{5,4},{6,5},{7,6},{8,11},{9,8},{10,9... | collective-permute-start | bytes 3145736 | tf_op jit(solution)/shard_map/ppermute | solution.py:586
  22.7 66.1 %all-to-all-start = ((bf16[8,80,2048]{2,1,0:T(8,128)(2,1)}), bf16[8,80,2048]{2,1,0:T(8,128)(2,1)}, u32[]{:S(2)}, u32[]{:S(2)}) async-start(bf16[8,80,2048]{2,1,0:T(8,128)(2,1)} %bitcast.260), calls=%async_computation | async-start | bytes 5242880 | tf_op jit(solution)/shard_map/all_to_all | solution.py:613
  27.3 97.2 %all-gather.5.cloned.1.call-start = ((), (), s32[]{:S(2)}) async-start(), calls=%async_computation.20 | async-start | bytes 6291456 | tf_op jit(solution)/shard_map/all_gather | solution.py:684
  88.9 43.6 %collective-permute-start.6 = (s32[8,256]{1,0:T(8,128)S(1)}, s32[8,256]{1,0:T(8,128)S(1)}, u32[]{:S(2)}, u32[]{:S(2)}) collective-permute-start(s32[8,256]{1,0:T(8,128)S(1)} %bitcast.286), channel_id=1, source_target_pairs={{0,1},{1,2},{2,3},{3,0},{4,5},{5,6},{6,7},{7,4},{8,9},{9,10},{10,1... | collective-permute-start | bytes 24584 | tf_op jit(solution)/shard_map/ppermute | solution.py:586
  89.3 43.2 %collective-permute-start.7 = (s32[8,256]{1,0:T(8,128)S(1)}, s32[8,256]{1,0:T(8,128)S(1)}, u32[]{:S(2)}, u32[]{:S(2)}) collective-permute-start(s32[8,256]{1,0:T(8,128)S(1)} %bitcast.287), channel_id=1, source_target_pairs={{0,2},{1,3},{2,0},{3,1},{4,6},{5,7},{6,4},{7,5},{8,10},{9,11},{10,... | collective-permute-start | bytes 24584 | tf_op jit(solution)/shard_map/ppermute | solution.py:586
  91.6 41.0 %collective-permute-start.8 = (s32[8,256]{1,0:T(8,128)S(1)}, s32[8,256]{1,0:T(8,128)S(1)}, u32[]{:S(2)}, u32[]{:S(2)}) collective-permute-start(s32[8,256]{1,0:T(8,128)S(1)} %bitcast.288), channel_id=1, source_target_pairs={{0,3},{1,0},{2,1},{3,2},{4,7},{5,4},{6,5},{7,6},{8,11},{9,8},{10,9... | collective-permute-start | bytes 24584 | tf_op jit(solution)/shard_map/ppermute | solution.py:586
  92.8 41.6 %collective-permute-start.4 = (bf16[256,2048]{1,0:T(8,128)(2,1)S(1)}, bf16[256,2048]{1,0:T(8,128)(2,1)}, u32[]{:S(2)}, u32[]{:S(2)}) collective-permute-start(bf16[256,2048]{1,0:T(8,128)(2,1)S(1)} %copy-done.6), channel_id=1, source_target_pairs={{0,1},{1,2},{2,3},{3,0},{4,5},{5,6},{6,7},{7,4},{8,9},{9,10},{10,1... | collective-permute-start | bytes 3145736 | tf_op jit(solution)/shard_map/ppermute | solution.py:586
  93.6 46.5 %collective-permute-start.5 = (bf16[256,2048]{1,0:T(8,128)(2,1)S(1)}, bf16[256,2048]{1,0:T(8,128)(2,1)}, u32[]{:S(2)}, u32[]{:S(2)}) collective-permute-start(bf16[256,2048]{1,0:T(8,128)(2,1)S(1)} %copy-done.6), channel_id=1, source_target_pairs={{0,3},{1,0},{2,1},{3,2},{4,7},{5,4},{6,5},{7,6},{8,11},{9,8},{10,9... | collective-permute-start | bytes 3145736 | tf_op jit(solution)/shard_map/ppermute | solution.py:586
  140.1 44.1 %all-to-all-start.1 = ((bf16[8,80,2048]{2,1,0:T(8,128)(2,1)}), bf16[8,80,2048]{2,1,0:T(8,128)(2,1)}, u32[]{:S(2)}, u32[]{:S(2)}) async-start(bf16[8,80,2048]{2,1,0:T(8,128)(2,1)} %bitcast.263), calls=%async_computation.1 | async-start | bytes 5242880 | tf_op jit(solution)/shard_map/all_to_all | solution.py:613
  184.9 44.8 %all-to-all-start.2 = ((bf16[8,80,2048]{2,1,0:T(8,128)(2,1)}), bf16[8,80,2048]{2,1,0:T(8,128)(2,1)}, u32[]{:S(2)}, u32[]{:S(2)}) async-start(bf16[8,80,2048]{2,1,0:T(8,128)(2,1)} %bitcast.261), calls=%async_computation.2 | async-start | bytes 5242880 | tf_op jit(solution)/shard_map/all_to_all | solution.py:613
  305.5 37.3 %all-to-all-start.5 = ((bf16[8,80,2048]{2,1,0:T(8,128)(2,1)}), bf16[8,80,2048]{2,1,0:T(8,128)(2,1)}, u32[]{:S(2)}, u32[]{:S(2)}) async-start(bf16[8,80,2048]{2,1,0:T(8,128)(2,1)} %bitcast.258), calls=%async_computation.5 | async-start | bytes 5242880 | tf_op jit(solution)/shard_map/all_to_all | solution.py:613
  416.6 37.1 %all-to-all-start.8 = ((bf16[8,80,2048]{2,1,0:T(8,128)(2,1)}), bf16[8,80,2048]{2,1,0:T(8,128)(2,1)}, u32[]{:S(2)}, u32[]{:S(2)}) async-start(bf16[8,80,2048]{2,1,0:T(8,128)(2,1)} %bitcast.278), calls=%async_computation.8 | async-start | bytes 5242880 | tf_op jit(solution)/shard_map/all_to_all | solution.py:613
  527.2 37.5 %all-to-all-start.11 = ((bf16[8,80,2048]{2,1,0:T(8,128)(2,1)}), bf16[8,80,2048]{2,1,0:T(8,128)(2,1)}, u32[]{:S(2)}, u32[]{:S(2)}) async-start(bf16[8,80,2048]{2,1,0:T(8,128)(2,1)} %bitcast.275), calls=%async_computation.11 | async-start | bytes 5242880 | tf_op jit(solution)/shard_map/all_to_all | solution.py:613
  576.2 48.3 %collective-permute-start.43 = (bf16[256,2048]{1,0:T(8,128)(2,1)}, bf16[256,2048]{1,0:T(8,128)(2,1)}, u32[]{:S(2)}, u32[]{:S(2)}) collective-permute-start(bf16[256,2048]{1,0:T(8,128)(2,1)} %get-tuple-element.571.left_ref.refs_0_), channel_id=1, source_target_pairs={{0,1},{1,2},{2,3},{3,0},{4,5},{5,6},{6,7},{7,4},{8,9},{9,10},{10,1... | collective-permute-start | bytes 3145736 | tf_op jit(solution)/shard_map/ppermute | solution.py:586
  576.8 47.7 %collective-permute-start.44 = (bf16[256,2048]{1,0:T(8,128)(2,1)}, bf16[256,2048]{1,0:T(8,128)(2,1)}, u32[]{:S(2)}, u32[]{:S(2)}) collective-permute-start(bf16[256,2048]{1,0:T(8,128)(2,1)} %get-tuple-element.571.left_ref.refs_0_), channel_id=1, source_target_pairs={{0,3},{1,0},{2,1},{3,2},{4,7},{5,4},{6,5},{7,6},{8,11},{9,8},{10,9... | collective-permute-start | bytes 3145736 | tf_op jit(solution)/shard_map/ppermute | solution.py:586
  583.5 51.1 %all-to-all-start.12 = ((bf16[8,80,2048]{2,1,0:T(8,128)(2,1)}), bf16[8,80,2048]{2,1,0:T(8,128)(2,1)}, u32[]{:S(2)}, u32[]{:S(2)}) async-start(bf16[8,80,2048]{2,1,0:T(8,128)(2,1)} %bitcast.274), calls=%async_computation.12 | async-start | bytes 5242880 | tf_op jit(solution)/shard_map/all_to_all | solution.py:613
  634.7 41.7 %all-to-all-start.13 = ((bf16[8,80,2048]{2,1,0:T(8,128)(2,1)}), bf16[8,80,2048]{2,1,0:T(8,128)(2,1)}, u32[]{:S(2)}, u32[]{:S(2)}) async-start(bf16[8,80,2048]{2,1,0:T(8,128)(2,1)} %bitcast.272), calls=%async_computation.13 | async-start | bytes 5242880 | tf_op jit(solution)/shard_map/all_to_all | solution.py:613
  722.4 87.7 %collective-permute-start.56 = (bf16[256,2048]{1,0:T(8,128)(2,1)}, bf16[256,2048]{1,0:T(8,128)(2,1)}, u32[]{:S(2)}, u32[]{:S(2)}) collective-permute-start(bf16[256,2048]{1,0:T(8,128)(2,1)} %product.37), channel_id=1, source_target_pairs={{0,1},{1,2},{2,3},{3,0},{4,5},{5,6},{6,7},{7,4},{8,9},{9,10},{10,1... | collective-permute-start | bytes 3145736 | tf_op jit(solution)/shard_map/ppermute | solution.py:586
  771.5 43.2 %all-to-all-start.16 = ((f32[8,1,20736]{2,1,0:T(1,128)}), f32[8,1,20736]{2,1,0:T(1,128)}, u32[]{:S(2)}, u32[]{:S(2)}) async-start(f32[8,1,20736]{2,1,0:T(1,128)} %reshape.436), calls=%async_computation.16 | async-start | bytes 1327104 | tf_op jit(solution)/shard_map/all_to_all | solution.py:613
  775.7 41.1 %collective-permute-start.53 = (bf16[128,2048]{1,0:T(8,128)(2,1)}, bf16[128,2048]{1,0:T(8,128)(2,1)}, u32[]{:S(2)}, u32[]{:S(2)}) collective-permute-start(bf16[128,2048]{1,0:T(8,128)(2,1)} %get-tuple-element.475), channel_id=1, source_target_pairs={{0,3},{1,0},{2,1},{3,2},{4,7},{5,4},{6,5},{7,6},{8,11},{9,8},{10,9... | collective-permute-start | bytes 1572872 | tf_op jit(solution)/shard_map/ppermute | solution.py:586
  775.8 41.0 %collective-permute-start.54 = (bf16[128,2048]{1,0:T(8,128)(2,1)}, bf16[128,2048]{1,0:T(8,128)(2,1)}, u32[]{:S(2)}, u32[]{:S(2)}) collective-permute-start(bf16[128,2048]{1,0:T(8,128)(2,1)} %get-tuple-element.476), channel_id=1, source_target_pairs={{0,1},{1,2},{2,3},{3,0},{4,5},{5,6},{6,7},{7,4},{8,9},{9,10},{10,1... | collective-permute-start | bytes 1572872 | tf_op jit(solution)/shard_map/ppermute | solution.py:586
  777.8 39.0 %collective-permute-start.55 = (bf16[128,2048]{1,0:T(8,128)(2,1)}, bf16[128,2048]{1,0:T(8,128)(2,1)}, u32[]{:S(2)}, u32[]{:S(2)}) collective-permute-start(bf16[128,2048]{1,0:T(8,128)(2,1)} %get-tuple-element.477), channel_id=1, source_target_pairs={{0,3},{1,0},{2,1},{3,2},{4,7},{5,4},{6,5},{7,6},{8,11},{9,8},{10,9... | collective-permute-start | bytes 1572872 | tf_op jit(solution)/shard_map/ppermute | solution.py:586
  832.4 37.6 %collective-permute-start.57 = (bf16[256,2048]{1,0:T(8,128)(2,1)}, bf16[256,2048]{1,0:T(8,128)(2,1)}, u32[]{:S(2)}, u32[]{:S(2)}) collective-permute-start(bf16[256,2048]{1,0:T(8,128)(2,1)} %product.38), channel_id=1, source_target_pairs={{0,1},{1,2},{2,3},{3,0},{4,5},{5,6},{6,7},{7,4},{8,9},{9,10},{10,1... | collective-permute-start | bytes 3145736 | tf_op jit(solution)/shard_map/ppermute | solution.py:586
  (96 other events, 2404.7 us)
Sparse Core Ops, SparseCore 0:
  10.9 18.3 all-gather.2
  30.8 14.8 all-gather.4
